TPU v7x, 128 devices: a whole 4x4x4 slice. The times are simulated.
128 devices in a mesh: rows: 8 (over z_hi, y), cols: 8 (over z_lo, x), rel: 2 (over core).
Axes of the slice: x: 4, y: 4, z: 4 (z_hi: 2, z_lo: 2; z = z_hi * 2 + z_lo), core: 2. Of those that a mesh axis runs over, the one named last changes fastest.
Arguments:
- features: bfloat16 [32768, 512], P('cols', 'rows'), may hold values from -6 to 6
- rel_weight: bfloat16 [8, 512, 512], P('rel'), may hold values from -0.25 to 0.25
- self_weight: bfloat16 [512, 512], replicated, may hold values from -0.25 to 0.25
- bias: float32 [512], replicated, may hold values from -3 to 3
- block_code: int32 [8, 8, 2, 128], P('rows', 'cols', 'rel'), may hold values from 0 to 4095, as said below
- block_counts: int32 [8, 8, 2, 128, 128, 128], P('rows', 'cols', 'rel'), may hold values from 0 to 3, as said below
Outputs:
- node_out: bfloat16 [32768, 512], P(('rows', 'cols', 'rel'))
Inputs may be any that keep to these rules, and one draw needn't show every extreme that they name: `block_code`: within one device the codes are distinct, each below 4096. `block_counts`: on each device the slots with counts come first, 128 // k of them for some k from 1 to 5; some device has all 128 slots in use; the other slots are all zero.
All inputs are finite; a program needn't handle non-finite values.
Results may differ from a plain program's by a relative error of at most 0.0036.
Values may be sent and summed in bfloat16 or wider, within the bound.
No kernel may reach another device: no remote copies, remote signals or barrier semaphores. Data moves between devices by JAX's collectives and lax.ppermute only.
A program may use at most 256 MiB of HBM per device.

v0:
```python
import jax
import jax.numpy as jnp
from jax import lax
from jax.sharding import PartitionSpec as P


def on_device(features, rel_weight, self_weight, bias, block_code, block_counts):
    group_rows = features.shape[0]
    width = rel_weight.shape[2]
    per_group = rel_weight.shape[0]
    codes = block_code[0, 0, 0]
    counts = block_counts[0, 0, 0]
    block = counts.shape[-1]
    nblk = group_rows // block
    all_weights = jnp.concatenate([rel_weight, self_weight[None]], axis=0)
    panel = lax.all_gather(features, "rows", axis=1, tiled=True)
    transformed = jnp.einsum("nk,rkd->rnd", panel, all_weights, preferred_element_type=jnp.float32)
    hidden = transformed[:per_group].astype(jnp.bfloat16).reshape(per_group * nblk, block, width)
    self_part = transformed[per_group]
    relation = codes // (nblk * nblk)
    target = codes // nblk % nblk
    source = codes % nblk
    segment = relation * nblk + target
    rowsum = jnp.sum(counts, axis=-1).astype(jnp.float32)
    seg_onehot = (segment[:, None] == jnp.arange(per_group * nblk)[None, :]).astype(jnp.float32)
    deg_part = jnp.dot(seg_onehot.T, rowsum, precision=lax.Precision.HIGHEST)
    degree = lax.psum(deg_part.astype(jnp.bfloat16), "cols").astype(jnp.float32)
    inverse = 1.0 / jnp.maximum(degree, 1.0)
    slot_scale = jnp.dot(seg_onehot, inverse, precision=lax.Precision.HIGHEST)
    weight = (counts.astype(jnp.float32) * slot_scale[:, :, None]).astype(jnp.bfloat16)
    source_rows = jnp.take(hidden, relation * nblk + source, axis=0)
    contrib = jnp.einsum("sij,sjd->sid", weight, source_rows, preferred_element_type=jnp.float32)
    aggregate = jnp.zeros((nblk, block, width), jnp.float32).at[target].add(contrib)
    aggregate = aggregate.reshape(group_rows, width)
    on_diagonal = (lax.axis_index("rows") == lax.axis_index("cols")) & (lax.axis_index("rel") == 0)
    term = aggregate + jnp.where(on_diagonal, 1.0, 0.0).astype(jnp.float32) * self_part
    summed = lax.psum_scatter(term, ("cols", "rel"), scatter_dimension=0, tiled=True)
    return jax.nn.relu(summed + bias).astype(jnp.bfloat16)


def solution(mesh):
    in_specs = (
        P("cols", "rows"),
        P("rel", None, None),
        P(),
        P(),
        P("rows", "cols", "rel", None),
        P("rows", "cols", "rel", None, None, None),
    )
    out_specs = P(("rows", "cols", "rel"), None)
    return jax.shard_map(
        on_device, mesh=mesh, in_specs=in_specs, out_specs=out_specs, check_vma=False
    )
```

profile of v0, /device:TPU:0, one launch (start us, length us, event | category | flops | bytes accessed | tf_op | source)
XLA Modules:
  0.0 354.6 jit_solution(5681228856327658341)
XLA Ops:
  6.5 0.0 all-gather.2.cloned.1.call-start
  6.5 0.7 all-gather.2.cloned.1.call-update
  7.3 0.0 reduce-scatter.2.cloned.1.call-start
  7.3 2.8 copy.11
  10.1 1.3 copy.10
  11.4 5.6 %reduce_sum.9 = s32[128,128]{1,0:T(8,128)S(1)} reduce(s32[1,1,1,128,128,128]{5,4,3,2,1,0:T(8,128)} %param.11, s32[]{:T(128)} %constant.70.clone.1), dimensions={0,1,2,5}, to_apply=%region_0.1 | reduce | flops 2080768 | bytes 8454148 | tf_op jit(solution)/shard_map/reduce_sum | solution.py:24
  17.0 0.0 copy-done.1
  17.0 0.3 convolution_convert_fusion
  17.4 35.0 %psum.7 = bf16[128,128]{1,0:T(8,128)(2,1)S(1)} all-reduce(bf16[128,128]{1,0:T(8,128)(2,1)S(1)} %convolution_convert_fusion), channel_id=1, replica_groups=mesh['rows'=8,'cols'=8,'rel'=2] {'cols'}, use_global_device_ids=true, to_apply=%region_1.2 | all-reduce | flops 16384 | bytes 65536 | tf_op jit(solution)/shard_map/psum | solution.py:27
  52.4 0.2 fusion.13
  52.6 31.3 %all-gather.2.cloned.1.call-done = bf16[4096,512]{0,1:T(8,128)(2,1)} async-done(((bf16[4096,64]{0,1:T(8,128)(2,1)}), bf16[4096,512]{0,1:T(8,128)(2,1)}) %all-gather.2.cloned.1.call-update) | async-done | bytes 4194320 | tf_op jit(solution)/shard_map/all_gather | solution.py:16
  83.9 18.9 %convolution_bitcast_fusion = f32[5,4096,512]{1,2,0:T(8,128)} fusion(bf16[4096,512]{0,1:T(8,128)(2,1)} %all-gather.2.cloned.1.call-done, bf16[1,512,512]{1,2,0:T(8,128)(2,1)S(1)} %bitcast.68, bf16[4,512,512]{1,2,0:T(8,128)(2,1)S(1)} %copy.11), kind=kOutput, calls=%fused_computation.6 | convolution fusion | flops 10738728960 | bytes 48758784 | tf_op jit(solution)/shard_map/nk,rkd->rnd/dot_general | solution.py:17
  102.8 17.3 %slice.19 = bf16[4,4096,512]{1,2,0:T(8,128)(2,1)} slice(f32[5,4096,512]{1,2,0:T(8,128)} %convolution_bitcast_fusion), slice={[0:4], [0:4096], [0:512]} | slice | bytes 33554432 | tf_op jit(solution)/shard_map/slice | solution.py:18
  120.1 21.2 %copy.12 = bf16[4,4096,512]{2,1,0:T(8,128)(2,1)} copy(bf16[4,4096,512]{1,2,0:T(8,128)(2,1)} %slice.19) | data formatting | bytes 33554432 | tf_op jit(solution)/shard_map/slice | solution.py:18
  141.3 14.0 %gather_fusion = bf16[128,128,512]{2,1,0:T(8,128)(2,1)} fusion(bf16[128,128,512]{2,1,0:T(8,128)(2,1)} %bitcast.67, s32[1024]{0:T(1024)S(1)} %pad_clamp_fusion), kind=kCustom, calls=%fused_computation | custom fusion | bytes 33554944 | tf_op jit(solution)/shard_map/jit(_take)/gather | solution.py:31
  155.4 20.1 %fusion = f32[128,128,512]{2,1,0:T(8,128)} fusion(bf16[128,128,512]{2,1,0:T(8,128)(2,1)} %gather_fusion, pred[128]{0:T(512)(128)(4,1)S(1)} %compare_and_fusion, s32[1,1,1,128,128,128]{5,4,3,2,1,0:T(8,128)} %param.11, f32[128,128]{1,0:T(8,128)S(1)} %fusion.13), kind=kOutput, calls=%fused_computation.3 | convolution fusion | flops 2162163712 | bytes 58785920 | tf_op jit(solution)/shard_map/sij,sjd->sid/dot_general | solution.py:32
  175.5 4.4 %broadcast_in_dim.21 = f32[32,128,512]{2,1,0:T(8,128)} broadcast(f32[]{:T(128)} %constant.68.clone.1), dimensions={} | broadcast | bytes 8388612 | tf_op jit(solution)/shard_map/broadcast_in_dim | solution.py:33
  179.8 72.6 %scatter_fusion = f32[32,128,512]{2,1,0:T(8,128)} fusion(f32[32,128,512]{2,1,0:T(8,128)} %broadcast_in_dim.21, s32[128]{0:T(128)S(1)} %get-tuple-element.8, f32[128,128,512]{2,1,0:T(8,128)} %fusion), kind=kCustom, calls=%fused_computation.1 | custom fusion | flops 8388608 | bytes 100663808 | tf_op jit(solution)/shard_map/scatter-add | solution.py:33
  252.4 8.9 %copy.15 = f32[4096,512]{0,1:T(8,128)} copy(f32[4096,512]{1,0:T(8,128)} %bitcast.66) | data formatting | bytes 16777216 | tf_op jit(solution)/shard_map/reshape | solution.py:34
  261.4 11.4 %fusion.4 = f32[4096,512]{0,1:T(8,128)} fusion(f32[4096,512]{0,1:T(8,128)} %copy.15, f32[5,4096,512]{1,2,0:T(8,128)} %convolution_bitcast_fusion, f32[]{:T(128)S(6)} %select_n.113), kind=kLoop, calls=%fused_computation.9 | loop fusion | flops 4194304 | bytes 25165828 | tf_op jit(solution)/shard_map/add | solution.py:36
  272.8 0.0 reduce-scatter.2.cloned.1.call-update
  272.8 73.0 %reduce-scatter.2.cloned.1.call-done = f32[256,512]{0,1:T(8,128)} async-done(((f32[4096,512]{0,1:T(8,128)}), f32[256,512]{0,1:T(8,128)}) %reduce-scatter.2.cloned.1.call-update) | async-done | bytes 524304 | tf_op jit(solution)/shard_map/reduce_scatter | solution.py:37
  345.8 1.2 maximum_convert_fusion
  347.0 0.8 copy.14
  (7 shorter events, 0.1 us)
Async XLA Ops:
  6.5 10.5 %copy-start.1 = (s32[1,1,1,128]{3,2,1,0:T(1,128)S(1)}, s32[1,1,1,128]{3,2,1,0:T(1,128)}, u32[]{:S(2)}) copy-start(s32[1,1,1,128]{3,2,1,0:T(1,128)} %param.10) | copy-start | bytes 1540
  6.5 77.3 %all-gather.2.cloned.1.call-start = ((), (), s32[]{:S(2)}) async-start(), calls=%async_computation.1 | async-start | bytes 4718592 | tf_op jit(solution)/shard_map/all_gather | solution.py:16
  7.3 338.5 %reduce-scatter.2.cloned.1.call-start = ((), (), s32[]{:S(2)}) async-start(), calls=%async_computation.2 | async-start | bytes 8912896 | tf_op jit(solution)/shard_map/reduce_scatter | solution.py:37
  272.8 73.0 %copy-start = (f32[512]{0:T(512)S(1)}, f32[512]{0:T(512)}, u32[]{:S(2)}) copy-start(f32[512]{0:T(512)} %param.9) | copy-start | bytes 6148
Sparse Core Ops, SparseCore 0:
  9.7 74.1 all-gather.1
  272.9 72.8 reduce-scatter.1
where the time goes:
time: 356 us; the launch traced here: 355 us
  waiting for transfers between devices  105 us (29%)
  other arithmetic  90.9 us (26%)
  local copies, waits for them, and re-layouts  70.8 us (20%)
  matrix products  39.6 us (11%)
  blocking collectives  35 us (10%)
  between operations  13.5 us (4%)
    reduce_scatter x1, waiting for transfers between devices, on_device(): lax.psum_scatter(term, ('cols', 'rel'), scatter_dimension=0, tiled=True)  73 us
    scatter-add x1, other arithmetic, on_device(): jnp.zeros((nblk, block, width), jnp.float32).at[target].add(contrib)  72.6 us
    slice x2, local copies, waits for them, and re-layouts, on_device(): transformed[:per_group].astype(jnp.bfloat16)  38.5 us
    psum x1, blocking collectives, on_device(): degree = lax.psum(deg_part.astype(jnp.bfloat16), 'cols').astype(jnp.float32)  35 us
    all_gather x1, waiting for transfers between devices, on_device(): panel = lax.all_gather(features, 'rows', axis=1, tiled=True)  31.3 us
    dot_general x1, matrix products, on_device(): jnp.einsum('sij,sjd->sid', weight, source_rows, preferred_element_type=jn...  20.1 us
    dot_general x1, matrix products, on_device(): jnp.einsum('nk,rkd->rnd', panel, all_weights, preferred_element_type=jnp....  18.9 us
    gather x1, local copies, waits for them, and re-layouts, on_device(): source_rows = jnp.take(hidden, relation * nblk + source, axis=0)  14 us
  transfers between devices with their start and end apart: 2, of which 2 were waited for; matrix products, arithmetic and copies ran while one was open for 3% of the time, Pallas kernels for 0%

commit v1 on v0

v1 whole, which is shorter than its diff:
```python
import functools

import jax
import jax.numpy as jnp
from jax import lax
from jax.experimental import pallas as pl
from jax.experimental.pallas import tpu as pltpu
from jax.sharding import PartitionSpec as P

BLOCK = 128
WIDTH = 512
NBLK = 32
NREL = 4
SLOTS = 128
PIECE = 64
NODES = NBLK * BLOCK
CHUNK = 512
HSTEPS = NODES // CHUNK
TSTEP = 8
NT = (((1,), (1,)), ((), ()))
OFF_CORE = (((0, 1), (1, 1), (0, 2)), ((0, 3), (1, 3), (1, 0)))
OFF_BOTH = (1, 2)


def shifted(row, off, sign):
    return (row // 4 + off[0]) % 2 * 4 + (row % 4 + sign * off[1]) % 4


def piece_order(row, core):
    first = [jnp.where(core == 0, shifted(row, a, -1), shifted(row, b, -1)) for a, b in zip(*OFF_CORE)]
    second = [jnp.where(core == 0, shifted(row, b, -1), shifted(row, a, -1)) for a, b in zip(*OFF_CORE)]
    return jnp.stack([row] + first + second + [shifted(row, OFF_BOTH, -1)])


def degree_kernel(seg_ref, counts_ref, deg_ref):
    step = pl.program_id(0)

    @pl.when(step == 0)
    def _():
        deg_ref[...] = jnp.zeros_like(deg_ref)

    per = counts_ref.shape[0]
    ones = jnp.ones((8, BLOCK), jnp.bfloat16)
    for s in range(per):
        c = counts_ref[s].astype(jnp.float32).astype(jnp.bfloat16)
        row = lax.dot_general(ones, c, NT, preferred_element_type=jnp.float32)
        seg = seg_ref[step * per + s]
        deg_ref[pl.ds(seg, 1), :] += row[0:1]


def partial_degrees(segment, counts):
    per = 16
    return pl.pallas_call(
        degree_kernel,
        grid_spec=pltpu.PrefetchScalarGridSpec(
            num_scalar_prefetch=1,
            grid=(SLOTS // per,),
            in_specs=[pl.BlockSpec((per, BLOCK, BLOCK), lambda i, s: (i, 0, 0))],
            out_specs=pl.BlockSpec((SLOTS, BLOCK), lambda i, s: (0, 0)),
        ),
        out_shape=jax.ShapeDtypeStruct((NREL * NBLK, BLOCK), jnp.float32),
        cost_estimate=pl.CostEstimate(flops=2 * SLOTS * BLOCK * BLOCK * 8, bytes_accessed=SLOTS * BLOCK * BLOCK * 4, transcendentals=0),
        name="degrees",
    )(segment, counts)


def main_kernel(
    meta_ref, order_ref, starts_ref, codes_ref,
    p0, p1, p2, p3, p4, p5, p6, half_own, half_sib, wt_ref, deg_ref, counts_hbm,
    sib_ref, own_ref,
    hid, cnt, inv_t, acc, sem,
):
    step = pl.program_id(0)
    counts_copy = pltpu.make_async_copy(counts_hbm, cnt, sem)

    @pl.when(step == 0)
    def _():
        counts_copy.start()
        degree = deg_ref[0]
        for k in range(1, deg_ref.shape[0]):
            degree = degree + deg_ref[k]
        inv_t[...] = (1.0 / jnp.maximum(degree, 1.0)).T

    @pl.when(step < HSTEPS)
    def _():
        chunk = lax.rem(meta_ref[0] * (HSTEPS // 2) + step, HSTEPS)
        last = jnp.where(step < HSTEPS // 2, half_own[...], half_sib[...])
        x = jnp.concatenate([p[...] for p in (p0, p1, p2, p3, p4, p5, p6)] + [last], axis=0)

        def one(r, carry):
            h = jnp.dot(wt_ref[r], x, preferred_element_type=jnp.float32).astype(jnp.bfloat16)
            for b in range(CHUNK // BLOCK):
                hid[r, chunk * (CHUNK // BLOCK) + b] = h[:, b * BLOCK : (b + 1) * BLOCK]
            return carry

        lax.fori_loop(0, NREL, one, 0)

    @pl.when(step == HSTEPS)
    def _():
        counts_copy.wait()

    def weights(slot, live):
        code = codes_ref[slot]
        seg = lax.shift_right_logical(code, 5)
        rel = lax.shift_right_logical(code, 10)
        src = jnp.bitwise_and(code, NBLK - 1)
        scale = jnp.take_along_axis(inv_t[...], jnp.full((BLOCK, BLOCK), seg, jnp.int32), axis=1)
        w = cnt[slot].astype(jnp.float32) * scale
        if live is not None:
            w = jnp.where(live, w, 0.0)
        return hid[rel, src], w.astype(jnp.bfloat16)

    def targets(first, out_ref):
        for u in range(TSTEP):
            begin = starts_ref[first + u]
            end = starts_ref[first + u + 1]
            acc[...] = jnp.zeros_like(acc)

            def pair(q, carry):
                at = begin + 2 * q
                h1, w1 = weights(order_ref[at], None)
                h2, w2 = weights(order_ref[jnp.minimum(at + 1, SLOTS - 1)], at + 1 < end)
                h = jnp.concatenate([h1, h2], axis=1)
                w = jnp.concatenate([w1, w2], axis=1)
                acc[...] += lax.dot_general(h, w, NT, preferred_element_type=jnp.float32)
                return carry

            lax.fori_loop(0, lax.div(end - begin + 1, 2), pair, 0)
            out_ref[u] = acc[...].astype(out_ref.dtype)

    half_steps = NBLK // 2 // TSTEP

    @pl.when((step >= HSTEPS) & (step < HSTEPS + half_steps))
    def _():
        targets((step - HSTEPS) * TSTEP, sib_ref)

    @pl.when(step >= HSTEPS + half_steps)
    def _():
        targets((step - HSTEPS) * TSTEP, own_ref)


def partial_aggregates(core, order, starts, codes, pieces, half_own, half_sib, weights_t, degrees, counts):
    half_steps = NBLK // 2 // TSTEP

    def piece_at(i, meta, *_):
        return (0, lax.rem(meta[0] * (HSTEPS // 2) + jnp.minimum(i, HSTEPS - 1), HSTEPS))

    in_specs = (
        [pl.BlockSpec((PIECE, CHUNK), piece_at)] * 7
        + [
            pl.BlockSpec((PIECE, CHUNK), lambda i, *_: (0, jnp.minimum(i, HSTEPS // 2 - 1))),
            pl.BlockSpec((PIECE, CHUNK), lambda i, *_: (0, jnp.clip(i - HSTEPS // 2, 0, HSTEPS // 2 - 1))),
            pl.BlockSpec((NREL, WIDTH, WIDTH), lambda i, *_: (0, 0, 0), pipeline_mode=pl.Buffered(1)),
            pl.BlockSpec(degrees.shape, lambda i, *_: (0, 0, 0), pipeline_mode=pl.Buffered(1)),
            pl.BlockSpec(memory_space=pl.ANY),
        ]
    )
    out_specs = [
        pl.BlockSpec((TSTEP, WIDTH, BLOCK), lambda i, *_: (jnp.clip(i - HSTEPS, 0, half_steps - 1), 0, 0)),
        pl.BlockSpec((TSTEP, WIDTH, BLOCK), lambda i, *_: (jnp.clip(i - HSTEPS - half_steps, 0, half_steps - 1), 0, 0)),
    ]
    return pl.pallas_call(
        main_kernel,
        grid_spec=pltpu.PrefetchScalarGridSpec(
            num_scalar_prefetch=4,
            grid=(HSTEPS + 2 * half_steps,),
            in_specs=in_specs,
            out_specs=out_specs,
            scratch_shapes=[
                pltpu.VMEM((NREL, NBLK, WIDTH, BLOCK), jnp.bfloat16),
                pltpu.VMEM((SLOTS, BLOCK, BLOCK), jnp.int32),
                pltpu.VMEM((BLOCK, BLOCK), jnp.float32),
                pltpu.VMEM((WIDTH, BLOCK), jnp.float32),
                pltpu.SemaphoreType.DMA(()),
            ],
        ),
        out_shape=[
            jax.ShapeDtypeStruct((NBLK // 2, WIDTH, BLOCK), jnp.bfloat16),
            jax.ShapeDtypeStruct((NBLK // 2, WIDTH, BLOCK), jnp.float32),
        ],
        compiler_params=pltpu.CompilerParams(vmem_limit_bytes=52 * 1024 * 1024),
        cost_estimate=pl.CostEstimate(flops=11 * 10**9, bytes_accessed=20 * 2**20, transcendentals=0),
        name="aggregate",
    )(core, order, starts, codes, *pieces, half_own, half_sib, weights_t, degrees, counts)


def finish_kernel(parts_ref, x_ref, w_ref, bias_ref, out_ref):
    self_part = lax.dot_general(x_ref[...], w_ref[...], (((0,), (0,)), ((), ())), preferred_element_type=jnp.float32)
    for b in range(2):
        total = parts_ref[0, b].astype(jnp.float32)
        for k in range(1, parts_ref.shape[0]):
            total = total + parts_ref[k, b].astype(jnp.float32)
        rows = slice(b * BLOCK, (b + 1) * BLOCK)
        out_ref[rows, :] = jnp.maximum(total.T + self_part[rows] + bias_ref[...], 0.0).astype(jnp.bfloat16)


def finish(parts, x_own, self_weight, bias):
    return pl.pallas_call(
        finish_kernel,
        out_shape=jax.ShapeDtypeStruct((2 * BLOCK, WIDTH), jnp.bfloat16),
        compiler_params=pltpu.CompilerParams(vmem_limit_bytes=32 * 1024 * 1024),
        name="finish",
    )(parts, x_own, self_weight, bias.reshape(1, WIDTH))


def on_device(features, rel_weight, self_weight, bias, block_code, block_counts):
    row, col, core = lax.axis_index("rows"), lax.axis_index("cols"), lax.axis_index("rel")
    codes = block_code[0, 0, 0]
    counts = block_counts[0, 0, 0]

    xt = features.T
    pair_axes = ("rows", "rel")

    def fetch(array, offs):
        moves = [(r * 2 + c, shifted(r, offs[c], 1) * 2 + c) for r in range(8) for c in range(2)]
        return lax.ppermute(array, pair_axes, moves)

    def swap(array):
        return lax.ppermute(array, "rel", [(0, 1), (1, 0)])

    xt_half = lax.dynamic_slice(xt, (0, core * (NODES // 2)), (PIECE, NODES // 2))
    got = [fetch(xt, (a, b)) for a, b in zip(*OFF_CORE)]
    half_own = fetch(xt_half, (OFF_BOTH, OFF_BOTH))
    other = [swap(p) for p in got]
    half_sib = swap(half_own)
    pieces = [xt] + got + other

    order_k = piece_order(row, core)
    weights_t = rel_weight.reshape(NREL, 8, PIECE, WIDTH)[:, order_k].reshape(NREL, WIDTH, WIDTH).transpose(0, 2, 1)

    at = (row * 2 + core) * (2 * BLOCK)
    half_at = at % (NODES // 2)
    tail = jnp.where(
        (at >= NODES // 2) == (core == 1),
        lax.dynamic_slice(half_own, (0, half_at), (PIECE, 2 * BLOCK)),
        lax.dynamic_slice(half_sib, (0, half_at), (PIECE, 2 * BLOCK)),
    )
    x_rows = jnp.concatenate([lax.dynamic_slice(p, (0, at), (PIECE, 2 * BLOCK)) for p in pieces] + [tail], axis=0)
    x_own = lax.ppermute(x_rows, ("rows", "cols"), [(a * 8 + b, b * 8 + a) for a in range(8) for b in range(8)])
    self_w = self_weight.reshape(8, PIECE, WIDTH)[piece_order(col, core)].reshape(WIDTH, WIDTH)

    segment = codes // NBLK
    deg_part = partial_degrees(segment, counts)
    degrees = lax.all_to_all(jnp.broadcast_to(deg_part[None], (8,) + deg_part.shape), "cols", 0, 0)

    target = segment % NBLK
    place = jnp.where(target // 2 % 2 == core, NBLK // 2, 0) + target // 4 * 2 + target % 2
    slots = jnp.arange(SLOTS, dtype=jnp.int32)
    key = place * SLOTS + slots
    rank = jnp.sum((key[None, :] < key[:, None]).astype(jnp.int32), axis=1)
    order = jnp.sum(jnp.where(rank[None, :] == slots[:, None], slots[None, :], 0), axis=1)
    bounds = jnp.arange(NBLK + 1, dtype=jnp.int32)
    starts = jnp.sum((place[None, :] < bounds[:, None]).astype(jnp.int32), axis=1)

    to_sib, own = partial_aggregates(
        core.reshape(1).astype(jnp.int32), order, starts, codes, pieces, half_own, half_sib, weights_t, degrees, counts
    )
    both = (own + swap(to_sib).astype(jnp.float32)).astype(jnp.bfloat16)
    parts = lax.all_to_all(both.reshape(8, 2, WIDTH, BLOCK), "cols", 0, 0)
    return finish(parts, x_own, self_w, bias)


def solution(mesh):
    in_specs = (
        P("cols", "rows"),
        P("rel", None, None),
        P(),
        P(),
        P("rows", "cols", "rel", None),
        P("rows", "cols", "rel", None, None, None),
    )
    out_specs = P(("rows", "cols", "rel"), None)
    return jax.shard_map(on_device, mesh=mesh, in_specs=in_specs, out_specs=out_specs, check_vma=False)
```

time: 356 us -> 151 us (0.42)
  the two profiles are of different devices: /device:TPU:0 before, /device:TPU:8 now
where the time goes in v1:
time: 151 us; the launch traced here: 150 us
  Pallas kernels  57.5 us (38%)
  waiting for transfers between devices  34.9 us (23%)
  starting transfers between devices  32.7 us (22%)
  local copies, waits for them, and re-layouts  18.4 us (12%)
  other arithmetic  5.81 us (4%)
    pallas_call x1, Pallas kernels, partial_aggregates(): pl.pallas_call(main_kernel, grid_spec=pltpu.PrefetchScalarGridSpec(num_sc...  46.4 us
    ppermute x1, waiting for transfers between devices, on_device(): lax.ppermute(x_rows, ('rows', 'cols'), [(a * 8 + b, b * 8 + a) for a in r...  29.8 us
    ppermute x5, starting transfers between devices, swap(): return lax.ppermute(array, 'rel', [(0, 1), (1, 0)])  10.8 us
    ppermute x4, starting transfers between devices, fetch(): return lax.ppermute(array, pair_axes, moves)  8.87 us
    pallas_call x1, Pallas kernels, partial_degrees(): pl.pallas_call(degree_kernel, grid_spec=pltpu.PrefetchScalarGridSpec(num_...  8.39 us
    all_to_all x1, starting transfers between devices, on_device(): lax.all_to_all(jnp.broadcast_to(deg_part[None], (8,) + deg_part.shape), '...  5.65 us
    gather x2, local copies, waits for them, and re-layouts, on_device(): rel_weight.reshape(NREL, 8, PIECE, WIDTH)[:, order_k]  5.13 us
    unnamed x15, local copies, waits for them, and re-layouts  4.6 us
  transfers between devices with their start and end apart: 12, of which 3 were waited for; matrix products, arithmetic and copies ran while one was open for 13% of the time, Pallas kernels for 6%

profile of v1, /device:TPU:8, one launch (start us, length us, event | category | flops | bytes accessed | tf_op | source)
XLA Modules:
  0.0 149.6 jit_solution(15321945301654157359)
XLA Ops:
  0.0 1.6 %collective-permute-start = (bf16[64,4096]{1,0:T(8,128)(2,1)}, bf16[64,4096]{1,0:T(8,128)(2,1)}, u32[]{:S(2)}, u32[]{:S(2)}) collective-permute-start(bf16[64,4096]{1,0:T(8,128)(2,1)} %bitcast.40), channel_id=1, source_target_pairs={{0,16},{1,49},{16,32},{17,1},{32,48},{33,17},{48,0},{49,33},{64,80... | collective-permute-start | bytes 1572872 | tf_op jit(solution)/shard_map/ppermute | solution.py:216
  1.6 4.6 %collective-permute-start.1 = (bf16[64,4096]{1,0:T(8,128)(2,1)}, bf16[64,4096]{1,0:T(8,128)(2,1)}, u32[]{:S(2)}, u32[]{:S(2)}) collective-permute-start(bf16[64,4096]{1,0:T(8,128)(2,1)} %bitcast.41), channel_id=1, source_target_pairs={{0,80},{1,113},{16,96},{17,65},{32,112},{33,81},{48,64},{49,97},{6... | collective-permute-start | bytes 1572872 | tf_op jit(solution)/shard_map/ppermute | solution.py:216
  6.2 1.2 collective-permute-start.2
  7.4 1.0 dynamic-slice_bitcast_fusion
  8.4 1.5 collective-permute-start.6
  9.9 1.2 iota_add_fusion
  11.1 8.4 %degrees.1 = f32[128,128]{1,0:T(8,128)} custom-call(s32[128]{0:T(128)} %get-tuple-element.11.seg_ref, s32[128,128,128]{2,1,0:T(8,128)} %bitcast.46), custom_call_target="tpu_custom_call" | custom-call | flops 33554432 | bytes 8388608 | tf_op jit(solution)/shard_map/degrees/pallas_call | solution.py:53
  19.5 1.7 %broadcast_in_dim.23 = f32[8,128,128]{2,1,0:T(8,128)} broadcast(f32[128,128]{1,0:T(8,128)} %degrees.1), dimensions={1,2} | broadcast | bytes 589824 | tf_op jit(solution)/shard_map/broadcast_in_dim | solution.py:244
  21.2 5.7 %all-to-all-start = ((f32[8,128,128]{2,1,0:T(8,128)}), f32[8,128,128]{2,1,0:T(8,128)}, u32[]{:S(2)}, u32[]{:S(2)}) async-start(f32[8,128,128]{2,1,0:T(8,128)} %broadcast_in_dim.23), calls=%async_computation | async-start | bytes 1048576 | tf_op jit(solution)/shard_map/all_to_all | solution.py:244
  27.1 1.1 collective-permute-done.1.p2
  28.3 9.4 %collective-permute-start.5 = (bf16[64,4096]{1,0:T(8,128)(2,1)}, bf16[64,4096]{1,0:T(8,128)(2,1)}, u32[]{:S(2)}, u32[]{:S(2)}) collective-permute-start(bf16[64,4096]{1,0:T(8,128)(2,1)} %collective-permute-done.2.p3), channel_id=1, source_target_pairs={{0,1},{1,0},{2,3},{3,2},{4,5},{5,4},{6,7},{7,6},{8,9},{9,8},{10,11... | collective-permute-start | bytes 1572872 | tf_op jit(solution)/shard_map/ppermute | solution.py:219
  37.9 2.0 %gather_fusion = bf16[8,4,64,512]{3,2,1,0:T(8,128)(2,1)} fusion(bf16[4,8,64,512]{3,2,1,0:T(8,128)(2,1)S(1)} %bitcast.38, s32[1024]{0:T(1024)S(1)} %pad_clamp_fusion.1), kind=kCustom, calls=%fused_computation | custom fusion | bytes 4194336 | tf_op jit(solution)/shard_map/gather | solution.py:229
  39.9 3.1 %copy.9 = bf16[4,8,64,512]{3,2,1,0:T(8,128)(2,1)} copy(bf16[4,8,64,512]{3,2,0,1:T(8,128)(2,1)} %bitcast.48) | data formatting | bytes 4194304 | tf_op jit(solution)/shard_map/gather | solution.py:229
  43.1 4.2 %copy.10 = bf16[4,512,512]{1,2,0:T(8,128)(2,1)} copy(bf16[4,512,512]{2,1,0:T(8,128)(2,1)} %bitcast.49) | data formatting | bytes 4194304 | tf_op jit(solution)/shard_map/reshape | solution.py:229
  47.6 46.4 %aggregate.1 = (bf16[16,512,128]{2,1,0:T(8,128)(2,1)}, f32[16,512,128]{2,1,0:T(8,128)}) custom-call(s32[1]{0:T(128)} %bitcast.meta_ref, s32[128]{0:T(128)S(1)} %select_reduce_fusion.order_ref, s32[33]{0:T(128)S(1)} %convert_reduce_fusion.1.starts_ref, s32[128]{0:T(128)S(1)} %bitcast.45, bf16[64,4096]{1,0:T(8,128)(2,1)S(1)} %bitcast.43, ...), custom_call_target="tpu_custom_call" | custom-call | flops 11000000512 | bytes 20971520 | tf_op jit(solution)/shard_map/aggregate/pallas_call | solution.py:162
  94.1 1.3 collective-permute-start.8
  95.3 4.0 %collective-permute-done.8 = bf16[16,512,128]{2,1,0:T(8,128)(2,1)S(1)} collective-permute-done((bf16[16,512,128]{2,1,0:T(8,128)(2,1)}, bf16[16,512,128]{2,1,0:T(8,128)(2,1)S(1)}, u32[]{:S(2)}, u32[]{:S(2)}) %collective-permute-start.8) | collective-permute-done | bytes 2097184 | tf_op jit(solution)/shard_map/ppermute | solution.py:219
  99.3 4.2 %add_convert_fusion = bf16[16,512,128]{2,1,0:T(8,128)(2,1)} fusion(f32[16,512,128]{2,1,0:T(8,128)} %get-tuple-element.7, bf16[16,512,128]{2,1,0:T(8,128)(2,1)S(1)} %collective-permute-done.8), kind=kLoop, calls=%fused_computation.2 | loop fusion | flops 3145728 | bytes 8388608 | tf_op jit(solution)/shard_map/convert_element_type | solution.py:258
  103.5 4.5 %all-to-all-start.1 = ((bf16[8,2,512,128]{3,2,1,0:T(8,128)(2,1)}), bf16[8,2,512,128]{3,2,1,0:T(8,128)(2,1)}, u32[]{:S(2)}, u32[]{:S(2)}) async-start(bf16[8,2,512,128]{3,2,1,0:T(8,128)(2,1)} %bitcast.50), calls=%async_computation.1 | async-start | bytes 4194304 | tf_op jit(solution)/shard_map/all_to_all | solution.py:259
  108.0 0.8 dynamic-slice_dynamic-update-slice_fusion.5
  112.6 2.8 %collective-permute-start.9 = (bf16[512,256]{1,0:T(8,128)(2,1)S(1)}, bf16[512,256]{1,0:T(8,128)(2,1)S(1)}, u32[]{:S(2)}, u32[]{:S(2)}) collective-permute-start(bf16[512,256]{1,0:T(8,128)(2,1)S(1)} %select_dynamic-update-slice_fusion), channel_id=1, source_target_pairs={{0,0},{2,16},{4,32},{6,48},{8,64},{10,80},{12,96},{14,112},{16,2},... | collective-permute-start | bytes 786440 | tf_op jit(solution)/shard_map/ppermute | solution.py:239
  115.5 1.6 %gather_fusion.1 = bf16[8,64,512]{2,1,0:T(8,128)(2,1)S(1)} fusion(bf16[8,64,512]{2,1,0:T(8,128)(2,1)} %bitcast.52, s32[1024]{0:T(1024)S(1)} %pad_clamp_fusion), kind=kCustom, calls=%fused_computation.1 | custom fusion | bytes 1048608 | tf_op jit(solution)/shard_map/gather | solution.py:240
  117.1 29.8 %collective-permute-done.9.x_ref = bf16[512,256]{1,0:T(8,128)(2,1)S(1)} collective-permute-done((bf16[512,256]{1,0:T(8,128)(2,1)S(1)}, bf16[512,256]{1,0:T(8,128)(2,1)S(1)}, u32[]{:S(2)}, u32[]{:S(2)}) %collective-permute-start.9) | collective-permute-done | bytes 262176 | tf_op jit(solution)/shard_map/ppermute | solution.py:239
  146.9 2.7 %finish.1 = bf16[256,512]{1,0:T(8,128)(2,1)} custom-call(bf16[8,2,512,128]{3,2,1,0:T(8,128)(2,1)} %all-to-all-done.1.parts_ref, bf16[512,256]{1,0:T(8,128)(2,1)S(1)} %collective-permute-done.9.x_ref, bf16[512,512]{1,0:T(8,128)(2,1)S(1)} %bitcast.39, f32[1,512]{1,0:T(1,128)S(1)} %bitcast.44), custom_call_target="tpu_custom_call" | custom-call | tf_op jit(solution)/shard_map/finish/pallas_call | solution.py:198
  (35 shorter events, 4.6 us)
Async XLA Ops:
  0.0 37.9 %copy-start = (bf16[4,512,512]{2,1,0:T(8,128)(2,1)S(1)}, bf16[4,512,512]{2,1,0:T(8,128)(2,1)}, u32[]{:S(2)}) copy-start(bf16[4,512,512]{2,1,0:T(8,128)(2,1)} %param.7) | copy-start | bytes 6291460
  0.0 27.0 %collective-permute-start = (bf16[64,4096]{1,0:T(8,128)(2,1)}, bf16[64,4096]{1,0:T(8,128)(2,1)}, u32[]{:S(2)}, u32[]{:S(2)}) collective-permute-start(bf16[64,4096]{1,0:T(8,128)(2,1)} %bitcast.40), channel_id=1, source_target_pairs={{0,16},{1,49},{16,32},{17,1},{32,48},{33,17},{48,0},{49,33},{64,80... | collective-permute-start | bytes 1572872 | tf_op jit(solution)/shard_map/ppermute | solution.py:216
  1.6 26.7 %collective-permute-start.1 = (bf16[64,4096]{1,0:T(8,128)(2,1)}, bf16[64,4096]{1,0:T(8,128)(2,1)}, u32[]{:S(2)}, u32[]{:S(2)}) collective-permute-start(bf16[64,4096]{1,0:T(8,128)(2,1)} %bitcast.41), channel_id=1, source_target_pairs={{0,80},{1,113},{16,96},{17,65},{32,112},{33,81},{48,64},{49,97},{6... | collective-permute-start | bytes 1572872 | tf_op jit(solution)/shard_map/ppermute | solution.py:216
  6.2 22.1 %collective-permute-start.2 = (bf16[64,4096]{1,0:T(8,128)(2,1)}, bf16[64,4096]{1,0:T(8,128)(2,1)}, u32[]{:S(2)}, u32[]{:S(2)}) collective-permute-start(bf16[64,4096]{1,0:T(8,128)(2,1)} %bitcast.42), channel_id=1, source_target_pairs={{0,32},{1,65},{16,48},{17,81},{32,0},{33,97},{48,16},{49,113},{64,... | collective-permute-start | bytes 1572872 | tf_op jit(solution)/shard_map/ppermute | solution.py:216
  8.4 29.4 %collective-permute-start.6 = (bf16[64,2048]{1,0:T(8,128)(2,1)S(1)}, bf16[64,2048]{1,0:T(8,128)(2,1)S(1)}, u32[]{:S(2)}, u32[]{:S(2)}) collective-permute-start(bf16[64,2048]{1,0:T(8,128)(2,1)S(1)} %dynamic-slice_bitcast_fusion), channel_id=1, source_target_pairs={{0,96},{1,97},{16,112},{17,113},{32,64},{33,65},{48,80},{49,81},{6... | collective-permute-start | bytes 786440 | tf_op jit(solution)/shard_map/ppermute | solution.py:216
  21.2 26.4 %all-to-all-start = ((f32[8,128,128]{2,1,0:T(8,128)}), f32[8,128,128]{2,1,0:T(8,128)}, u32[]{:S(2)}, u32[]{:S(2)}) async-start(f32[8,128,128]{2,1,0:T(8,128)} %broadcast_in_dim.23), calls=%async_computation | async-start | bytes 1048576 | tf_op jit(solution)/shard_map/all_to_all | solution.py:244
  27.0 20.5 %collective-permute-start.3 = (bf16[64,4096]{1,0:T(8,128)(2,1)}, bf16[64,4096]{1,0:T(8,128)(2,1)}, u32[]{:S(2)}, u32[]{:S(2)}) collective-permute-start(bf16[64,4096]{1,0:T(8,128)(2,1)} %collective-permute-done.p1), channel_id=1, source_target_pairs={{0,1},{1,0},{2,3},{3,2},{4,5},{5,4},{6,7},{7,6},{8,9},{9,8},{10,11... | collective-permute-start | bytes 1572872 | tf_op jit(solution)/shard_map/ppermute | solution.py:219
  28.3 19.3 %collective-permute-start.4 = (bf16[64,4096]{1,0:T(8,128)(2,1)}, bf16[64,4096]{1,0:T(8,128)(2,1)}, u32[]{:S(2)}, u32[]{:S(2)}) collective-permute-start(bf16[64,4096]{1,0:T(8,128)(2,1)} %collective-permute-done.1.p2), channel_id=1, source_target_pairs={{0,1},{1,0},{2,3},{3,2},{4,5},{5,4},{6,7},{7,6},{8,9},{9,8},{10,11... | collective-permute-start | bytes 1572872 | tf_op jit(solution)/shard_map/ppermute | solution.py:219
  28.3 19.3 %collective-permute-start.5 = (bf16[64,4096]{1,0:T(8,128)(2,1)}, bf16[64,4096]{1,0:T(8,128)(2,1)}, u32[]{:S(2)}, u32[]{:S(2)}) collective-permute-start(bf16[64,4096]{1,0:T(8,128)(2,1)} %collective-permute-done.2.p3), channel_id=1, source_target_pairs={{0,1},{1,0},{2,3},{3,2},{4,5},{5,4},{6,7},{7,6},{8,9},{9,8},{10,11... | collective-permute-start | bytes 1572872 | tf_op jit(solution)/shard_map/ppermute | solution.py:219
  37.8 9.8 %collective-permute-start.7 = (bf16[64,2048]{1,0:T(8,128)(2,1)S(1)}, bf16[64,2048]{1,0:T(8,128)(2,1)S(1)}, u32[]{:S(2)}, u32[]{:S(2)}) collective-permute-start(bf16[64,2048]{1,0:T(8,128)(2,1)S(1)} %collective-permute-done.6.half_own), channel_id=1, source_target_pairs={{0,1},{1,0},{2,3},{3,2},{4,5},{5,4},{6,7},{7,6},{8,9},{9,8},{10,11... | collective-permute-start | bytes 786440 | tf_op jit(solution)/shard_map/ppermute | solution.py:219
  43.0 4.5 %copy-start.1 = (bf16[4096,64]{0,1:T(8,128)(2,1)S(1)}, bf16[4096,64]{0,1:T(8,128)(2,1)}, u32[]{:S(2)}) copy-start(bf16[4096,64]{0,1:T(8,128)(2,1)} %param.6) | copy-start | bytes 1572868
  43.1 4.6 %copy-start.3 = (s32[1,1,1,128]{3,2,1,0:T(1,128)S(1)}, s32[1,1,1,128]{3,2,1,0:T(1,128)}, u32[]{:S(2)}) copy-start(s32[1,1,1,128]{3,2,1,0:T(1,128)} %param.10) | copy-start | bytes 1540
  94.1 5.3 %collective-permute-start.8 = (bf16[16,512,128]{2,1,0:T(8,128)(2,1)}, bf16[16,512,128]{2,1,0:T(8,128)(2,1)S(1)}, u32[]{:S(2)}, u32[]{:S(2)}) collective-permute-start(bf16[16,512,128]{2,1,0:T(8,128)(2,1)} %get-tuple-element.8), channel_id=1, source_target_pairs={{0,1},{1,0},{2,3},{3,2},{4,5},{5,4},{6,7},{7,6},{8,9},{9,8},{10,11... | collective-permute-start | bytes 6291464 | tf_op jit(solution)/shard_map/ppermute | solution.py:219
  103.5 43.4 %copy-start.2 = (f32[512]{0:T(512)S(1)}, f32[512]{0:T(512)}, u32[]{:S(2)}) copy-start(f32[512]{0:T(512)} %param.9) | copy-start | bytes 6148
  103.5 43.4 %all-to-all-start.1 = ((bf16[8,2,512,128]{3,2,1,0:T(8,128)(2,1)}), bf16[8,2,512,128]{3,2,1,0:T(8,128)(2,1)}, u32[]{:S(2)}, u32[]{:S(2)}) async-start(bf16[8,2,512,128]{3,2,1,0:T(8,128)(2,1)} %bitcast.50), calls=%async_computation.1 | async-start | bytes 4194304 | tf_op jit(solution)/shard_map/all_to_all | solution.py:259
  112.6 34.3 %collective-permute-start.9 = (bf16[512,256]{1,0:T(8,128)(2,1)S(1)}, bf16[512,256]{1,0:T(8,128)(2,1)S(1)}, u32[]{:S(2)}, u32[]{:S(2)}) collective-permute-start(bf16[512,256]{1,0:T(8,128)(2,1)S(1)} %select_dynamic-update-slice_fusion), channel_id=1, source_target_pairs={{0,0},{2,16},{4,32},{6,48},{8,64},{10,80},{12,96},{14,112},{16,2},... | collective-permute-start | bytes 786440 | tf_op jit(solution)/shard_map/ppermute | solution.py:239

commit v2 on v0

v2 whole, which is shorter than its diff:
```python
import jax
import jax.numpy as jnp
from jax import lax
from jax.experimental import pallas as pl
from jax.experimental.pallas import tpu as pltpu
from jax.sharding import PartitionSpec as P

BLOCK = 128
WIDTH = 512
NBLK = 32
NREL = 4
SLOTS = 128
PIECE = 64
NODES = NBLK * BLOCK
HALF = NODES // 2
CHUNK = 512
UNROLL = 4
PAIRS = 72
MIB = 1024 * 1024
NT = (((1,), (1,)), ((), ()))
TN = (((0,), (0,)), ((), ()))
VMEM_SPEC = pl.BlockSpec(memory_space=pltpu.VMEM)
SMEM_SPEC = pl.BlockSpec(memory_space=pltpu.SMEM)


def params(mib):
    return pltpu.CompilerParams(vmem_limit_bytes=mib * MIB)


def prep_kernel(codes_ref, counts_ref, weight_ref, deg_ref, cnt_ref, wt_ref):
    step = pl.program_id(0)

    @pl.when(step == 0)
    def _():
        deg_ref[...] = jnp.zeros_like(deg_ref)

    per = counts_ref.shape[0]
    ones = jnp.ones((8, BLOCK), jnp.bfloat16)
    for s in range(per):
        slot = step * per + s
        c = counts_ref[s].astype(jnp.float32).astype(jnp.bfloat16)
        cnt_ref[slot] = c
        row = lax.dot_general(ones, c, NT, preferred_element_type=jnp.float32)
        seg = lax.shift_right_logical(codes_ref[slot], 5)
        deg_ref[0, pl.ds(seg, 1), :] += row[0:1]
    wt_ref[step // 2, pl.ds(pl.multiple_of(step % 2 * 256, 256), 256), :] = weight_ref[0].T

    @pl.when(step == pl.num_programs(0) - 1)
    def _():
        for k in range(1, deg_ref.shape[0]):
            deg_ref[k] = deg_ref[0]


def prep(codes, counts, rel_weight):
    per = 16
    return pl.pallas_call(
        prep_kernel,
        grid=(SLOTS // per,),
        in_specs=[
            SMEM_SPEC,
            pl.BlockSpec((per, BLOCK, BLOCK), lambda i: (i, 0, 0)),
            pl.BlockSpec((1, WIDTH, 256), lambda i: (i // 2, 0, i % 2)),
        ],
        out_specs=[VMEM_SPEC, VMEM_SPEC, VMEM_SPEC],
        out_shape=[
            jax.ShapeDtypeStruct((8, NREL * NBLK, BLOCK), jnp.float32),
            pltpu.VMEM((SLOTS, BLOCK, BLOCK), jnp.bfloat16),
            pltpu.VMEM((NREL, WIDTH, WIDTH), jnp.bfloat16),
        ],
        compiler_params=params(24),
        cost_estimate=pl.CostEstimate(flops=2 * SLOTS * BLOCK * BLOCK * 8, bytes_accessed=10 * MIB, transcendentals=0),
        name="prep",
    )(codes, counts, rel_weight)


def scale_kernel(codes_ref, deg_ref, cnt_ref, out_ref, inv_ref):
    degree = deg_ref[0]
    for k in range(1, deg_ref.shape[0]):
        degree = degree + deg_ref[k]
    inv_ref[...] = (1.0 / jnp.maximum(degree, 1.0)).T
    out_ref[SLOTS:] = jnp.zeros_like(out_ref[SLOTS:])

    def some(q, carry):
        for u in range(8):
            slot = q * 8 + u
            seg = lax.shift_right_logical(codes_ref[slot], 5)
            scale = jnp.take_along_axis(inv_ref[...], jnp.full((BLOCK, BLOCK), seg, jnp.int32), axis=1)
            out_ref[slot] = (cnt_ref[slot].astype(jnp.float32) * scale).astype(jnp.bfloat16)
        return carry

    lax.fori_loop(0, SLOTS // 8, some, 0)


def scaled(codes, degrees, cnt):
    return pl.pallas_call(
        scale_kernel,
        in_specs=[SMEM_SPEC, VMEM_SPEC, VMEM_SPEC],
        out_specs=VMEM_SPEC,
        out_shape=pltpu.VMEM((SLOTS + 1, BLOCK, BLOCK), jnp.bfloat16),
        scratch_shapes=[pltpu.VMEM((BLOCK, BLOCK), jnp.float32)],
        compiler_params=params(24),
        cost_estimate=pl.CostEstimate(flops=4 * SLOTS * BLOCK * BLOCK, bytes_accessed=8 * MIB, transcendentals=0),
        name="scale",
    )(codes, degrees, cnt)


def hidden_chunk(half, step, x, wt_ref, hid_ref):
    per = CHUNK // BLOCK
    first = half * (NBLK // 2) + step * per

    def one(r, carry):
        h = jnp.dot(wt_ref[r], x, preferred_element_type=jnp.float32).astype(jnp.bfloat16)
        for b in range(per):
            hid_ref[r * NBLK + first + b] = h[:, b * BLOCK : (b + 1) * BLOCK]
        return carry

    lax.fori_loop(0, NREL, one, 0)


def own_hidden_kernel(core_ref, x_ref, wt_ref, hid_ref):
    hidden_chunk(core_ref[0], pl.program_id(0), x_ref[...], wt_ref, hid_ref)


HID = (NREL * NBLK, WIDTH, BLOCK)
HSTEPS = HALF // CHUNK


def own_hidden(core, x, wt):
    return pl.pallas_call(
        own_hidden_kernel,
        grid=(HSTEPS,),
        in_specs=[SMEM_SPEC, pl.BlockSpec((WIDTH, CHUNK), lambda i: (0, i)), VMEM_SPEC],
        out_specs=VMEM_SPEC,
        out_shape=pltpu.VMEM(HID, jnp.bfloat16),
        compiler_params=params(12),
        cost_estimate=pl.CostEstimate(flops=2 * HALF * WIDTH * WIDTH * NREL, bytes_accessed=4 * MIB, transcendentals=0),
        name="own_hidden",
    )(core, x, wt)


def slot_pairs(codes_ref, pairs_ref, which, hid_ref, w_ref, acc_ref):
    def some(q, carry):
        for u in range(UNROLL):
            k = q * UNROLL + u
            s1, s2, place = pairs_ref[which, 0, k], pairs_ref[which, 1, k], pairs_ref[which, 2, k]
            hs = []
            for s in (s1, s2):
                code = codes_ref[s]
                hs.append(hid_ref[lax.shift_right_logical(code, 10) * NBLK + jnp.bitwise_and(code, NBLK - 1)])
            h = jnp.concatenate(hs, axis=1)
            w = jnp.concatenate([w_ref[s1], w_ref[s2]], axis=1)
            acc_ref[place] += lax.dot_general(h, w, NT, preferred_element_type=jnp.float32)
        return carry

    lax.fori_loop(0, pairs_ref[which, 3, 0], some, 0)


def sib_kernel(core_ref, codes_ref, pairs_ref, x_ref, wt_ref, w_ref, hid_in, hid_ref, out_ref, acc):
    step = pl.program_id(0)
    hidden_chunk(1 - core_ref[0], step, x_ref[...], wt_ref, hid_ref)
    per = NBLK // 2 // HSTEPS
    acc[pl.ds(step * per, per)] = jnp.zeros((per, WIDTH, BLOCK), jnp.float32)

    @pl.when(step == HSTEPS - 1)
    def _():
        slot_pairs(codes_ref, pairs_ref, 0, hid_ref, w_ref, acc)

        def one(t, carry):
            out_ref[t] = acc[t].astype(jnp.bfloat16)
            return carry

        lax.fori_loop(0, NBLK // 2, one, 0)


def sibling_part(core, codes, pairs, x, wt, w, hid):
    return pl.pallas_call(
        sib_kernel,
        grid=(HSTEPS,),
        in_specs=[
            SMEM_SPEC, SMEM_SPEC, SMEM_SPEC,
            pl.BlockSpec((WIDTH, CHUNK), lambda i: (0, i)), VMEM_SPEC, VMEM_SPEC, VMEM_SPEC,
        ],
        out_specs=[VMEM_SPEC, VMEM_SPEC],
        out_shape=[
            pltpu.VMEM(HID, jnp.bfloat16),
            jax.ShapeDtypeStruct((NBLK // 2, WIDTH, BLOCK), jnp.bfloat16),
        ],
        input_output_aliases={6: 0},
        scratch_shapes=[pltpu.VMEM((NBLK // 2, WIDTH, BLOCK), jnp.float32)],
        compiler_params=params(16),
        cost_estimate=pl.CostEstimate(flops=2 * HALF * WIDTH * WIDTH * NREL * 2, bytes_accessed=4 * MIB, transcendentals=0),
        name="sibling_part",
    )(core, codes, pairs, x, wt, w, hid)


def own_kernel(codes_ref, pairs_ref, w_ref, hid_ref, acc):
    def one(t, carry):
        acc[t] = jnp.zeros((WIDTH, BLOCK), jnp.float32)
        return carry

    lax.fori_loop(0, NBLK // 2, one, 0)
    slot_pairs(codes_ref, pairs_ref, 1, hid_ref, w_ref, acc)


def own_part(codes, pairs, w, hid):
    return pl.pallas_call(
        own_kernel,
        in_specs=[SMEM_SPEC, SMEM_SPEC, VMEM_SPEC, VMEM_SPEC],
        out_specs=VMEM_SPEC,
        out_shape=pltpu.VMEM((NBLK // 2, WIDTH, BLOCK), jnp.float32),
        compiler_params=params(12),
        cost_estimate=pl.CostEstimate(flops=2 * HALF * WIDTH * WIDTH * NREL, bytes_accessed=4 * MIB, transcendentals=0),
        name="own_part",
    )(codes, pairs, w, hid)


def join_kernel(own_ref, other_ref, out_ref):
    out_ref[...] = (own_ref[...] + other_ref[...].astype(jnp.float32)).astype(jnp.bfloat16)


def join(own, other):
    spec = pl.BlockSpec((4, WIDTH, BLOCK), lambda i: (i, 0, 0))
    return pl.pallas_call(
        join_kernel,
        grid=(NBLK // 2 // 4,),
        in_specs=[spec, spec],
        out_specs=spec,
        out_shape=jax.ShapeDtypeStruct((NBLK // 2, WIDTH, BLOCK), jnp.bfloat16),
        compiler_params=params(12),
        cost_estimate=pl.CostEstimate(flops=MIB, bytes_accessed=8 * MIB, transcendentals=0),
        name="join",
    )(own, other)


def finish_kernel(parts_ref, x_ref, w_ref, bias_ref, out_ref):
    self_part = lax.dot_general(x_ref[...], w_ref[...], TN, preferred_element_type=jnp.float32)
    for b in range(2):
        total = parts_ref[0, b].astype(jnp.float32)
        for k in range(1, parts_ref.shape[0]):
            total = total + parts_ref[k, b].astype(jnp.float32)
        rows = slice(b * BLOCK, (b + 1) * BLOCK)
        out_ref[rows, :] = jnp.maximum(total.T + self_part[rows] + bias_ref[...], 0.0).astype(jnp.bfloat16)


def finish(parts, x_own, self_weight, bias):
    return pl.pallas_call(
        finish_kernel,
        out_shape=jax.ShapeDtypeStruct((2 * BLOCK, WIDTH), jnp.bfloat16),
        compiler_params=params(32),
        name="finish",
    )(parts, x_own, self_weight, bias.reshape(1, WIDTH))


def pair_lists(codes, core):
    slots = jnp.arange(SLOTS, dtype=jnp.int32)
    target = codes // NBLK % NBLK
    half = (target // 2 % 2 == core).astype(jnp.int32)
    place = target // 4 * 2 + target % 2
    group = half * (NBLK // 2) + place
    same = group[None, :] == group[:, None]
    nth = jnp.sum((same & (slots[None, :] < slots[:, None])).astype(jnp.int32), axis=1)
    groups = jnp.arange(NBLK, dtype=jnp.int32)
    size = jnp.sum((group[None, :] == groups[:, None]).astype(jnp.int32), axis=1)
    need = (size + 1) // 2
    before = (groups[None, :] < groups[:, None]) & (groups[None, :] // (NBLK // 2) == groups[:, None] // (NBLK // 2))
    base = jnp.sum(jnp.where(before, need[None, :], 0), axis=1)
    at = half * PAIRS + nth // 2 + jnp.sum(jnp.where(group[:, None] == groups[None, :], base[None, :], 0), axis=1)
    entries = jnp.arange(2 * PAIRS, dtype=jnp.int32)
    match = at[None, :] == entries[:, None]
    is_first = match & (nth % 2 == 0)[None, :]
    is_second = match & (nth % 2 == 1)[None, :]
    first = SLOTS + jnp.sum(jnp.where(is_first, slots[None, :] - SLOTS, 0), axis=1)
    second = SLOTS + jnp.sum(jnp.where(is_second, slots[None, :] - SLOTS, 0), axis=1)
    where = jnp.sum(jnp.where(is_first, place[None, :], 0), axis=1)
    steps = (jnp.sum(need.reshape(2, NBLK // 2), axis=1) + UNROLL - 1) // UNROLL
    steps = jnp.broadcast_to(steps[:, None], (2, PAIRS))
    return jnp.stack([first.reshape(2, PAIRS), second.reshape(2, PAIRS), where.reshape(2, PAIRS), steps], axis=1)


def swap(array):
    return lax.ppermute(array, "rel", [(0, 1), (1, 0)])


def on_device(features, rel_weight, self_weight, bias, block_code, block_counts):
    row, core = lax.axis_index("rows"), lax.axis_index("rel")
    codes = block_code[0, 0, 0]
    counts = block_counts[0, 0, 0]
    core_arg = core.reshape(1).astype(jnp.int32)
    padded = jnp.concatenate([codes, jnp.zeros((8,), jnp.int32)])

    x_half = lax.dynamic_slice(features.T, (0, core * HALF), (PIECE, HALF))
    x_mine = lax.all_to_all(jnp.broadcast_to(x_half[None], (8, PIECE, HALF)), "rows", 0, 0)
    x_mine = x_mine.reshape(WIDTH, HALF)

    deg_parts, cnt, wt = prep(codes, counts, rel_weight)
    degrees = lax.all_to_all(deg_parts, "cols", 0, 0)
    w = scaled(codes, degrees, cnt)
    pairs = pair_lists(codes, core)

    x_other = swap(x_mine)
    x_rows = lax.dynamic_slice(x_mine, (0, row * (2 * BLOCK)), (WIDTH, 2 * BLOCK))
    moves = [
        ((a * 8 + b) * 2 + g, (b * 8 + 4 * g + a // 2) * 2 + a % 2) for a in range(8) for b in range(8) for g in range(2)
    ]
    x_own = lax.ppermute(x_rows, ("rows", "cols", "rel"), moves)

    hid = own_hidden(core_arg, x_mine, wt)
    hid, to_sib = sibling_part(core_arg, padded, pairs, x_other, wt, w, hid)
    other = swap(to_sib)
    own = own_part(padded, pairs, w, hid)
    both = join(own, other)
    both, x_own = lax.optimization_barrier((both, x_own))
    parts = lax.all_to_all(both.reshape(8, 2, WIDTH, BLOCK), "cols", 0, 0)
    return finish(parts, x_own, self_weight, bias)


def solution(mesh):
    in_specs = (
        P("cols", "rows"),
        P("rel", None, None),
        P(),
        P(),
        P("rows", "cols", "rel", None),
        P("rows", "cols", "rel", None, None, None),
    )
    out_specs = P(("rows", "cols", "rel"), None)
    return jax.shard_map(on_device, mesh=mesh, in_specs=in_specs, out_specs=out_specs, check_vma=False)
```

time: 356 us -> 143 us (0.40)
  other arithmetic: 90.9 us -> 0.99 us
  waiting for transfers between devices: 105 us -> 23.8 us
  local copies, waits for them, and re-layouts: 70.8 us -> 28.1 us
  matrix products: 39.6 us -> 0 us
  Pallas kernels: 0 us -> 39.4 us
  starting transfers between devices: 0.04 us -> 13.4 us
  between operations: 13.5 us -> 0.23 us
    reduce_scatter x1 -> x0, waiting for transfers between devices: 73 us -> none  [on_device(): lax.psum_scatter(term, ('cols', 'rel'), scatter_dimension=0, tiled=True)]
    scatter-add x1 -> x0, other arithmetic: 72.6 us -> none  [on_device(): jnp.zeros((nblk, block, width), jnp.float32).at[target].add(contrib)]
    dot_general x4 -> x0, matrix products: 39.6 us -> none  [the longest x1 20.1 us: on_device(): jnp.einsum('sij,sjd->sid', weight, source_rows, preferred_element_type=jn...]
    pallas_call x0 -> x7, Pallas kernels: none -> 39.4 us  [the longest x1 14.9 us: sibling_part(): pl.pallas_call(sib_kernel, grid=(HSTEPS,), in_specs=[SMEM_SPEC, SMEM_SPEC...]
    slice x2 -> x0, local copies, waits for them, and re-layouts: 38.5 us -> none  [on_device(): transformed[:per_group].astype(jnp.bfloat16)]
    all_to_all x0 -> x1, blocking collectives: none -> 36.5 us  [on_device(): parts = lax.all_to_all(both.reshape(8, 2, WIDTH, BLOCK), 'cols', 0, 0)]
    psum x1 -> x0, blocking collectives: 35 us -> none  [on_device(): degree = lax.psum(deg_part.astype(jnp.bfloat16), 'cols').astype(jnp.float32)]
    all_gather x1 -> x0, waiting for transfers between devices: 31.3 us -> none  [on_device(): panel = lax.all_gather(features, 'rows', axis=1, tiled=True)]
  transfers between devices with their start and end apart: 2 -> 5, of which waited for: 2 -> 2; matrix products, arithmetic and copies ran while one was open for 3% -> 1% of each run, Pallas kernels for 0% -> 16%
where the time goes in v2:
time: 143 us; the launch traced here: 142 us
  Pallas kernels  39.4 us (28%)
  blocking collectives  36.5 us (26%)
  local copies, waits for them, and re-layouts  28.1 us (20%)
  waiting for transfers between devices  23.8 us (17%)
  starting transfers between devices  13.4 us (9%)
    all_to_all x1, blocking collectives, on_device(): parts = lax.all_to_all(both.reshape(8, 2, WIDTH, BLOCK), 'cols', 0, 0)  36.5 us
    unnamed x30, local copies, waits for them, and re-layouts  26 us
    pallas_call x1, Pallas kernels, sibling_part(): pl.pallas_call(sib_kernel, grid=(HSTEPS,), in_specs=[SMEM_SPEC, SMEM_SPEC...  14.9 us
    all_to_all x1, waiting for transfers between devices, on_device(): lax.all_to_all(jnp.broadcast_to(x_half[None], (8, PIECE, HALF)), 'rows',...  14.7 us
    all_to_all x1, waiting for transfers between devices, on_device(): degrees = lax.all_to_all(deg_parts, 'cols', 0, 0)  9.06 us
    all_to_all x1, starting transfers between devices, on_device(): lax.all_to_all(jnp.broadcast_to(x_half[None], (8, PIECE, HALF)), 'rows',...  8 us
    pallas_call x1, Pallas kernels, own_hidden(): pl.pallas_call(own_hidden_kernel, grid=(HSTEPS,), in_specs=[SMEM_SPEC, pl...  7.42 us
    pallas_call x1, Pallas kernels, own_part(): pl.pallas_call(own_kernel, in_specs=[SMEM_SPEC, SMEM_SPEC, VMEM_SPEC, VME...  5.14 us
  transfers between devices with their start and end apart: 5, of which 2 were waited for; matrix products, arithmetic and copies ran while one was open for 1% of the time, Pallas kernels for 16%

profile of v2, /device:TPU:0, one launch (start us, length us, event | category | flops | bytes accessed | tf_op | source)
XLA Modules:
  0.0 142.5 jit_solution(12217810357754515471)
XLA Ops:
  0.0 1.0 copy-done
  1.1 1.6 %broadcast_in_dim.83 = bf16[8,64,2048]{2,1,0:T(8,128)(2,1)} broadcast(bf16[64,2048]{1,0:T(8,128)(2,1)S(1)} %dynamic-slice_bitcast_fusion), dimensions={1,2} | broadcast | bytes 2359296 | tf_op jit(solution)/shard_map/broadcast_in_dim | solution.py:292
  2.7 8.0 %all-to-all-start.1 = ((bf16[8,64,2048]{2,1,0:T(8,128)(2,1)}), bf16[8,64,2048]{2,1,0:T(8,128)(2,1)S(1)}, u32[]{:S(2)}, u32[]{:S(2)}) async-start(bf16[8,64,2048]{2,1,0:T(8,128)(2,1)} %broadcast_in_dim.83), calls=%async_computation.1 | async-start | bytes 4194304 | tf_op jit(solution)/shard_map/all_to_all | solution.py:292
  10.7 3.4 %copy-done.5 = s32[1,1,1,128,128,128]{5,4,3,2,1,0:T(8,128)S(1)} copy-done((s32[1,1,1,128,128,128]{5,4,3,2,1,0:T(8,128)S(1)}, s32[1,1,1,128,128,128]{5,4,3,2,1,0:T(8,128)}, u32[]{:S(2)}) %copy-start.5) | copy-done | bytes 8388632
  14.1 1.6 %copy-done.10 = bf16[4,512,512]{2,1,0:T(8,128)(2,1)S(1)} copy-done((bf16[4,512,512]{2,1,0:T(8,128)(2,1)S(1)}, bf16[4,512,512]{2,1,0:T(8,128)(2,1)}, u32[]{:S(2)}) %copy-start.10) | copy-done | bytes 2097176
  15.6 4.0 %prep.1 = (f32[8,128,128]{2,1,0:T(8,128)S(1)}, bf16[128,128,128]{2,1,0:T(8,128)(2,1)S(1)}, bf16[4,512,512]{2,1,0:T(8,128)(2,1)S(1)}) custom-call(s32[128]{0:T(128)S(1)} %bitcast.14, s32[128,128,128]{2,1,0:T(8,128)S(1)} %bitcast.12, bf16[4,512,512]{2,1,0:T(8,128)(2,1)S(1)} %copy-done.10), custom_call_target="tpu_custom_call" | custom-call | flops 33554432 | bytes 10485760 | tf_op jit(solution)/shard_map/prep/pallas_call | solution.py:56
  19.6 1.9 %copy-done.6 = bf16[128,128,128]{2,1,0:T(8,128)(2,1)} copy-done((bf16[128,128,128]{2,1,0:T(8,128)(2,1)}, bf16[128,128,128]{2,1,0:T(8,128)(2,1)S(1)}, u32[]{:S(2)}) %copy-start.6) | copy-done | bytes 4194328
  21.6 1.3 copy-done.8
  22.9 0.8 copy-done.11
  24.4 14.7 %all-to-all-done.1 = bf16[8,64,2048]{2,1,0:T(8,128)(2,1)S(1)} async-done(((bf16[8,64,2048]{2,1,0:T(8,128)(2,1)}), bf16[8,64,2048]{2,1,0:T(8,128)(2,1)S(1)}, u32[]{:S(2)}, u32[]{:S(2)}) %all-to-all-start.1) | async-done | bytes 2097184 | tf_op jit(solution)/shard_map/all_to_all | solution.py:292
  39.1 4.8 %all-to-all-start = ((f32[8,128,128]{2,1,0:T(8,128)}), f32[8,128,128]{2,1,0:T(8,128)S(1)}, u32[]{:S(2)}, u32[]{:S(2)}) async-start(f32[8,128,128]{2,1,0:T(8,128)} %copy-done.11), calls=%async_computation | async-start | bytes 1048576 | tf_op jit(solution)/shard_map/all_to_all | solution.py:296
  44.7 9.1 %all-to-all-done.deg_ref = f32[8,128,128]{2,1,0:T(8,128)S(1)} async-done(((f32[8,128,128]{2,1,0:T(8,128)}), f32[8,128,128]{2,1,0:T(8,128)S(1)}, u32[]{:S(2)}, u32[]{:S(2)}) %all-to-all-start) | async-done | bytes 524320 | tf_op jit(solution)/shard_map/all_to_all | solution.py:296
  53.8 2.2 %copy-done.7 = bf16[128,128,128]{2,1,0:T(8,128)(2,1)S(1)} copy-done((bf16[128,128,128]{2,1,0:T(8,128)(2,1)S(1)}, bf16[128,128,128]{2,1,0:T(8,128)(2,1)}, u32[]{:S(2)}) %copy-start.7) | copy-done | bytes 4194328
  56.0 4.4 %scale.1.w_ref = bf16[129,128,128]{2,1,0:T(8,128)(2,1)S(1)} custom-call(s32[128]{0:T(128)S(1)} %bitcast.16, f32[8,128,128]{2,1,0:T(8,128)S(1)} %all-to-all-done.deg_ref, bf16[128,128,128]{2,1,0:T(8,128)(2,1)S(1)} %copy-done.7), custom_call_target="tpu_custom_call" | custom-call | flops 8388608 | bytes 8388608 | tf_op jit(solution)/shard_map/scale/pallas_call | solution.py:95
  60.3 7.4 %own_hidden.1.hid_in = bf16[128,512,128]{2,1,0:T(8,128)(2,1)S(1)} custom-call(s32[1]{0:T(128)} %bitcast.2.core_ref, bf16[512,2048]{1,0:T(8,128)(2,1)S(1)} %bitcast.10, bf16[4,512,512]{2,1,0:T(8,128)(2,1)S(1)} %copy-done.9), custom_call_target="tpu_custom_call" | custom-call | flops 4294967296 | bytes 4194304 | tf_op jit(solution)/shard_map/own_hidden/pallas_call | solution.py:129
  67.8 14.9 %sibling_part.1 = (bf16[128,512,128]{2,1,0:T(8,128)(2,1)S(1)}, bf16[16,512,128]{2,1,0:T(8,128)(2,1)}) custom-call(s32[1]{0:T(128)} %bitcast.2.core_ref, s32[136]{0:T(256)S(1)} %concatenate.3.codes_ref, s32[2,4,72]{2,1,0:T(4,128)S(1)} %pad_add_fusion.pairs_ref, bf16[512,2048]{1,0:T(8,128)(2,1)} %collective-permute-done.x_ref, ...), custom_call_target="tpu_custom_call", output_to_operand_aliasing={{0}: (6, {})} | custom-call | flops 8589934592 | bytes 4194304 | tf_op jit(solution)/shard_map/sibling_part/pallas_call | solution.py:176
  82.7 5.7 %copy-done.1 = bf16[128,512,128]{2,1,0:T(8,128)(2,1)} copy-done((bf16[128,512,128]{2,1,0:T(8,128)(2,1)}, bf16[128,512,128]{2,1,0:T(8,128)(2,1)S(1)}, u32[]{:S(2)}) %copy-start.1) | copy-done | bytes 16777240
  88.4 0.7 collective-permute-start.2
  89.1 5.8 %copy-done.2 = bf16[128,512,128]{2,1,0:T(8,128)(2,1)S(1)} copy-done((bf16[128,512,128]{2,1,0:T(8,128)(2,1)S(1)}, bf16[128,512,128]{2,1,0:T(8,128)(2,1)}, u32[]{:S(2)}) %copy-start.2) | copy-done | bytes 16777240
  94.9 2.2 %copy-done.4 = bf16[129,128,128]{2,1,0:T(8,128)(2,1)S(1)} copy-done((bf16[129,128,128]{2,1,0:T(8,128)(2,1)S(1)}, bf16[129,128,128]{2,1,0:T(8,128)(2,1)}, u32[]{:S(2)}) %copy-start.4) | copy-done | bytes 4227096
  97.1 5.1 %own_part.1.own_ref = f32[16,512,128]{2,1,0:T(8,128)S(1)} custom-call(s32[136]{0:T(256)S(1)} %concatenate.3.codes_ref, s32[2,4,72]{2,1,0:T(4,128)S(1)} %pad_add_fusion.pairs_ref, bf16[129,128,128]{2,1,0:T(8,128)(2,1)S(1)} %copy-done.4, bf16[128,512,128]{2,1,0:T(8,128)(2,1)S(1)} %copy-done.2), custom_call_target="tpu_custom_call" | custom-call | flops 4294967296 | bytes 4194304 | tf_op jit(solution)/shard_map/own_part/pallas_call | solution.py:206
  102.2 2.5 %join.1 = bf16[16,512,128]{2,1,0:T(8,128)(2,1)S(1)} custom-call(f32[16,512,128]{2,1,0:T(8,128)S(1)} %own_part.1.own_ref, bf16[16,512,128]{2,1,0:T(8,128)(2,1)} %collective-permute-done.1.other_ref), custom_call_target="tpu_custom_call" | custom-call | flops 1048576 | bytes 8388608 | tf_op jit(solution)/shard_map/join/pallas_call | solution.py:223
  104.8 36.5 %all_to_all.15.parts_ref = bf16[8,2,512,128]{3,2,1,0:T(8,128)(2,1)S(1)} all-to-all(bf16[8,2,512,128]{3,2,1,0:T(8,128)(2,1)S(1)} %bitcast.13), channel_id=1, replica_groups=mesh['rows'=8,'cols'=8,'rel'=2] {'cols'}, dimensions={0} | all-to-all | bytes 4194304 | tf_op jit(solution)/shard_map/all_to_all | solution.py:313
  141.3 1.1 finish.1
  (49 shorter events, 1.5 us)
Async XLA Ops:
  0.0 1.0 copy-start
  2.7 8.0 %copy-start.13 = (s32[1,1,1,128]{3,2,1,0:T(1,128)S(1)}, s32[1,1,1,128]{3,2,1,0:T(1,128)}, u32[]{:S(2)}) copy-start(s32[1,1,1,128]{3,2,1,0:T(1,128)} %param.10) | copy-start | bytes 1540
  2.7 36.4 %all-to-all-start.1 = ((bf16[8,64,2048]{2,1,0:T(8,128)(2,1)}), bf16[8,64,2048]{2,1,0:T(8,128)(2,1)S(1)}, u32[]{:S(2)}, u32[]{:S(2)}) async-start(bf16[8,64,2048]{2,1,0:T(8,128)(2,1)} %broadcast_in_dim.83), calls=%async_computation.1 | async-start | bytes 4194304 | tf_op jit(solution)/shard_map/all_to_all | solution.py:292
  10.7 3.4 %copy-start.5 = (s32[1,1,1,128,128,128]{5,4,3,2,1,0:T(8,128)S(1)}, s32[1,1,1,128,128,128]{5,4,3,2,1,0:T(8,128)}, u32[]{:S(2)}) copy-start(s32[1,1,1,128,128,128]{5,4,3,2,1,0:T(8,128)} %param.11) | copy-start | bytes 25165828
  14.1 1.6 %copy-start.10 = (bf16[4,512,512]{2,1,0:T(8,128)(2,1)S(1)}, bf16[4,512,512]{2,1,0:T(8,128)(2,1)}, u32[]{:S(2)}) copy-start(bf16[4,512,512]{2,1,0:T(8,128)(2,1)} %weight_ref.1) | copy-start | bytes 6291460
  19.6 1.9 %copy-start.6 = (bf16[128,128,128]{2,1,0:T(8,128)(2,1)}, bf16[128,128,128]{2,1,0:T(8,128)(2,1)S(1)}, u32[]{:S(2)}) copy-start(bf16[128,128,128]{2,1,0:T(8,128)(2,1)S(1)} %get-tuple-element.13.cnt_ref) | copy-start | bytes 12582916
  21.6 1.3 copy-start.8
  22.9 0.8 copy-start.11
  39.1 14.7 %all-to-all-start = ((f32[8,128,128]{2,1,0:T(8,128)}), f32[8,128,128]{2,1,0:T(8,128)S(1)}, u32[]{:S(2)}, u32[]{:S(2)}) async-start(f32[8,128,128]{2,1,0:T(8,128)} %copy-done.11), calls=%async_computation | async-start | bytes 1048576 | tf_op jit(solution)/shard_map/all_to_all | solution.py:296
  43.9 23.9 %collective-permute-start = (bf16[512,2048]{1,0:T(8,128)(2,1)S(1)}, bf16[512,2048]{1,0:T(8,128)(2,1)}, u32[]{:S(2)}, u32[]{:S(2)}) collective-permute-start(bf16[512,2048]{1,0:T(8,128)(2,1)S(1)} %bitcast.9), channel_id=1, source_target_pairs={{0,1},{1,0},{2,3},{3,2},{4,5},{5,4},{6,7},{7,6},{8,9},{9,8},{10,11... | collective-permute-start | bytes 6291464 | tf_op jit(solution)/shard_map/ppermute | solution.py:281
  53.8 2.2 %copy-start.7 = (bf16[128,128,128]{2,1,0:T(8,128)(2,1)S(1)}, bf16[128,128,128]{2,1,0:T(8,128)(2,1)}, u32[]{:S(2)}) copy-start(bf16[128,128,128]{2,1,0:T(8,128)(2,1)} %copy-done.6) | copy-start | bytes 12582916
  56.0 4.4 %copy-start.9 = (bf16[4,512,512]{2,1,0:T(8,128)(2,1)S(1)}, bf16[4,512,512]{2,1,0:T(8,128)(2,1)}, u32[]{:S(2)}) copy-start(bf16[4,512,512]{2,1,0:T(8,128)(2,1)} %copy-done.8) | copy-start | bytes 6291460
  60.3 7.5 %copy-start.3 = (bf16[129,128,128]{2,1,0:T(8,128)(2,1)}, bf16[129,128,128]{2,1,0:T(8,128)(2,1)S(1)}, u32[]{:S(2)}) copy-start(bf16[129,128,128]{2,1,0:T(8,128)(2,1)S(1)} %scale.1.w_ref) | copy-start | bytes 12681220
  82.7 5.7 %copy-start.1 = (bf16[128,512,128]{2,1,0:T(8,128)(2,1)}, bf16[128,512,128]{2,1,0:T(8,128)(2,1)S(1)}, u32[]{:S(2)}) copy-start(bf16[128,512,128]{2,1,0:T(8,128)(2,1)S(1)} %get-tuple-element.15.hid_ref) | copy-start | bytes 50331652
  88.4 13.8 %collective-permute-start.1 = (bf16[16,512,128]{2,1,0:T(8,128)(2,1)}, bf16[16,512,128]{2,1,0:T(8,128)(2,1)}, u32[]{:S(2)}, u32[]{:S(2)}) collective-permute-start(bf16[16,512,128]{2,1,0:T(8,128)(2,1)} %get-tuple-element.16), channel_id=1, source_target_pairs={{0,1},{1,0},{2,3},{3,2},{4,5},{5,4},{6,7},{7,6},{8,9},{9,8},{10,11... | collective-permute-start | bytes 6291464 | tf_op jit(solution)/shard_map/ppermute | solution.py:281
  88.4 16.3 %collective-permute-start.2 = (bf16[512,256]{1,0:T(8,128)(2,1)S(1)}, bf16[512,256]{1,0:T(8,128)(2,1)S(1)}, u32[]{:S(2)}, u32[]{:S(2)}) collective-permute-start(bf16[512,256]{1,0:T(8,128)(2,1)S(1)} %constant_dynamic-slice_fusion), channel_id=1, source_target_pairs={{0,0},{1,8},{2,16},{3,24},{4,32},{5,40},{6,48},{7,56},{8,64},{9,72... | collective-permute-start | bytes 786440 | tf_op jit(solution)/shard_map/ppermute | solution.py:305
  89.1 5.8 %copy-start.2 = (bf16[128,512,128]{2,1,0:T(8,128)(2,1)S(1)}, bf16[128,512,128]{2,1,0:T(8,128)(2,1)}, u32[]{:S(2)}) copy-start(bf16[128,512,128]{2,1,0:T(8,128)(2,1)} %copy-done.1) | copy-start | bytes 50331652
  94.9 2.2 %copy-start.4 = (bf16[129,128,128]{2,1,0:T(8,128)(2,1)S(1)}, bf16[129,128,128]{2,1,0:T(8,128)(2,1)}, u32[]{:S(2)}) copy-start(bf16[129,128,128]{2,1,0:T(8,128)(2,1)} %copy-done.3) | copy-start | bytes 12681220
  104.8 36.6 %copy-start.12 = (bf16[512,512]{1,0:T(8,128)(2,1)S(1)}, bf16[512,512]{1,0:T(8,128)(2,1)}, u32[]{:S(2)}) copy-start(bf16[512,512]{1,0:T(8,128)(2,1)} %w_ref.1) | copy-start | bytes 1572868
  104.8 36.6 %copy-start.14 = (f32[512]{0:T(512)S(1)}, f32[512]{0:T(512)}, u32[]{:S(2)}) copy-start(f32[512]{0:T(512)} %param.9) | copy-start | bytes 6148

commit v3 on v2

v3 whole, which is shorter than its diff:
```python
import jax
import jax.numpy as jnp
from jax import lax
from jax.experimental import pallas as pl
from jax.experimental.pallas import tpu as pltpu
from jax.sharding import PartitionSpec as P

BLOCK = 128
WIDTH = 512
NBLK = 32
NREL = 4
SLOTS = 128
PIECE = 64
NODES = NBLK * BLOCK
HALF = NODES // 2
CHUNK = 512
UNROLL = 8
PAIRS = 72
MIB = 1024 * 1024
NT = (((1,), (1,)), ((), ()))
TN = (((0,), (0,)), ((), ()))
VMEM_SPEC = pl.BlockSpec(memory_space=pltpu.VMEM)
SMEM_SPEC = pl.BlockSpec(memory_space=pltpu.SMEM)


def params(mib):
    return pltpu.CompilerParams(vmem_limit_bytes=mib * MIB)


def prep_kernel(codes_ref, counts_ref, weight_ref, deg_ref, wt_ref):
    step = pl.program_id(0)

    @pl.when(step == 0)
    def _():
        deg_ref[...] = jnp.zeros_like(deg_ref)

    per = counts_ref.shape[0]
    ones = jnp.ones((8, BLOCK), jnp.bfloat16)
    for s in range(per):
        c = counts_ref[s].astype(jnp.float32).astype(jnp.bfloat16)
        row = lax.dot_general(ones, c, NT, preferred_element_type=jnp.float32)
        seg = lax.shift_right_logical(codes_ref[step * per + s], 5)
        deg_ref[pl.ds(seg, 1), :] += row[0:1]
    wt_ref[0] = weight_ref[0].T


def prep(codes, counts, rel_weight):
    per = 16
    return pl.pallas_call(
        prep_kernel,
        grid=(SLOTS // per,),
        in_specs=[
            SMEM_SPEC,
            pl.BlockSpec((per, BLOCK, BLOCK), lambda i: (i, 0, 0)),
            pl.BlockSpec((1, WIDTH, 256), lambda i: (i // 2, 0, i % 2)),
        ],
        out_specs=[
            pl.BlockSpec((NREL * NBLK, BLOCK), lambda i: (0, 0)),
            pl.BlockSpec((1, 256, WIDTH), lambda i: (i // 2, i % 2, 0)),
        ],
        out_shape=[
            jax.ShapeDtypeStruct((NREL * NBLK, BLOCK), jnp.float32),
            jax.ShapeDtypeStruct((NREL, WIDTH, WIDTH), jnp.bfloat16),
        ],
        compiler_params=params(58),
        cost_estimate=pl.CostEstimate(flops=2 * SLOTS * BLOCK * BLOCK * 8, bytes_accessed=12 * MIB, transcendentals=0),
        name="prep",
    )(codes, counts, rel_weight)


def scale_kernel(codes_ref, *refs):
    deg_refs, (counts_ref, out_ref, inv_ref) = refs[:8], refs[8:]
    step = pl.program_id(0)

    @pl.when(step == 0)
    def _():
        degree = deg_refs[0][...]
        for ref in deg_refs[1:]:
            degree = degree + ref[...]
        inv_ref[...] = (1.0 / jnp.maximum(degree, 1.0)).T

    per = counts_ref.shape[0]
    for u in range(per):
        slot = step * per + u
        seg = lax.shift_right_logical(codes_ref[slot], 5)
        scale = jnp.take_along_axis(inv_ref[...], jnp.full((BLOCK, BLOCK), seg, jnp.int32), axis=1)
        out_ref[u] = (counts_ref[u].astype(jnp.float32) * scale).astype(jnp.bfloat16)


def scaled(codes, degrees, counts):
    per = 16
    return pl.pallas_call(
        scale_kernel,
        grid=(SLOTS // per,),
        in_specs=[SMEM_SPEC]
        + [pl.BlockSpec((NREL * NBLK, BLOCK), lambda i: (0, 0))] * 8
        + [pl.BlockSpec((per, BLOCK, BLOCK), lambda i: (i, 0, 0))],
        out_specs=pl.BlockSpec((per, BLOCK, BLOCK), lambda i: (i, 0, 0)),
        out_shape=jax.ShapeDtypeStruct((SLOTS, BLOCK, BLOCK), jnp.bfloat16),
        scratch_shapes=[pltpu.VMEM((BLOCK, BLOCK), jnp.float32)],
        compiler_params=params(58),
        cost_estimate=pl.CostEstimate(flops=4 * SLOTS * BLOCK * BLOCK, bytes_accessed=13 * MIB, transcendentals=0),
        name="scale",
    )(codes, *degrees, counts)


HID = (NREL * NBLK, WIDTH, BLOCK)


def hidden_half(half, x_ref, wt_ref, hid_ref, ready):
    per = CHUNK // BLOCK

    def one(r, carry):
        ready(r)
        for n in range(HALF // CHUNK):
            x = x_ref[:, n * CHUNK : (n + 1) * CHUNK]
            h = jnp.dot(wt_ref[r], x, preferred_element_type=jnp.float32).astype(jnp.bfloat16)
            for b in range(per):
                hid_ref[r * NBLK + half * (NBLK // 2) + n * per + b] = h[:, b * BLOCK : (b + 1) * BLOCK]
        return carry

    lax.fori_loop(0, NREL, one, 0)


def own_hidden_kernel(place_ref, x_ref, wt_hbm, w_hbm, hid_ref, wt_ref, w_ref, rows_ref, sems):
    copies = [pltpu.make_async_copy(wt_hbm.at[r], wt_ref.at[r], sems.at[r]) for r in range(NREL)]
    copies.append(pltpu.make_async_copy(w_hbm, w_ref.at[pl.ds(0, SLOTS)], sems.at[NREL]))
    for copy in copies:
        copy.start()
    w_ref[SLOTS] = jnp.zeros((BLOCK, BLOCK), jnp.bfloat16)
    at = pl.multiple_of(place_ref[1] * (2 * BLOCK), 2 * BLOCK)
    rows_ref[...] = x_ref[:, pl.ds(at, 2 * BLOCK)]

    def ready(r):
        pltpu.make_async_copy(wt_hbm.at[r], wt_ref.at[r], sems.at[r]).wait()

    hidden_half(place_ref[0], x_ref, wt_ref, hid_ref, ready)
    copies[-1].wait()


def own_hidden(place, x, wt, w):
    return pl.pallas_call(
        own_hidden_kernel,
        in_specs=[SMEM_SPEC, VMEM_SPEC, pl.BlockSpec(memory_space=pl.ANY), pl.BlockSpec(memory_space=pl.ANY)],
        out_specs=[VMEM_SPEC] * 4,
        out_shape=[
            pltpu.VMEM(HID, jnp.bfloat16),
            pltpu.VMEM((NREL, WIDTH, WIDTH), jnp.bfloat16),
            pltpu.VMEM((SLOTS + 1, BLOCK, BLOCK), jnp.bfloat16),
            jax.ShapeDtypeStruct((WIDTH, 2 * BLOCK), jnp.bfloat16),
        ],
        scratch_shapes=[pltpu.SemaphoreType.DMA((NREL + 1,))],
        compiler_params=params(12),
        cost_estimate=pl.CostEstimate(flops=2 * HALF * WIDTH * WIDTH * NREL, bytes_accessed=8 * MIB, transcendentals=0),
        name="own_hidden",
    )(place, x, wt, w)


def slot_pairs(codes_ref, pairs_ref, which, hid_ref, w_ref, acc_ref):
    def some(q, carry):
        for u in range(UNROLL):
            k = q * UNROLL + u
            s1, s2, place = pairs_ref[which, 0, k], pairs_ref[which, 1, k], pairs_ref[which, 2, k]
            hs = []
            for s in (s1, s2):
                code = codes_ref[s]
                hs.append(hid_ref[lax.shift_right_logical(code, 10) * NBLK + jnp.bitwise_and(code, NBLK - 1)])
            h = jnp.concatenate(hs, axis=1)
            w = jnp.concatenate([w_ref[s1], w_ref[s2]], axis=1)
            acc_ref[place] += lax.dot_general(h, w, NT, preferred_element_type=jnp.float32)
        return carry

    lax.fori_loop(0, pairs_ref[which, 3, 0], some, 0)


def clear(acc):
    def one(t, carry):
        acc[t] = jnp.zeros((WIDTH, BLOCK), jnp.float32)
        return carry

    lax.fori_loop(0, NBLK // 2, one, 0)


def sib_kernel(place_ref, codes_ref, pairs_ref, x_ref, wt_ref, w_ref, hid_in, hid_ref, out_ref, acc):
    hidden_half(1 - place_ref[0], x_ref, wt_ref, hid_ref, lambda r: None)
    clear(acc)
    slot_pairs(codes_ref, pairs_ref, 0, hid_ref, w_ref, acc)

    def one(t, carry):
        out_ref[t] = acc[t].astype(jnp.bfloat16)
        return carry

    lax.fori_loop(0, NBLK // 2, one, 0)


def sibling_part(place, codes, pairs, x, wt, w, hid):
    return pl.pallas_call(
        sib_kernel,
        in_specs=[SMEM_SPEC] * 3 + [VMEM_SPEC] * 4,
        out_specs=[VMEM_SPEC, VMEM_SPEC],
        out_shape=[
            pltpu.VMEM(HID, jnp.bfloat16),
            pltpu.VMEM((NBLK // 2, WIDTH, BLOCK), jnp.bfloat16),
        ],
        input_output_aliases={6: 0},
        scratch_shapes=[pltpu.VMEM((NBLK // 2, WIDTH, BLOCK), jnp.float32)],
        compiler_params=params(16),
        cost_estimate=pl.CostEstimate(flops=2 * HALF * WIDTH * WIDTH * NREL * 2, bytes_accessed=4 * MIB, transcendentals=0),
        name="sibling_part",
    )(place, codes, pairs, x, wt, w, hid)


def own_kernel(codes_ref, pairs_ref, w_ref, hid_ref, acc):
    clear(acc)
    slot_pairs(codes_ref, pairs_ref, 1, hid_ref, w_ref, acc)


def own_part(codes, pairs, w, hid):
    return pl.pallas_call(
        own_kernel,
        in_specs=[SMEM_SPEC, SMEM_SPEC, VMEM_SPEC, VMEM_SPEC],
        out_specs=VMEM_SPEC,
        out_shape=pltpu.VMEM((NBLK // 2, WIDTH, BLOCK), jnp.float32),
        compiler_params=params(12),
        cost_estimate=pl.CostEstimate(flops=2 * HALF * WIDTH * WIDTH * NREL, bytes_accessed=4 * MIB, transcendentals=0),
        name="own_part",
    )(codes, pairs, w, hid)


def join_kernel(own_ref, other_ref, out_ref):
    per = out_ref.shape[0]
    step = pl.program_id(0)
    for t in range(per):
        out_ref[t] = (own_ref[step * per + t] + other_ref[t].astype(jnp.float32)).astype(jnp.bfloat16)


def join(own, other):
    spec = pl.BlockSpec((4, WIDTH, BLOCK), lambda i: (i, 0, 0))
    return pl.pallas_call(
        join_kernel,
        grid=(NBLK // 2 // 4,),
        in_specs=[VMEM_SPEC, spec],
        out_specs=spec,
        out_shape=jax.ShapeDtypeStruct((NBLK // 2, WIDTH, BLOCK), jnp.bfloat16),
        compiler_params=params(12),
        cost_estimate=pl.CostEstimate(flops=MIB, bytes_accessed=8 * MIB, transcendentals=0),
        name="join",
    )(own, other)


def finish_kernel(parts_ref, x_ref, w_ref, bias_ref, out_ref):
    self_part = lax.dot_general(x_ref[...], w_ref[...], TN, preferred_element_type=jnp.float32)
    for b in range(2):
        total = parts_ref[0, b].astype(jnp.float32)
        for k in range(1, parts_ref.shape[0]):
            total = total + parts_ref[k, b].astype(jnp.float32)
        rows = slice(b * BLOCK, (b + 1) * BLOCK)
        out_ref[rows, :] = jnp.maximum(total.T + self_part[rows] + bias_ref[...], 0.0).astype(jnp.bfloat16)


def finish(parts, x_own, self_weight, bias):
    return pl.pallas_call(
        finish_kernel,
        out_shape=jax.ShapeDtypeStruct((2 * BLOCK, WIDTH), jnp.bfloat16),
        compiler_params=params(32),
        name="finish",
    )(parts, x_own, self_weight, bias.reshape(1, WIDTH))


def pair_lists(codes, core):
    slots = jnp.arange(SLOTS, dtype=jnp.int32)
    target = codes // NBLK % NBLK
    half = (target // 2 % 2 == core).astype(jnp.int32)
    place = target // 4 * 2 + target % 2
    group = half * (NBLK // 2) + place
    same = group[None, :] == group[:, None]
    nth = jnp.sum((same & (slots[None, :] < slots[:, None])).astype(jnp.int32), axis=1)
    groups = jnp.arange(NBLK, dtype=jnp.int32)
    size = jnp.sum((group[None, :] == groups[:, None]).astype(jnp.int32), axis=1)
    need = (size + 1) // 2
    before = (groups[None, :] < groups[:, None]) & (groups[None, :] // (NBLK // 2) == groups[:, None] // (NBLK // 2))
    base = jnp.sum(jnp.where(before, need[None, :], 0), axis=1)
    at = half * PAIRS + nth // 2 + jnp.sum(jnp.where(group[:, None] == groups[None, :], base[None, :], 0), axis=1)
    entries = jnp.arange(2 * PAIRS, dtype=jnp.int32)
    match = at[None, :] == entries[:, None]
    is_first = match & (nth % 2 == 0)[None, :]
    is_second = match & (nth % 2 == 1)[None, :]
    first = SLOTS + jnp.sum(jnp.where(is_first, slots[None, :] - SLOTS, 0), axis=1)
    second = SLOTS + jnp.sum(jnp.where(is_second, slots[None, :] - SLOTS, 0), axis=1)
    where = jnp.sum(jnp.where(is_first, place[None, :], 0), axis=1)
    steps = (jnp.sum(need.reshape(2, NBLK // 2), axis=1) + UNROLL - 1) // UNROLL
    steps = jnp.broadcast_to(steps[:, None], (2, PAIRS))
    return jnp.stack([first.reshape(2, PAIRS), second.reshape(2, PAIRS), where.reshape(2, PAIRS), steps], axis=1)


def swap(array):
    return lax.ppermute(array, "rel", [(0, 1), (1, 0)])


def gather_half(x_half):
    return lax.all_to_all(jnp.broadcast_to(x_half[None], (8, PIECE, HALF)), "rows", 0, 0).reshape(WIDTH, HALF)


def on_device(features, rel_weight, self_weight, bias, block_code, block_counts):
    row, core = lax.axis_index("rows"), lax.axis_index("rel")
    codes = block_code[0, 0, 0]
    counts = block_counts[0, 0, 0]
    place = jnp.stack([core, row]).astype(jnp.int32)
    padded = jnp.concatenate([codes, jnp.zeros((8,), jnp.int32)])

    x_half = lax.dynamic_slice(features.T, (0, core * HALF), (PIECE, HALF))
    x_mine = gather_half(x_half)

    deg_part, wt = prep(codes, counts, rel_weight)
    degrees = [deg_part] + [lax.ppermute(deg_part, "cols", [(i, (i + k) % 8) for i in range(8)]) for k in range(1, 8)]
    w = scaled(codes, degrees, counts)
    pairs = pair_lists(codes, core)
    x_mine, w, pairs, padded, place = lax.optimization_barrier((x_mine, w, pairs, padded, place))

    x_other = swap(x_mine)
    hid, wt, w, x_rows = own_hidden(place, x_mine, wt, w)
    moves = [
        ((a * 8 + b) * 2 + g, (b * 8 + 4 * g + a // 2) * 2 + a % 2) for a in range(8) for b in range(8) for g in range(2)
    ]
    x_own = lax.ppermute(x_rows, ("rows", "cols", "rel"), moves)
    hid, to_sib = sibling_part(place, padded, pairs, x_other, wt, w, hid)
    other = swap(to_sib)
    own = own_part(padded, pairs, w, hid)
    both = join(own, other)
    both, x_own = lax.optimization_barrier((both, x_own))
    parts = lax.all_to_all(both.reshape(8, 2, WIDTH, BLOCK), "cols", 0, 0)
    return finish(parts, x_own, self_weight, bias)


def solution(mesh):
    in_specs = (
        P("cols", "rows"),
        P("rel", None, None),
        P(),
        P(),
        P("rows", "cols", "rel", None),
        P("rows", "cols", "rel", None, None, None),
    )
    out_specs = P(("rows", "cols", "rel"), None)
    return jax.shard_map(on_device, mesh=mesh, in_specs=in_specs, out_specs=out_specs, check_vma=False)
```

time: 143 us -> 129 us (0.902); the launches traced: 142 us -> 127 us
  local copies, waits for them, and re-layouts: 28.1 us -> 6.47 us
  waiting for transfers between devices: 23.8 us -> 13.9 us
  blocking collectives: 36.5 us -> 45.1 us
  starting transfers between devices: 13.4 us -> 20 us
    unnamed x30 -> x28, local copies, waits for them, and re-layouts: 26 us -> 4.44 us
    all_to_all x2 -> x1, waiting for transfers between devices: 23.8 us -> 5.59 us  [gather_half(): lax.all_to_all(jnp.broadcast_to(x_half[None], (8, PIECE, HALF)), 'rows',...]
    ppermute x0 -> x7, starting transfers between devices: none -> 10.8 us  [on_device(): lax.ppermute(deg_part, 'cols', [(i, (i + k) % 8) for i in range(8)])]
    all_to_all x1, blocking collectives: 36.5 us -> 45.1 us  [on_device(): parts = lax.all_to_all(both.reshape(8, 2, WIDTH, BLOCK), 'cols', 0, 0)]
    ppermute x0 -> x7, waiting for transfers between devices: none -> 8.35 us  [on_device(): lax.ppermute(deg_part, 'cols', [(i, (i + k) % 8) for i in range(8)])]
    all_to_all x2 -> x1, starting transfers between devices: 12.8 us -> 7.91 us  [gather_half(): lax.all_to_all(jnp.broadcast_to(x_half[None], (8, PIECE, HALF)), 'rows',...]
    pallas_call x1, Pallas kernels: 3.98 us -> 8.33 us  [prep(): pl.pallas_call(prep_kernel, grid=(SLOTS // per,), in_specs=[SMEM_SPEC, pl...]
    pallas_call x4, Pallas kernels: 29.1 us -> 25.6 us  [the longest x1 10 us: sibling_part(): pl.pallas_call(sib_kernel, in_specs=[SMEM_SPEC] * 3 + [VMEM_SPEC] * 4, ou...]
  transfers between devices with their start and end apart: 5 -> 11, of which waited for: 2 -> 3; matrix products, arithmetic and copies ran while one was open for 1% -> 2% of each run, Pallas kernels for 16% -> 16%
where the time goes in v3:
time: 129 us; the launch traced here: 127 us
  blocking collectives  45.1 us (35%)
  Pallas kernels  39.7 us (31%)
  starting transfers between devices  20 us (16%)
  waiting for transfers between devices  13.9 us (11%)
  local copies, waits for them, and re-layouts  6.47 us (5%)
    all_to_all x1, blocking collectives, on_device(): parts = lax.all_to_all(both.reshape(8, 2, WIDTH, BLOCK), 'cols', 0, 0)  45.1 us
    ppermute x7, starting transfers between devices, on_device(): lax.ppermute(deg_part, 'cols', [(i, (i + k) % 8) for i in range(8)])  10.8 us
    pallas_call x1, Pallas kernels, sibling_part(): pl.pallas_call(sib_kernel, in_specs=[SMEM_SPEC] * 3 + [VMEM_SPEC] * 4, ou...  10 us
    pallas_call x1, Pallas kernels, scaled(): pl.pallas_call(scale_kernel, grid=(SLOTS // per,), in_specs=[SMEM_SPEC] +...  9.06 us
    ppermute x7, waiting for transfers between devices, on_device(): lax.ppermute(deg_part, 'cols', [(i, (i + k) % 8) for i in range(8)])  8.35 us
    pallas_call x1, Pallas kernels, prep(): pl.pallas_call(prep_kernel, grid=(SLOTS // per,), in_specs=[SMEM_SPEC, pl...  8.33 us
    all_to_all x1, starting transfers between devices, gather_half(): lax.all_to_all(jnp.broadcast_to(x_half[None], (8, PIECE, HALF)), 'rows',...  7.91 us
    pallas_call x1, Pallas kernels, own_hidden(): pl.pallas_call(own_hidden_kernel, in_specs=[SMEM_SPEC, VMEM_SPEC, pl.Bloc...  6.09 us
  transfers between devices with their start and end apart: 11, of which 3 were waited for; matrix products, arithmetic and copies ran while one was open for 2% of the time, Pallas kernels for 16%

profile of v3, /device:TPU:0, one launch (start us, length us, event | category | flops | bytes accessed | tf_op | source)
XLA Modules:
  0.0 126.5 jit_solution(2657854342329969093)
XLA Ops:
  0.0 8.3 %prep.1 = (f32[128,128]{1,0:T(8,128)}, bf16[4,512,512]{2,1,0:T(8,128)(2,1)}) custom-call(s32[128]{0:T(128)} %bitcast.16, s32[128,128,128]{2,1,0:T(8,128)} %bitcast.14, bf16[4,512,512]{2,1,0:T(8,128)(2,1)} %weight_ref.1), custom_call_target="tpu_custom_call" | custom-call | flops 33554432 | bytes 12582912 | tf_op jit(solution)/shard_map/prep/pallas_call | solution.py:49
  8.3 4.2 %collective-permute-start.6 = (f32[128,128]{1,0:T(8,128)}, f32[128,128]{1,0:T(8,128)S(1)}, u32[]{:S(2)}, u32[]{:S(2)}) collective-permute-start(f32[128,128]{1,0:T(8,128)} %get-tuple-element.20.refs_0_), channel_id=1, source_target_pairs={{0,14},{2,0},{4,2},{6,4},{8,6},{10,8},{12,10},{14,12},{1,15},{3,1}... | collective-permute-start | bytes 196616 | tf_op jit(solution)/shard_map/ppermute | solution.py:315
  12.5 0.8 collective-permute-start.5
  13.3 0.4 collective-permute-start.4
  13.8 1.9 %collective-permute-start.3 = (f32[128,128]{1,0:T(8,128)}, f32[128,128]{1,0:T(8,128)S(1)}, u32[]{:S(2)}, u32[]{:S(2)}) collective-permute-start(f32[128,128]{1,0:T(8,128)} %get-tuple-element.20.refs_0_), channel_id=1, source_target_pairs={{0,8},{2,10},{4,12},{6,14},{8,0},{10,2},{12,4},{14,6},{1,9},{3,11}... | collective-permute-start | bytes 196616 | tf_op jit(solution)/shard_map/ppermute | solution.py:315
  15.7 1.0 collective-permute-start.2
  16.7 1.6 %broadcast_in_dim.76 = bf16[8,64,2048]{2,1,0:T(8,128)(2,1)} broadcast(bf16[64,2048]{1,0:T(8,128)(2,1)S(1)} %dynamic-slice_bitcast_fusion), dimensions={1,2} | broadcast | bytes 2359296 | tf_op jit(solution)/shard_map/broadcast_in_dim | solution.py:301
  18.3 7.9 %all-to-all-start = ((bf16[8,64,2048]{2,1,0:T(8,128)(2,1)}), bf16[8,64,2048]{2,1,0:T(8,128)(2,1)S(1)}, u32[]{:S(2)}, u32[]{:S(2)}) async-start(bf16[8,64,2048]{2,1,0:T(8,128)(2,1)} %broadcast_in_dim.76), calls=%async_computation | async-start | bytes 4194304 | tf_op jit(solution)/shard_map/all_to_all | solution.py:301
  27.7 2.5 %collective-permute-start.1 = (f32[128,128]{1,0:T(8,128)S(1)}, f32[128,128]{1,0:T(8,128)S(1)}, u32[]{:S(2)}, u32[]{:S(2)}) collective-permute-start(f32[128,128]{1,0:T(8,128)S(1)} %copy-done.5), channel_id=1, source_target_pairs={{0,4},{2,6},{4,8},{6,10},{8,12},{10,14},{12,0},{14,2},{1,5},{3,7},... | collective-permute-start | bytes 196616 | tf_op jit(solution)/shard_map/ppermute | solution.py:315
  30.3 5.7 %collective-permute-done.1.refs_2_ = f32[128,128]{1,0:T(8,128)S(1)} collective-permute-done((f32[128,128]{1,0:T(8,128)S(1)}, f32[128,128]{1,0:T(8,128)S(1)}, u32[]{:S(2)}, u32[]{:S(2)}) %collective-permute-start.1) | collective-permute-done | bytes 65568 | tf_op jit(solution)/shard_map/ppermute | solution.py:315
  36.0 2.6 %collective-permute-done.refs_1_ = f32[128,128]{1,0:T(8,128)S(1)} collective-permute-done((f32[128,128]{1,0:T(8,128)S(1)}, f32[128,128]{1,0:T(8,128)S(1)}, u32[]{:S(2)}, u32[]{:S(2)}) %collective-permute-start) | collective-permute-done | bytes 65568 | tf_op jit(solution)/shard_map/ppermute | solution.py:315
  38.7 0.6 copy-done.12
  39.3 9.1 %scale.1.w_hbm = bf16[128,128,128]{2,1,0:T(8,128)(2,1)} custom-call(s32[128]{0:T(128)} %bitcast.17, f32[128,128]{1,0:T(8,128)} %get-tuple-element.20.refs_0_, f32[128,128]{1,0:T(8,128)} %copy-done.12, f32[128,128]{1,0:T(8,128)} %copy-done.11, f32[128,128]{1,0:T(8,128)} %copy-done.10, f32[128,128]{1,0:T(8,128)} %copy-done.9, f32[128,128]{1,0:T(8,128)} %copy-done.8, ...), custom_call_target="tpu_custom_call" | custom-call | flops 8388608 | bytes 13631488 | tf_op jit(solution)/shard_map/scale/pallas_call | solution.py:92
  48.4 5.6 %all-to-all-done = bf16[8,64,2048]{2,1,0:T(8,128)(2,1)S(1)} async-done(((bf16[8,64,2048]{2,1,0:T(8,128)(2,1)}), bf16[8,64,2048]{2,1,0:T(8,128)(2,1)S(1)}, u32[]{:S(2)}, u32[]{:S(2)}) %all-to-all-start) | async-done | bytes 2097184 | tf_op jit(solution)/shard_map/all_to_all | solution.py:301
  54.0 2.2 %copy-done.1 = bf16[128,128,128]{2,1,0:T(8,128)(2,1)S(1)} copy-done((bf16[128,128,128]{2,1,0:T(8,128)(2,1)S(1)}, bf16[128,128,128]{2,1,0:T(8,128)(2,1)}, u32[]{:S(2)}) %copy-start.1) | copy-done | bytes 4194328
  56.2 1.6 %copy-done.4 = bf16[4,512,512]{2,1,0:T(8,128)(2,1)S(1)} copy-done((bf16[4,512,512]{2,1,0:T(8,128)(2,1)S(1)}, bf16[4,512,512]{2,1,0:T(8,128)(2,1)}, u32[]{:S(2)}) %copy-start.4) | copy-done | bytes 2097176
  57.8 6.1 %own_hidden.1 = (bf16[128,512,128]{2,1,0:T(8,128)(2,1)S(1)}, bf16[4,512,512]{2,1,0:T(8,128)(2,1)S(1)}, bf16[129,128,128]{2,1,0:T(8,128)(2,1)S(1)}, bf16[512,256]{1,0:T(8,128)(2,1)S(1)}) custom-call(s32[2]{0:T(128)S(1)} %pad_add_fusion.1.place_ref, bf16[512,2048]{1,0:T(8,128)(2,1)S(1)} %bitcast.12, bf16[4,512,512]{2,1,0:T(8,128)(2,1)S(1)} %copy-done.4, ...), custom_call_target="tpu_custom_call" | custom-call | flops 4294967296 | bytes 8388608 | tf_op jit(solution)/shard_map/own_hidden/pallas_call | solution.py:142
  63.9 10.0 %sibling_part.1 = (bf16[128,512,128]{2,1,0:T(8,128)(2,1)S(1)}, bf16[16,512,128]{2,1,0:T(8,128)(2,1)S(1)}) custom-call(s32[2]{0:T(128)S(1)} %pad_add_fusion.1.place_ref, s32[136]{0:T(256)S(1)} %concatenate.3.codes_ref, s32[2,4,72]{2,1,0:T(4,128)S(1)} %pad_add_fusion.pairs_ref, ...), custom_call_target="tpu_custom_call", output_to_operand_aliasing={{0}: (6, {})} | custom-call | flops 8589934592 | bytes 4194304 | tf_op jit(solution)/shard_map/sibling_part/pallas_call | solution.py:197
  73.9 0.6 collective-permute-start.8
  74.5 0.7 collective-permute-start.9
  75.2 4.7 %own_part.1.own_ref = f32[16,512,128]{2,1,0:T(8,128)S(1)} custom-call(s32[136]{0:T(256)S(1)} %concatenate.3.codes_ref, s32[2,4,72]{2,1,0:T(4,128)S(1)} %pad_add_fusion.pairs_ref, bf16[129,128,128]{2,1,0:T(8,128)(2,1)S(1)} %get-tuple-element.27.w_ref, bf16[128,512,128]{2,1,0:T(8,128)(2,1)S(1)} %get-tuple-element.30.hid_ref), custom_call_target="tpu_custom_call" | custom-call | flops 4294967296 | bytes 4194304 | tf_op jit(solution)/shard_map/own_part/pallas_call | solution.py:219
  79.9 0.4 join.1
  80.3 45.1 %all_to_all.10.parts_ref = bf16[8,2,512,128]{3,2,1,0:T(8,128)(2,1)S(1)} all-to-all(bf16[8,2,512,128]{3,2,1,0:T(8,128)(2,1)S(1)} %bitcast.10), channel_id=1, replica_groups=mesh['rows'=8,'cols'=8,'rel'=2] {'cols'}, dimensions={0} | all-to-all | bytes 4194304 | tf_op jit(solution)/shard_map/all_to_all | solution.py:331
  125.4 1.1 finish.1
  (59 shorter events, 1.6 us)
Async XLA Ops:
  0.0 16.7 %copy-start = (bf16[4096,64]{0,1:T(8,128)(2,1)S(1)}, bf16[4096,64]{0,1:T(8,128)(2,1)}, u32[]{:S(2)}) copy-start(bf16[4096,64]{0,1:T(8,128)(2,1)} %param.6) | copy-start | bytes 1572868
  8.3 19.4 %collective-permute-start.6 = (f32[128,128]{1,0:T(8,128)}, f32[128,128]{1,0:T(8,128)S(1)}, u32[]{:S(2)}, u32[]{:S(2)}) collective-permute-start(f32[128,128]{1,0:T(8,128)} %get-tuple-element.20.refs_0_), channel_id=1, source_target_pairs={{0,14},{2,0},{4,2},{6,4},{8,6},{10,8},{12,10},{14,12},{1,15},{3,1}... | collective-permute-start | bytes 196616 | tf_op jit(solution)/shard_map/ppermute | solution.py:315
  12.5 17.7 %collective-permute-start.5 = (f32[128,128]{1,0:T(8,128)}, f32[128,128]{1,0:T(8,128)S(1)}, u32[]{:S(2)}, u32[]{:S(2)}) collective-permute-start(f32[128,128]{1,0:T(8,128)} %get-tuple-element.20.refs_0_), channel_id=1, source_target_pairs={{0,12},{2,14},{4,0},{6,2},{8,4},{10,6},{12,8},{14,10},{1,13},{3,15... | collective-permute-start | bytes 196616 | tf_op jit(solution)/shard_map/ppermute | solution.py:315
  13.3 17.0 %collective-permute-start.4 = (f32[128,128]{1,0:T(8,128)}, f32[128,128]{1,0:T(8,128)S(1)}, u32[]{:S(2)}, u32[]{:S(2)}) collective-permute-start(f32[128,128]{1,0:T(8,128)} %get-tuple-element.20.refs_0_), channel_id=1, source_target_pairs={{0,10},{2,12},{4,14},{6,0},{8,2},{10,4},{12,6},{14,8},{1,11},{3,13... | collective-permute-start | bytes 196616 | tf_op jit(solution)/shard_map/ppermute | solution.py:315
  13.8 16.5 %collective-permute-start.3 = (f32[128,128]{1,0:T(8,128)}, f32[128,128]{1,0:T(8,128)S(1)}, u32[]{:S(2)}, u32[]{:S(2)}) collective-permute-start(f32[128,128]{1,0:T(8,128)} %get-tuple-element.20.refs_0_), channel_id=1, source_target_pairs={{0,8},{2,10},{4,12},{6,14},{8,0},{10,2},{12,4},{14,6},{1,9},{3,11}... | collective-permute-start | bytes 196616 | tf_op jit(solution)/shard_map/ppermute | solution.py:315
  15.7 14.6 %collective-permute-start.2 = (f32[128,128]{1,0:T(8,128)}, f32[128,128]{1,0:T(8,128)S(1)}, u32[]{:S(2)}, u32[]{:S(2)}) collective-permute-start(f32[128,128]{1,0:T(8,128)} %get-tuple-element.20.refs_0_), channel_id=1, source_target_pairs={{0,6},{2,8},{4,10},{6,12},{8,14},{10,0},{12,2},{14,4},{1,7},{3,9},... | collective-permute-start | bytes 196616 | tf_op jit(solution)/shard_map/ppermute | solution.py:315
  18.3 7.9 %copy-start.13 = (s32[1,1,1,128]{3,2,1,0:T(1,128)S(1)}, s32[1,1,1,128]{3,2,1,0:T(1,128)}, u32[]{:S(2)}) copy-start(s32[1,1,1,128]{3,2,1,0:T(1,128)} %param.10) | copy-start | bytes 1540
  18.3 9.4 %copy-start.5 = (f32[128,128]{1,0:T(8,128)S(1)}, f32[128,128]{1,0:T(8,128)}, u32[]{:S(2)}) copy-start(f32[128,128]{1,0:T(8,128)} %get-tuple-element.20.refs_0_) | copy-start | bytes 196612
  18.3 35.7 %all-to-all-start = ((bf16[8,64,2048]{2,1,0:T(8,128)(2,1)}), bf16[8,64,2048]{2,1,0:T(8,128)(2,1)S(1)}, u32[]{:S(2)}, u32[]{:S(2)}) async-start(bf16[8,64,2048]{2,1,0:T(8,128)(2,1)} %broadcast_in_dim.76), calls=%async_computation | async-start | bytes 4194304 | tf_op jit(solution)/shard_map/all_to_all | solution.py:301
  27.7 11.0 %copy-start.6 = (f32[128,128]{1,0:T(8,128)}, f32[128,128]{1,0:T(8,128)S(1)}, u32[]{:S(2)}) copy-start(f32[128,128]{1,0:T(8,128)S(1)} %collective-permute-done.6.refs_7_) | copy-start | bytes 196612
  27.7 8.3 %collective-permute-start.1 = (f32[128,128]{1,0:T(8,128)S(1)}, f32[128,128]{1,0:T(8,128)S(1)}, u32[]{:S(2)}, u32[]{:S(2)}) collective-permute-start(f32[128,128]{1,0:T(8,128)S(1)} %copy-done.5), channel_id=1, source_target_pairs={{0,4},{2,6},{4,8},{6,10},{8,12},{10,14},{12,0},{14,2},{1,5},{3,7},... | collective-permute-start | bytes 196616 | tf_op jit(solution)/shard_map/ppermute | solution.py:315
  30.2 8.5 %copy-start.7 = (f32[128,128]{1,0:T(8,128)}, f32[128,128]{1,0:T(8,128)S(1)}, u32[]{:S(2)}) copy-start(f32[128,128]{1,0:T(8,128)S(1)} %collective-permute-done.5.refs_6_) | copy-start | bytes 196612
  30.2 8.5 %collective-permute-start = (f32[128,128]{1,0:T(8,128)S(1)}, f32[128,128]{1,0:T(8,128)S(1)}, u32[]{:S(2)}, u32[]{:S(2)}) collective-permute-start(f32[128,128]{1,0:T(8,128)S(1)} %copy-done.5), channel_id=1, source_target_pairs={{0,2},{2,4},{4,6},{6,8},{8,10},{10,12},{12,14},{14,0},{1,3},{3,5},... | collective-permute-start | bytes 196616 | tf_op jit(solution)/shard_map/ppermute | solution.py:315
  30.3 8.4 %copy-start.8 = (f32[128,128]{1,0:T(8,128)}, f32[128,128]{1,0:T(8,128)S(1)}, u32[]{:S(2)}) copy-start(f32[128,128]{1,0:T(8,128)S(1)} %collective-permute-done.4.refs_5_) | copy-start | bytes 196612
  30.3 8.4 %copy-start.9 = (f32[128,128]{1,0:T(8,128)}, f32[128,128]{1,0:T(8,128)S(1)}, u32[]{:S(2)}) copy-start(f32[128,128]{1,0:T(8,128)S(1)} %collective-permute-done.3.refs_4_) | copy-start | bytes 196612
  30.3 8.4 %copy-start.10 = (f32[128,128]{1,0:T(8,128)}, f32[128,128]{1,0:T(8,128)S(1)}, u32[]{:S(2)}) copy-start(f32[128,128]{1,0:T(8,128)S(1)} %collective-permute-done.2.refs_3_) | copy-start | bytes 196612
  36.0 2.7 %copy-start.11 = (f32[128,128]{1,0:T(8,128)}, f32[128,128]{1,0:T(8,128)S(1)}, u32[]{:S(2)}) copy-start(f32[128,128]{1,0:T(8,128)S(1)} %collective-permute-done.1.refs_2_) | copy-start | bytes 196612
  54.0 9.9 %collective-permute-start.7 = (bf16[512,2048]{1,0:T(8,128)(2,1)S(1)}, bf16[512,2048]{1,0:T(8,128)(2,1)S(1)}, u32[]{:S(2)}, u32[]{:S(2)}) collective-permute-start(bf16[512,2048]{1,0:T(8,128)(2,1)S(1)} %bitcast.11), channel_id=1, source_target_pairs={{0,1},{1,0},{2,3},{3,2},{4,5},{5,4},{6,7},{7,6},{8,9},{9,8},{10,11... | collective-permute-start | bytes 6291464 | tf_op jit(solution)/shard_map/ppermute | solution.py:297
  54.0 2.2 %copy-start.1 = (bf16[128,128,128]{2,1,0:T(8,128)(2,1)S(1)}, bf16[128,128,128]{2,1,0:T(8,128)(2,1)}, u32[]{:S(2)}) copy-start(bf16[128,128,128]{2,1,0:T(8,128)(2,1)} %scale.1.w_hbm) | copy-start | bytes 12582916
  56.2 1.6 %copy-start.4 = (bf16[4,512,512]{2,1,0:T(8,128)(2,1)S(1)}, bf16[4,512,512]{2,1,0:T(8,128)(2,1)}, u32[]{:S(2)}) copy-start(bf16[4,512,512]{2,1,0:T(8,128)(2,1)} %get-tuple-element.25.wt_hbm) | copy-start | bytes 6291460
  73.9 6.0 %collective-permute-start.8 = (bf16[16,512,128]{2,1,0:T(8,128)(2,1)S(1)}, bf16[16,512,128]{2,1,0:T(8,128)(2,1)S(1)}, u32[]{:S(2)}, u32[]{:S(2)}) collective-permute-start(bf16[16,512,128]{2,1,0:T(8,128)(2,1)S(1)} %get-tuple-element.31), channel_id=1, source_target_pairs={{0,1},{1,0},{2,3},{3,2},{4,5},{5,4},{6,7},{7,6},{8,9},{9,8},{10,11... | collective-permute-start | bytes 6291464 | tf_op jit(solution)/shard_map/ppermute | solution.py:297
  74.5 5.8 %collective-permute-start.9 = (bf16[512,256]{1,0:T(8,128)(2,1)S(1)}, bf16[512,256]{1,0:T(8,128)(2,1)S(1)}, u32[]{:S(2)}, u32[]{:S(2)}) collective-permute-start(bf16[512,256]{1,0:T(8,128)(2,1)S(1)} %get-tuple-element.32), channel_id=1, source_target_pairs={{0,0},{1,8},{2,16},{3,24},{4,32},{5,40},{6,48},{7,56},{8,64},{9,72... | collective-permute-start | bytes 786440 | tf_op jit(solution)/shard_map/ppermute | solution.py:325
  80.3 45.1 %copy-start.2 = (bf16[512,512]{1,0:T(8,128)(2,1)S(1)}, bf16[512,512]{1,0:T(8,128)(2,1)}, u32[]{:S(2)}) copy-start(bf16[512,512]{1,0:T(8,128)(2,1)} %w_ref.1) | copy-start | bytes 1572868
  80.3 45.1 %copy-start.3 = (f32[512]{0:T(512)S(1)}, f32[512]{0:T(512)}, u32[]{:S(2)}) copy-start(f32[512]{0:T(512)} %param.9) | copy-start | bytes 6148
  (1 other events, 0.6 us)

commit v4 on v3

v4 whole, which is shorter than its diff:
```python
import jax
import jax.numpy as jnp
from jax import lax
from jax.experimental import pallas as pl
from jax.experimental.pallas import tpu as pltpu
from jax.sharding import PartitionSpec as P

BLOCK = 128
WIDTH = 512
NBLK = 32
NREL = 4
SLOTS = 128
PIECE = 64
NODES = NBLK * BLOCK
HALF = NODES // 2
CHUNK = 512
UNROLL = 8
PAIRS = 72
MIB = 1024 * 1024
NT = (((1,), (1,)), ((), ()))
TN = (((0,), (0,)), ((), ()))
VMEM_SPEC = pl.BlockSpec(memory_space=pltpu.VMEM)
SMEM_SPEC = pl.BlockSpec(memory_space=pltpu.SMEM)


def params(mib):
    return pltpu.CompilerParams(vmem_limit_bytes=mib * MIB)


ANY_SPEC = pl.BlockSpec(memory_space=pl.ANY)
CHUNKS = 8
PER = SLOTS // CHUNKS


def counts_copies(hbm, vmem, sems):
    def copy(i):
        at = pl.ds(i * PER, PER)
        return pltpu.make_async_copy(hbm.at[at], vmem.at[at], sems.at[i])

    return copy


def prep_kernel(codes_ref, counts_hbm, weight_hbm, deg_ref, cnt_hbm, wt_hbm, counts, cnt, weight, wt, sems):
    counts_copy = counts_copies(counts_hbm, counts, sems)
    weight_copy = pltpu.make_async_copy(weight_hbm, weight, sems.at[CHUNKS])
    wt_copy = pltpu.make_async_copy(wt, wt_hbm, sems.at[CHUNKS + 1])
    weight_copy.start()
    for i in range(CHUNKS):
        counts_copy(i).start()
    deg_ref[...] = jnp.zeros_like(deg_ref)
    weight_copy.wait()

    def turn(r, carry):
        wt[r] = weight[r].T
        return carry

    lax.fori_loop(0, NREL, turn, 0)
    wt_copy.start()
    ones = jnp.ones((8, BLOCK), jnp.bfloat16)

    def cnt_copy(i):
        at = pl.ds(i * PER, PER)
        return pltpu.make_async_copy(cnt.at[at], cnt_hbm.at[at], sems.at[CHUNKS + 2 + i])

    def some(i, carry):
        counts_copy(i).wait()
        for s in range(PER):
            slot = i * PER + s
            c = counts[slot].astype(jnp.float32).astype(jnp.bfloat16)
            cnt[slot] = c
            row = lax.dot_general(ones, c, NT, preferred_element_type=jnp.float32)
            seg = lax.shift_right_logical(codes_ref[slot], 5)
            deg_ref[pl.ds(seg, 1), :] += row[0:1]
        cnt_copy(i).start()
        return carry

    lax.fori_loop(0, CHUNKS, some, 0)
    wt_copy.wait()
    for i in range(CHUNKS):
        cnt_copy(i).wait()


def prep(codes, counts, rel_weight):
    return pl.pallas_call(
        prep_kernel,
        in_specs=[SMEM_SPEC, ANY_SPEC, ANY_SPEC],
        out_specs=[VMEM_SPEC, ANY_SPEC, ANY_SPEC],
        out_shape=[
            jax.ShapeDtypeStruct((NREL * NBLK, BLOCK), jnp.float32),
            jax.ShapeDtypeStruct((SLOTS, BLOCK, BLOCK), jnp.bfloat16),
            jax.ShapeDtypeStruct((NREL, WIDTH, WIDTH), jnp.bfloat16),
        ],
        scratch_shapes=[
            pltpu.VMEM((SLOTS, BLOCK, BLOCK), jnp.int32),
            pltpu.VMEM((SLOTS, BLOCK, BLOCK), jnp.bfloat16),
            pltpu.VMEM((NREL, WIDTH, WIDTH), jnp.bfloat16),
            pltpu.VMEM((NREL, WIDTH, WIDTH), jnp.bfloat16),
            pltpu.SemaphoreType.DMA((2 * CHUNKS + 2,)),
        ],
        compiler_params=params(58),
        cost_estimate=pl.CostEstimate(flops=2 * SLOTS * BLOCK * BLOCK * 8, bytes_accessed=16 * MIB, transcendentals=0),
        name="prep",
    )(codes, counts, rel_weight)


HALF_BLOCKS = NBLK // 2
HID = (NREL, NBLK, WIDTH, BLOCK)


def hidden_half(first, x_ref, wt_ref, hid_ref, before, after):
    per = CHUNK // BLOCK

    def one(r, carry):
        before(r)
        for n in range(HALF // CHUNK):
            x = x_ref[:, n * CHUNK : (n + 1) * CHUNK]
            h = jnp.dot(wt_ref[r], x, preferred_element_type=jnp.float32).astype(jnp.bfloat16)
            for b in range(per):
                hid_ref[r, first + n * per + b] = h[:, b * BLOCK : (b + 1) * BLOCK]
        after(r)
        return carry

    lax.fori_loop(0, NREL, one, 0)


def own_hidden_kernel(x_ref, wt_hbm, hid_hbm, hid, wt, sems):
    def wt_copy(r):
        return pltpu.make_async_copy(wt_hbm.at[r], wt.at[r], sems.at[r])

    def hid_copy(r):
        return pltpu.make_async_copy(hid.at[r], hid_hbm.at[r], sems.at[NREL + r])

    for r in range(NREL):
        wt_copy(r).start()
    hidden_half(0, x_ref, wt, hid, lambda r: wt_copy(r).wait(), lambda r: hid_copy(r).start())
    for r in range(NREL):
        hid_copy(r).wait()


def own_hidden(x, wt):
    shape = (NREL, HALF_BLOCKS, WIDTH, BLOCK)
    return pl.pallas_call(
        own_hidden_kernel,
        in_specs=[VMEM_SPEC, ANY_SPEC],
        out_specs=ANY_SPEC,
        out_shape=jax.ShapeDtypeStruct(shape, jnp.bfloat16),
        scratch_shapes=[
            pltpu.VMEM(shape, jnp.bfloat16),
            pltpu.VMEM((NREL, WIDTH, WIDTH), jnp.bfloat16),
            pltpu.SemaphoreType.DMA((2 * NREL,)),
        ],
        compiler_params=params(56),
        cost_estimate=pl.CostEstimate(flops=2 * HALF * WIDTH * WIDTH * NREL, bytes_accessed=12 * MIB, transcendentals=0),
        name="own_hidden",
    )(x, wt)


def slot_pairs(codes_ref, pairs_ref, which, hid_ref, w_ref, acc_ref):
    def some(q, carry):
        for u in range(UNROLL):
            k = q * UNROLL + u
            s1, s2, place = pairs_ref[which, 0, k], pairs_ref[which, 1, k], pairs_ref[which, 2, k]
            hs = []
            for s in (s1, s2):
                code = codes_ref[s]
                hs.append(hid_ref[lax.shift_right_logical(code, 10), jnp.bitwise_and(code, NBLK - 1)])
            h = jnp.concatenate(hs, axis=1)
            w = jnp.concatenate([w_ref[s1], w_ref[s2]], axis=1)
            acc_ref[place] += lax.dot_general(h, w, NT, preferred_element_type=jnp.float32)
        return carry

    lax.fori_loop(0, pairs_ref[which, 3, 0], some, 0)


def rest_kernel(place_ref, codes_ref, pairs_ref, *refs):
    deg_refs, refs = refs[:8], refs[8:]
    x_ref, wt_hbm, cnt_hbm, hid_hbm, sib_hbm, own_ref, hid, wt, w, acc, sib, inv_ref, sems = refs
    core = place_ref[0]
    other_first = (1 - core) * HALF_BLOCKS

    def wt_copy(r):
        return pltpu.make_async_copy(wt_hbm.at[r], wt.at[r], sems.at[r])

    def hid_copy(r):
        return pltpu.make_async_copy(hid_hbm.at[r], hid.at[r, pl.ds(core * HALF_BLOCKS, HALF_BLOCKS)], sems.at[NREL + r])

    def cnt_copy(r):
        at = pl.ds(r * (SLOTS // NREL), SLOTS // NREL)
        return pltpu.make_async_copy(cnt_hbm.at[at], w.at[at], sems.at[2 * NREL + r])

    sib_copy = pltpu.make_async_copy(sib, sib_hbm, sems.at[3 * NREL])
    for r in range(NREL):
        wt_copy(r).start()
        cnt_copy(r).start()
    for r in range(NREL):
        hid_copy(r).start()
    degree = deg_refs[0][...]
    for ref in deg_refs[1:]:
        degree = degree + ref[...]
    inv_ref[...] = (1.0 / jnp.maximum(degree, 1.0)).T
    w[SLOTS] = jnp.zeros((BLOCK, BLOCK), jnp.bfloat16)

    def before(r):
        wt_copy(r).wait()
        cnt_copy(r).wait()
        for u in range(SLOTS // NREL):
            slot = r * (SLOTS // NREL) + u
            seg = lax.shift_right_logical(codes_ref[slot], 5)
            factor = jnp.take_along_axis(inv_ref[...], jnp.full((BLOCK, BLOCK), seg, jnp.int32), axis=1)
            w[slot] = (w[slot].astype(jnp.float32) * factor).astype(jnp.bfloat16)
        zeros = jnp.zeros((HALF_BLOCKS // NREL, WIDTH, BLOCK), jnp.float32)
        acc[pl.ds(r * (HALF_BLOCKS // NREL), HALF_BLOCKS // NREL)] = zeros
        own_ref[pl.ds(r * (HALF_BLOCKS // NREL), HALF_BLOCKS // NREL)] = zeros

    hidden_half(other_first, x_ref, wt, hid, before, lambda r: None)
    for r in range(NREL):
        hid_copy(r).wait()
    slot_pairs(codes_ref, pairs_ref, 0, hid, w, acc)

    def one(t, carry):
        sib[t] = acc[t].astype(jnp.bfloat16)
        return carry

    lax.fori_loop(0, HALF_BLOCKS, one, 0)
    sib_copy.start()
    slot_pairs(codes_ref, pairs_ref, 1, hid, w, own_ref)
    sib_copy.wait()


def rest(place, codes, pairs, degrees, x, wt, cnt, hid):
    return pl.pallas_call(
        rest_kernel,
        in_specs=[SMEM_SPEC] * 3 + [VMEM_SPEC] * 9 + [ANY_SPEC] * 3,
        out_specs=[ANY_SPEC, VMEM_SPEC],
        out_shape=[
            jax.ShapeDtypeStruct((HALF_BLOCKS, WIDTH, BLOCK), jnp.bfloat16),
            jax.ShapeDtypeStruct((HALF_BLOCKS, WIDTH, BLOCK), jnp.float32),
        ],
        scratch_shapes=[
            pltpu.VMEM(HID, jnp.bfloat16),
            pltpu.VMEM((NREL, WIDTH, WIDTH), jnp.bfloat16),
            pltpu.VMEM((SLOTS + 1, BLOCK, BLOCK), jnp.bfloat16),
            pltpu.VMEM((HALF_BLOCKS, WIDTH, BLOCK), jnp.float32),
            pltpu.VMEM((HALF_BLOCKS, WIDTH, BLOCK), jnp.bfloat16),
            pltpu.VMEM((BLOCK, BLOCK), jnp.float32),
            pltpu.SemaphoreType.DMA((3 * NREL + 1,)),
        ],
        compiler_params=params(REST_MIB),
        cost_estimate=pl.CostEstimate(flops=2 * HALF * WIDTH * WIDTH * NREL * 3, bytes_accessed=20 * MIB, transcendentals=0),
        name="rest",
    )(place, codes, pairs, *degrees, x, wt, cnt, hid)


REST_MIB = 50


def join_kernel(own_ref, other_ref, out_ref):
    per = out_ref.shape[0]
    step = pl.program_id(0)
    for t in range(per):
        out_ref[t] = (own_ref[step * per + t] + other_ref[t].astype(jnp.float32)).astype(jnp.bfloat16)


def join(own, other):
    spec = pl.BlockSpec((4, WIDTH, BLOCK), lambda i: (i, 0, 0))
    return pl.pallas_call(
        join_kernel,
        grid=(NBLK // 2 // 4,),
        in_specs=[VMEM_SPEC, spec],
        out_specs=spec,
        out_shape=jax.ShapeDtypeStruct((NBLK // 2, WIDTH, BLOCK), jnp.bfloat16),
        compiler_params=params(12),
        cost_estimate=pl.CostEstimate(flops=MIB, bytes_accessed=8 * MIB, transcendentals=0),
        name="join",
    )(own, other)


def finish_kernel(parts_ref, x_ref, w_ref, bias_ref, out_ref):
    self_part = lax.dot_general(x_ref[...], w_ref[...], TN, preferred_element_type=jnp.float32)
    for b in range(2):
        total = parts_ref[0, b].astype(jnp.float32)
        for k in range(1, parts_ref.shape[0]):
            total = total + parts_ref[k, b].astype(jnp.float32)
        rows = slice(b * BLOCK, (b + 1) * BLOCK)
        out_ref[rows, :] = jnp.maximum(total.T + self_part[rows] + bias_ref[...], 0.0).astype(jnp.bfloat16)


def finish(parts, x_own, self_weight, bias):
    return pl.pallas_call(
        finish_kernel,
        out_shape=jax.ShapeDtypeStruct((2 * BLOCK, WIDTH), jnp.bfloat16),
        compiler_params=params(32),
        name="finish",
    )(parts, x_own, self_weight, bias.reshape(1, WIDTH))


def pair_lists(codes, core):
    slots = jnp.arange(SLOTS, dtype=jnp.int32)
    target = codes // NBLK % NBLK
    half = (target // 2 % 2 == core).astype(jnp.int32)
    place = target // 4 * 2 + target % 2
    group = half * (NBLK // 2) + place
    same = group[None, :] == group[:, None]
    nth = jnp.sum((same & (slots[None, :] < slots[:, None])).astype(jnp.int32), axis=1)
    groups = jnp.arange(NBLK, dtype=jnp.int32)
    size = jnp.sum((group[None, :] == groups[:, None]).astype(jnp.int32), axis=1)
    need = (size + 1) // 2
    before = (groups[None, :] < groups[:, None]) & (groups[None, :] // (NBLK // 2) == groups[:, None] // (NBLK // 2))
    base = jnp.sum(jnp.where(before, need[None, :], 0), axis=1)
    at = half * PAIRS + nth // 2 + jnp.sum(jnp.where(group[:, None] == groups[None, :], base[None, :], 0), axis=1)
    entries = jnp.arange(2 * PAIRS, dtype=jnp.int32)
    match = at[None, :] == entries[:, None]
    is_first = match & (nth % 2 == 0)[None, :]
    is_second = match & (nth % 2 == 1)[None, :]
    first = SLOTS + jnp.sum(jnp.where(is_first, slots[None, :] - SLOTS, 0), axis=1)
    second = SLOTS + jnp.sum(jnp.where(is_second, slots[None, :] - SLOTS, 0), axis=1)
    where = jnp.sum(jnp.where(is_first, place[None, :], 0), axis=1)
    steps = (jnp.sum(need.reshape(2, NBLK // 2), axis=1) + UNROLL - 1) // UNROLL
    steps = jnp.broadcast_to(steps[:, None], (2, PAIRS))
    return jnp.stack([first.reshape(2, PAIRS), second.reshape(2, PAIRS), where.reshape(2, PAIRS), steps], axis=1)


def swap(array):
    return lax.ppermute(array, "rel", [(0, 1), (1, 0)])


def on_device(features, rel_weight, self_weight, bias, block_code, block_counts):
    row, col, core = lax.axis_index("rows"), lax.axis_index("cols"), lax.axis_index("rel")
    codes = block_code[0, 0, 0]
    counts = block_counts[0, 0, 0]
    place = jnp.stack([core, row]).astype(jnp.int32)
    padded = jnp.concatenate([codes, jnp.zeros((8,), jnp.int32)])

    x_half = lax.dynamic_slice(features.T, (0, core * HALF), (PIECE, HALF))
    x_sent = jnp.broadcast_to(x_half[None], (8, PIECE, HALF))
    pairs = pair_lists(codes, core)
    x_sent, padded, pairs, place = lax.optimization_barrier((x_sent, padded, pairs, place))
    x_mine = lax.all_to_all(x_sent, "rows", 0, 0).reshape(WIDTH, HALF)

    deg_part, cnt, wt = prep(padded, counts, rel_weight)
    degrees = [deg_part] + [lax.ppermute(deg_part, "cols", [(i, (i + k) % 8) for i in range(8)]) for k in range(1, 8)]
    x_mine, cnt, wt, degrees = lax.optimization_barrier((x_mine, cnt, wt, degrees))

    x_other = swap(x_mine)
    at = ((col + row) % 4 * 2 + row // 4) * (2 * BLOCK)
    x_rows = lax.dynamic_slice(x_mine, (0, at), (WIDTH, 2 * BLOCK))
    moves = [
        ((a * 8 + b) * 2 + g, (b * 8 + 4 * g + (b + a) % 4) * 2 + a // 4)
        for a in range(8)
        for b in range(8)
        for g in range(2)
    ]
    x_mine, x_rows = lax.optimization_barrier((x_mine, x_rows))
    x_own = lax.ppermute(x_rows, ("rows", "cols", "rel"), moves)
    hid = own_hidden(x_mine, wt)
    x_other, x_own, hid = lax.optimization_barrier((x_other, x_own, hid))
    to_sib, own = rest(place, padded, pairs, degrees, x_other, wt, cnt, hid)
    other = swap(to_sib)
    both = join(own, other)
    parts = lax.all_to_all(both.reshape(8, 2, WIDTH, BLOCK), "cols", 0, 0)
    return finish(parts, x_own, self_weight, bias)


def solution(mesh):
    in_specs = (
        P("cols", "rows"),
        P("rel", None, None),
        P(),
        P(),
        P("rows", "cols", "rel", None),
        P("rows", "cols", "rel", None, None, None),
    )
    out_specs = P(("rows", "cols", "rel"), None)
    return jax.shard_map(on_device, mesh=mesh, in_specs=in_specs, out_specs=out_specs, check_vma=False)
```

time: 129 us -> 120 us (0.930); the launches traced: 127 us -> 119 us
  blocking collectives: 45.1 us -> 36.8 us
  starting transfers between devices: 20 us -> 25.4 us
  Pallas kernels: 39.7 us -> 37.5 us
  waiting for transfers between devices: 13.9 us -> 11.7 us
    all_to_all x1, blocking collectives: 45.1 us -> 36.8 us  [on_device(): parts = lax.all_to_all(both.reshape(8, 2, WIDTH, BLOCK), 'cols', 0, 0)]
    all_to_all x1, waiting for transfers between devices: 5.59 us -> 0.96 us  [on_device(): x_mine = lax.all_to_all(x_sent, 'rows', 0, 0).reshape(WIDTH, HALF)]
    ppermute x7, starting transfers between devices: 10.8 us -> 15 us  [on_device(): lax.ppermute(deg_part, 'cols', [(i, (i + k) % 8) for i in range(8)])]
    ppermute x2, waiting for transfers between devices: 0.01 us -> 3.79 us  [swap(): return lax.ppermute(array, 'rel', [(0, 1), (1, 0)])]
    pallas_call x5 -> x3, Pallas kernels: 38.2 us -> 36 us  [the longest x1 18.7 us: rest(): pl.pallas_call(rest_kernel, in_specs=[SMEM_SPEC] * 3 + [VMEM_SPEC] * 9 +...]
    unnamed x28 -> x14, local copies, waits for them, and re-layouts: 4.44 us -> 2.67 us
    ppermute x7, waiting for transfers between devices: 8.35 us -> 7 us  [on_device(): lax.ppermute(deg_part, 'cols', [(i, (i + k) % 8) for i in range(8)])]
  transfers between devices with their start and end apart: 11 -> 11, of which waited for: 3 -> 3; matrix products, arithmetic and copies ran while one was open for 2% -> 0% of each run, Pallas kernels for 16% -> 14%
where the time goes in v4:
time: 120 us; the launch traced here: 119 us
  Pallas kernels  37.5 us (31%)
  blocking collectives  36.8 us (31%)
  starting transfers between devices  25.4 us (21%)
  waiting for transfers between devices  11.7 us (10%)
  local copies, waits for them, and re-layouts  5.9 us (5%)
  other arithmetic  1.77 us (1%)
    all_to_all x1, blocking collectives, on_device(): parts = lax.all_to_all(both.reshape(8, 2, WIDTH, BLOCK), 'cols', 0, 0)  36.8 us
    pallas_call x1, Pallas kernels, rest(): pl.pallas_call(rest_kernel, in_specs=[SMEM_SPEC] * 3 + [VMEM_SPEC] * 9 +...  18.7 us
    ppermute x7, starting transfers between devices, on_device(): lax.ppermute(deg_part, 'cols', [(i, (i + k) % 8) for i in range(8)])  15 us
    pallas_call x1, Pallas kernels, own_hidden(): pl.pallas_call(own_hidden_kernel, in_specs=[VMEM_SPEC, ANY_SPEC], out_spe...  9.07 us
    pallas_call x1, Pallas kernels, prep(): pl.pallas_call(prep_kernel, in_specs=[SMEM_SPEC, ANY_SPEC, ANY_SPEC], out...  8.23 us
    all_to_all x1, starting transfers between devices, on_device(): x_mine = lax.all_to_all(x_sent, 'rows', 0, 0).reshape(WIDTH, HALF)  7.87 us
    ppermute x7, waiting for transfers between devices, on_device(): lax.ppermute(deg_part, 'cols', [(i, (i + k) % 8) for i in range(8)])  7 us
    ppermute x2, waiting for transfers between devices, swap(): return lax.ppermute(array, 'rel', [(0, 1), (1, 0)])  3.79 us
  transfers between devices with their start and end apart: 11, of which 3 were waited for; matrix products, arithmetic and copies ran while one was open for 0% of the time, Pallas kernels for 14%

profile of v4, /device:TPU:0, one launch (start us, length us, event | category | flops | bytes accessed | tf_op | source)
XLA Modules:
  0.0 119.4 jit_solution(11600399244185406918)
XLA Ops:
  0.0 0.7 fusion.8
  1.0 1.2 concatenate.3.codes_ref
  3.4 1.6 %broadcast_in_dim.76 = bf16[8,64,2048]{2,1,0:T(8,128)(2,1)} broadcast(bf16[64,2048]{1,0:T(8,128)(2,1)S(1)} %dynamic-slice_bitcast_fusion), dimensions={1,2} | broadcast | bytes 2359296 | tf_op jit(solution)/shard_map/broadcast_in_dim | solution.py:335
  5.0 7.9 %all-to-all-start = ((bf16[8,64,2048]{2,1,0:T(8,128)(2,1)}), bf16[8,64,2048]{2,1,0:T(8,128)(2,1)S(1)}, u32[]{:S(2)}, u32[]{:S(2)}) async-start(bf16[8,64,2048]{2,1,0:T(8,128)(2,1)} %broadcast_in_dim.76), calls=%async_computation | async-start | bytes 4194304 | tf_op jit(solution)/shard_map/all_to_all | solution.py:338
  12.9 8.2 %prep.1 = (f32[128,128]{1,0:T(8,128)}, bf16[128,128,128]{2,1,0:T(8,128)(2,1)}, bf16[4,512,512]{2,1,0:T(8,128)(2,1)}) custom-call(s32[136]{0:T(256)} %concatenate.3.codes_ref, s32[128,128,128]{2,1,0:T(8,128)} %bitcast.12, bf16[4,512,512]{2,1,0:T(8,128)(2,1)} %weight_hbm.1), custom_call_target="tpu_custom_call" | custom-call | flops 33554432 | bytes 16777216 | tf_op jit(solution)/shard_map/prep/pallas_call | solution.py:84
  21.1 3.3 %collective-permute-start.6 = (f32[128,128]{1,0:T(8,128)}, f32[128,128]{1,0:T(8,128)S(1)}, u32[]{:S(2)}, u32[]{:S(2)}) collective-permute-start(f32[128,128]{1,0:T(8,128)} %get-tuple-element.37.refs_0_), channel_id=1, source_target_pairs={{0,14},{2,0},{4,2},{6,4},{8,6},{10,8},{12,10},{14,12},{1,15},{3,1}... | collective-permute-start | bytes 196616 | tf_op jit(solution)/shard_map/ppermute | solution.py:341
  24.4 0.8 collective-permute-start.5
  25.2 1.3 %collective-permute-start.4 = (f32[128,128]{1,0:T(8,128)}, f32[128,128]{1,0:T(8,128)S(1)}, u32[]{:S(2)}, u32[]{:S(2)}) collective-permute-start(f32[128,128]{1,0:T(8,128)} %get-tuple-element.37.refs_0_), channel_id=1, source_target_pairs={{0,10},{2,12},{4,14},{6,0},{8,2},{10,4},{12,6},{14,8},{1,11},{3,13... | collective-permute-start | bytes 196616 | tf_op jit(solution)/shard_map/ppermute | solution.py:341
  26.5 1.0 collective-permute-start.3
  27.6 1.9 %collective-permute-start.2 = (f32[128,128]{1,0:T(8,128)}, f32[128,128]{1,0:T(8,128)S(1)}, u32[]{:S(2)}, u32[]{:S(2)}) collective-permute-start(f32[128,128]{1,0:T(8,128)} %get-tuple-element.37.refs_0_), channel_id=1, source_target_pairs={{0,6},{2,8},{4,10},{6,12},{8,14},{10,0},{12,2},{14,4},{1,7},{3,9},... | collective-permute-start | bytes 196616 | tf_op jit(solution)/shard_map/ppermute | solution.py:341
  29.5 2.4 %collective-permute-start.1 = (f32[128,128]{1,0:T(8,128)}, f32[128,128]{1,0:T(8,128)S(1)}, u32[]{:S(2)}, u32[]{:S(2)}) collective-permute-start(f32[128,128]{1,0:T(8,128)} %get-tuple-element.37.refs_0_), channel_id=1, source_target_pairs={{0,4},{2,6},{4,8},{6,10},{8,12},{10,14},{12,0},{14,2},{1,5},{3,7},... | collective-permute-start | bytes 196616 | tf_op jit(solution)/shard_map/ppermute | solution.py:341
  31.9 4.3 %collective-permute-start = (f32[128,128]{1,0:T(8,128)}, f32[128,128]{1,0:T(8,128)S(1)}, u32[]{:S(2)}, u32[]{:S(2)}) collective-permute-start(f32[128,128]{1,0:T(8,128)} %get-tuple-element.37.refs_0_), channel_id=1, source_target_pairs={{0,2},{2,4},{4,6},{6,8},{8,10},{10,12},{12,14},{14,0},{1,3},{3,5},... | collective-permute-start | bytes 196616 | tf_op jit(solution)/shard_map/ppermute | solution.py:341
  36.2 7.0 %collective-permute-done.3.refs_4_ = f32[128,128]{1,0:T(8,128)S(1)} collective-permute-done((f32[128,128]{1,0:T(8,128)}, f32[128,128]{1,0:T(8,128)S(1)}, u32[]{:S(2)}, u32[]{:S(2)}) %collective-permute-start.3) | collective-permute-done | bytes 65568 | tf_op jit(solution)/shard_map/ppermute | solution.py:341
  43.2 1.0 all-to-all-done
  44.2 0.8 collective-permute-start.8
  45.0 0.5 copy-done.6
  45.5 9.1 %own_hidden.1.refs_11_ = bf16[4,16,512,128]{3,2,1,0:T(8,128)(2,1)} custom-call(bf16[512,2048]{1,0:T(8,128)(2,1)} %bitcast.15, bf16[4,512,512]{2,1,0:T(8,128)(2,1)} %get-tuple-element.48.wt_hbm.refs_9_), custom_call_target="tpu_custom_call" | custom-call | flops 4294967296 | bytes 12582912 | tf_op jit(solution)/shard_map/own_hidden/pallas_call | solution.py:142
  54.6 18.7 %rest.1 = (bf16[16,512,128]{2,1,0:T(8,128)(2,1)S(1)}, f32[16,512,128]{2,1,0:T(8,128)}) custom-call(s32[2]{0:T(128)S(1)} %pad_add_fusion.1.place_ref, s32[136]{0:T(256)S(1)} %copy-done.3, s32[2,4,72]{2,1,0:T(4,128)S(1)} %pad_add_fusion.pairs_ref, f32[128,128]{1,0:T(8,128)S(1)} %copy-done.5, f32[128,128]{1,0:T(8,128)S(1)} %collective-permute-done.refs_1_, ...), custom_call_target="tpu_custom_call" | custom-call | flops 12884901888 | bytes 20971520 | tf_op jit(solution)/shard_map/rest/pallas_call | solution.py:231
  73.2 1.7 %collective-permute-start.9 = (bf16[16,512,128]{2,1,0:T(8,128)(2,1)S(1)}, bf16[16,512,128]{2,1,0:T(8,128)(2,1)S(1)}, u32[]{:S(2)}, u32[]{:S(2)}) collective-permute-start(bf16[16,512,128]{2,1,0:T(8,128)(2,1)S(1)} %get-tuple-element.53), channel_id=1, source_target_pairs={{0,1},{1,0},{2,3},{3,2},{4,5},{5,4},{6,7},{7,6},{8,9},{9,8},{10,11... | collective-permute-start | bytes 6291464 | tf_op jit(solution)/shard_map/ppermute | solution.py:324
  75.0 3.8 %collective-permute-done.9.other_ref = bf16[16,512,128]{2,1,0:T(8,128)(2,1)S(1)} collective-permute-done((bf16[16,512,128]{2,1,0:T(8,128)(2,1)S(1)}, bf16[16,512,128]{2,1,0:T(8,128)(2,1)S(1)}, u32[]{:S(2)}, u32[]{:S(2)}) %collective-permute-start.9) | collective-permute-done | bytes 2097184 | tf_op jit(solution)/shard_map/ppermute | solution.py:324
  78.8 2.2 %copy-done.1 = f32[16,512,128]{2,1,0:T(8,128)S(1)} copy-done((f32[16,512,128]{2,1,0:T(8,128)S(1)}, f32[16,512,128]{2,1,0:T(8,128)}, u32[]{:S(2)}) %copy-start.1) | copy-done | bytes 4194328
  80.9 0.4 join.1
  81.4 36.8 %all_to_all.10.parts_ref = bf16[8,2,512,128]{3,2,1,0:T(8,128)(2,1)S(1)} all-to-all(bf16[8,2,512,128]{3,2,1,0:T(8,128)(2,1)S(1)} %bitcast.10), channel_id=1, replica_groups=mesh['rows'=8,'cols'=8,'rel'=2] {'cols'}, dimensions={0} | all-to-all | bytes 4194304 | tf_op jit(solution)/shard_map/all_to_all | solution.py:360
  118.2 1.1 finish.1
  (44 shorter events, 1.5 us)
Async XLA Ops:
  0.0 3.3 %copy-start = (bf16[4096,64]{0,1:T(8,128)(2,1)S(1)}, bf16[4096,64]{0,1:T(8,128)(2,1)}, u32[]{:S(2)}) copy-start(bf16[4096,64]{0,1:T(8,128)(2,1)} %param.6) | copy-start | bytes 1572868
  5.0 39.1 %all-to-all-start = ((bf16[8,64,2048]{2,1,0:T(8,128)(2,1)}), bf16[8,64,2048]{2,1,0:T(8,128)(2,1)S(1)}, u32[]{:S(2)}, u32[]{:S(2)}) async-start(bf16[8,64,2048]{2,1,0:T(8,128)(2,1)} %broadcast_in_dim.76), calls=%async_computation | async-start | bytes 4194304 | tf_op jit(solution)/shard_map/all_to_all | solution.py:338
  21.1 8.3 %collective-permute-start.6 = (f32[128,128]{1,0:T(8,128)}, f32[128,128]{1,0:T(8,128)S(1)}, u32[]{:S(2)}, u32[]{:S(2)}) collective-permute-start(f32[128,128]{1,0:T(8,128)} %get-tuple-element.37.refs_0_), channel_id=1, source_target_pairs={{0,14},{2,0},{4,2},{6,4},{8,6},{10,8},{12,10},{14,12},{1,15},{3,1}... | collective-permute-start | bytes 196616 | tf_op jit(solution)/shard_map/ppermute | solution.py:341
  24.4 7.5 %collective-permute-start.5 = (f32[128,128]{1,0:T(8,128)}, f32[128,128]{1,0:T(8,128)S(1)}, u32[]{:S(2)}, u32[]{:S(2)}) collective-permute-start(f32[128,128]{1,0:T(8,128)} %get-tuple-element.37.refs_0_), channel_id=1, source_target_pairs={{0,12},{2,14},{4,0},{6,2},{8,4},{10,6},{12,8},{14,10},{1,13},{3,15... | collective-permute-start | bytes 196616 | tf_op jit(solution)/shard_map/ppermute | solution.py:341
  25.2 11.0 %collective-permute-start.4 = (f32[128,128]{1,0:T(8,128)}, f32[128,128]{1,0:T(8,128)S(1)}, u32[]{:S(2)}, u32[]{:S(2)}) collective-permute-start(f32[128,128]{1,0:T(8,128)} %get-tuple-element.37.refs_0_), channel_id=1, source_target_pairs={{0,10},{2,12},{4,14},{6,0},{8,2},{10,4},{12,6},{14,8},{1,11},{3,13... | collective-permute-start | bytes 196616 | tf_op jit(solution)/shard_map/ppermute | solution.py:341
  26.5 16.6 %collective-permute-start.3 = (f32[128,128]{1,0:T(8,128)}, f32[128,128]{1,0:T(8,128)S(1)}, u32[]{:S(2)}, u32[]{:S(2)}) collective-permute-start(f32[128,128]{1,0:T(8,128)} %get-tuple-element.37.refs_0_), channel_id=1, source_target_pairs={{0,8},{2,10},{4,12},{6,14},{8,0},{10,2},{12,4},{14,6},{1,9},{3,11}... | collective-permute-start | bytes 196616 | tf_op jit(solution)/shard_map/ppermute | solution.py:341
  27.6 15.6 %collective-permute-start.2 = (f32[128,128]{1,0:T(8,128)}, f32[128,128]{1,0:T(8,128)S(1)}, u32[]{:S(2)}, u32[]{:S(2)}) collective-permute-start(f32[128,128]{1,0:T(8,128)} %get-tuple-element.37.refs_0_), channel_id=1, source_target_pairs={{0,6},{2,8},{4,10},{6,12},{8,14},{10,0},{12,2},{14,4},{1,7},{3,9},... | collective-permute-start | bytes 196616 | tf_op jit(solution)/shard_map/ppermute | solution.py:341
  29.5 13.7 %collective-permute-start.1 = (f32[128,128]{1,0:T(8,128)}, f32[128,128]{1,0:T(8,128)S(1)}, u32[]{:S(2)}, u32[]{:S(2)}) collective-permute-start(f32[128,128]{1,0:T(8,128)} %get-tuple-element.37.refs_0_), channel_id=1, source_target_pairs={{0,4},{2,6},{4,8},{6,10},{8,12},{10,14},{12,0},{14,2},{1,5},{3,7},... | collective-permute-start | bytes 196616 | tf_op jit(solution)/shard_map/ppermute | solution.py:341
  31.9 11.3 %collective-permute-start = (f32[128,128]{1,0:T(8,128)}, f32[128,128]{1,0:T(8,128)S(1)}, u32[]{:S(2)}, u32[]{:S(2)}) collective-permute-start(f32[128,128]{1,0:T(8,128)} %get-tuple-element.37.refs_0_), channel_id=1, source_target_pairs={{0,2},{2,4},{4,6},{6,8},{8,10},{10,12},{12,14},{14,0},{1,3},{3,5},... | collective-permute-start | bytes 196616 | tf_op jit(solution)/shard_map/ppermute | solution.py:341
  44.1 1.3 %copy-start.6 = (bf16[8,64,2048]{2,1,0:T(8,128)(2,1)}, bf16[8,64,2048]{2,1,0:T(8,128)(2,1)S(1)}, u32[]{:S(2)}) copy-start(bf16[8,64,2048]{2,1,0:T(8,128)(2,1)S(1)} %all-to-all-done) | copy-start | bytes 6291460
  44.1 10.4 %collective-permute-start.7 = (bf16[512,2048]{1,0:T(8,128)(2,1)S(1)}, bf16[512,2048]{1,0:T(8,128)(2,1)}, u32[]{:S(2)}, u32[]{:S(2)}) collective-permute-start(bf16[512,2048]{1,0:T(8,128)(2,1)S(1)} %bitcast.13), channel_id=1, source_target_pairs={{0,1},{1,0},{2,3},{3,2},{4,5},{5,4},{6,7},{7,6},{8,9},{9,8},{10,11... | collective-permute-start | bytes 6291464 | tf_op jit(solution)/shard_map/ppermute | solution.py:324
  44.2 10.4 %copy-start.3 = (s32[136]{0:T(256)S(1)}, s32[136]{0:T(256)}, u32[]{:S(2)}) copy-start(s32[136]{0:T(256)} %concatenate.3.codes_ref) | copy-start | bytes 1636
  44.2 10.4 %copy-start.5 = (f32[128,128]{1,0:T(8,128)S(1)}, f32[128,128]{1,0:T(8,128)}, u32[]{:S(2)}) copy-start(f32[128,128]{1,0:T(8,128)} %get-tuple-element.37.refs_0_) | copy-start | bytes 196612
  44.2 10.4 %collective-permute-start.8 = (bf16[512,256]{1,0:T(8,128)(2,1)S(1)}, bf16[512,256]{1,0:T(8,128)(2,1)S(1)}, u32[]{:S(2)}, u32[]{:S(2)}) collective-permute-start(bf16[512,256]{1,0:T(8,128)(2,1)S(1)} %constant_dynamic-slice_fusion), channel_id=1, source_target_pairs={{0,0},{1,8},{2,18},{3,26},{4,36},{5,44},{6,54},{7,62},{8,64},{9,72... | collective-permute-start | bytes 786440 | tf_op jit(solution)/shard_map/ppermute | solution.py:354
  73.2 5.5 %collective-permute-start.9 = (bf16[16,512,128]{2,1,0:T(8,128)(2,1)S(1)}, bf16[16,512,128]{2,1,0:T(8,128)(2,1)S(1)}, u32[]{:S(2)}, u32[]{:S(2)}) collective-permute-start(bf16[16,512,128]{2,1,0:T(8,128)(2,1)S(1)} %get-tuple-element.53), channel_id=1, source_target_pairs={{0,1},{1,0},{2,3},{3,2},{4,5},{5,4},{6,7},{7,6},{8,9},{9,8},{10,11... | collective-permute-start | bytes 6291464 | tf_op jit(solution)/shard_map/ppermute | solution.py:324
  78.8 2.2 %copy-start.1 = (f32[16,512,128]{2,1,0:T(8,128)S(1)}, f32[16,512,128]{2,1,0:T(8,128)}, u32[]{:S(2)}) copy-start(f32[16,512,128]{2,1,0:T(8,128)} %get-tuple-element.52.own_ref) | copy-start | bytes 12582916
  81.4 36.9 %copy-start.2 = (bf16[512,512]{1,0:T(8,128)(2,1)S(1)}, bf16[512,512]{1,0:T(8,128)(2,1)}, u32[]{:S(2)}) copy-start(bf16[512,512]{1,0:T(8,128)(2,1)} %w_ref.1) | copy-start | bytes 1572868
  81.4 36.9 %copy-start.4 = (f32[512]{0:T(512)S(1)}, f32[512]{0:T(512)}, u32[]{:S(2)}) copy-start(f32[512]{0:T(512)} %param.9) | copy-start | bytes 6148

commit v5 on v4

v5 whole, which is shorter than its diff:
```python
import jax
import jax.numpy as jnp
from jax import lax
from jax.experimental import pallas as pl
from jax.experimental.pallas import tpu as pltpu
from jax.sharding import PartitionSpec as P

BLOCK = 128
WIDTH = 512
NBLK = 32
NREL = 4
SLOTS = 128
PIECE = 64
NODES = NBLK * BLOCK
HALF = NODES // 2
CHUNK = 512
UNROLL = 8
PAIRS = 72
MIB = 1024 * 1024
NT = (((1,), (1,)), ((), ()))
TN = (((0,), (0,)), ((), ()))
VMEM_SPEC = pl.BlockSpec(memory_space=pltpu.VMEM)
SMEM_SPEC = pl.BlockSpec(memory_space=pltpu.SMEM)


def params(mib):
    return pltpu.CompilerParams(vmem_limit_bytes=mib * MIB)


ANY_SPEC = pl.BlockSpec(memory_space=pl.ANY)
CHUNKS = 8
PER = SLOTS // CHUNKS


CORE, DIAGONAL = 0, 1


def counts_copies(hbm, vmem, sems):
    def copy(i):
        at = pl.ds(i * PER, PER)
        return pltpu.make_async_copy(hbm.at[at], vmem.at[at], sems.at[i])

    return copy


def prep_kernel(codes_ref, counts_hbm, weight_hbm, out_ref, wt_hbm, counts, weight, wt, deg_ref, sems):
    counts_copy = counts_copies(counts_hbm, counts, sems)
    weight_copy = pltpu.make_async_copy(weight_hbm, weight, sems.at[CHUNKS])
    wt_copy = pltpu.make_async_copy(wt, wt_hbm, sems.at[CHUNKS + 1])
    for i in range(CHUNKS):
        counts_copy(i).start()
    weight_copy.start()
    deg_ref[...] = jnp.zeros_like(deg_ref)
    ones = jnp.ones((8, BLOCK), jnp.bfloat16)

    def some(i, carry):
        counts_copy(i).wait()
        for s in range(PER):
            slot = i * PER + s
            c = counts[slot].astype(jnp.float32).astype(jnp.bfloat16)
            row = lax.dot_general(ones, c, NT, preferred_element_type=jnp.float32)
            seg = lax.shift_right_logical(codes_ref[slot], 5)
            deg_ref[pl.ds(seg, 1), :] += row[0:1]
        return carry

    lax.fori_loop(0, CHUNKS, some, 0)
    out_ref[...] = deg_ref[...].astype(jnp.bfloat16)
    weight_copy.wait()

    def turn(r, carry):
        wt[r] = weight[r].T
        return carry

    lax.fori_loop(0, NREL, turn, 0)
    wt_copy.start()
    wt_copy.wait()


def prep(codes, counts, rel_weight):
    return pl.pallas_call(
        prep_kernel,
        in_specs=[SMEM_SPEC, ANY_SPEC, ANY_SPEC],
        out_specs=[VMEM_SPEC, ANY_SPEC],
        out_shape=[
            jax.ShapeDtypeStruct((NREL * NBLK, BLOCK), jnp.bfloat16),
            jax.ShapeDtypeStruct((NREL, WIDTH, WIDTH), jnp.bfloat16),
        ],
        scratch_shapes=[
            pltpu.VMEM((SLOTS, BLOCK, BLOCK), jnp.int32),
            pltpu.VMEM((NREL, WIDTH, WIDTH), jnp.bfloat16),
            pltpu.VMEM((NREL, WIDTH, WIDTH), jnp.bfloat16),
            pltpu.VMEM((NREL * NBLK, BLOCK), jnp.float32),
            pltpu.SemaphoreType.DMA((CHUNKS + 2,)),
        ],
        compiler_params=params(52),
        cost_estimate=pl.CostEstimate(flops=2 * SLOTS * BLOCK * BLOCK * 8, bytes_accessed=12 * MIB, transcendentals=0),
        name="prep",
    )(codes, counts, rel_weight)


HALF_BLOCKS = NBLK // 2
HID = (NREL, NBLK, WIDTH, BLOCK)


def slot_pairs(codes_ref, pairs_ref, which, hid_ref, w_ref, acc_ref):
    def some(q, carry):
        for u in range(UNROLL):
            k = q * UNROLL + u
            s1, s2, place = pairs_ref[which, 0, k], pairs_ref[which, 1, k], pairs_ref[which, 2, k]
            hs = []
            for s in (s1, s2):
                code = codes_ref[s]
                hs.append(hid_ref[lax.shift_right_logical(code, 10), jnp.bitwise_and(code, NBLK - 1)])
            h = jnp.concatenate(hs, axis=1)
            w = jnp.concatenate([w_ref[s1], w_ref[s2]], axis=1)
            acc_ref[place] += lax.dot_general(h, w, NT, preferred_element_type=jnp.float32)
        return carry

    lax.fori_loop(0, pairs_ref[which, 3, 0], some, 0)


STEPS = NODES // CHUNK
PER_STEP = SLOTS // STEPS


def aggregate_kernel(place_ref, codes_ref, pairs_ref, *refs):
    deg_refs, refs = refs[:8], refs[8:]
    xm_hbm, xo_hbm, wt_hbm, counts_hbm, self_hbm, sib_hbm, own_ref, x, hid, wt, w, counts, acc, sib, inv_ref, self_w, sems = refs
    core = place_ref[CORE]
    near = STEPS // 2

    def x_copy(n, source):
        at = pl.ds(pl.multiple_of(lax.rem(n, near) * CHUNK, CHUNK), CHUNK)
        return pltpu.make_async_copy(source.at[:, at], x.at[n], sems.at[n])

    def counts_copy(n):
        at = pl.ds(n * PER_STEP, PER_STEP)
        return pltpu.make_async_copy(counts_hbm.at[at], counts.at[lax.rem(n, 4)], sems.at[STEPS + n])

    wt_copy = pltpu.make_async_copy(wt_hbm, wt, sems.at[2 * STEPS])
    sib_copy = pltpu.make_async_copy(sib, sib_hbm, sems.at[2 * STEPS + 1])
    self_copy = pltpu.make_async_copy(self_hbm, self_w, sems.at[2 * STEPS + 2])
    wt_copy.start()
    for n in range(STEPS):
        x_copy(n, xm_hbm if n < near else xo_hbm).start()
        if n < 4:
            counts_copy(n).start()

    @pl.when(place_ref[DIAGONAL] == 1)
    def _():
        self_copy.start()

    degree = deg_refs[0][...].astype(jnp.float32)
    for ref in deg_refs[1:]:
        degree = degree + ref[...].astype(jnp.float32)
    inv_ref[...] = (1.0 / jnp.maximum(degree, 1.0)).T
    w[SLOTS] = jnp.zeros((BLOCK, BLOCK), jnp.bfloat16)
    wt_copy.wait()

    def step(n, carry):
        x_copy(n, xm_hbm).wait()
        counts_copy(n).wait()
        for u in range(PER_STEP):
            slot = n * PER_STEP + u
            seg = lax.shift_right_logical(codes_ref[slot], 5)
            factor = jnp.take_along_axis(inv_ref[...], jnp.full((BLOCK, BLOCK), seg, jnp.int32), axis=1)
            w[slot] = (counts[lax.rem(n, 4), u].astype(jnp.float32) * factor).astype(jnp.bfloat16)
        zeros = jnp.zeros((HALF_BLOCKS // STEPS, WIDTH, BLOCK), jnp.float32)
        acc[pl.ds(n * (HALF_BLOCKS // STEPS), HALF_BLOCKS // STEPS)] = zeros
        own_ref[pl.ds(n * (HALF_BLOCKS // STEPS), HALF_BLOCKS // STEPS)] = zeros
        first = jnp.where(n < near, core, 1 - core) * HALF_BLOCKS + lax.rem(n, near) * (CHUNK // BLOCK)
        for r in range(NREL):
            h = jnp.dot(wt[r], x[n], preferred_element_type=jnp.float32).astype(jnp.bfloat16)
            for b in range(CHUNK // BLOCK):
                hid[r, first + b] = h[:, b * BLOCK : (b + 1) * BLOCK]

        @pl.when(n < STEPS - 4)
        def _():
            counts_copy(n + 4).start()

        return carry

    lax.fori_loop(0, STEPS, step, 0)

    @pl.when(place_ref[DIAGONAL] == 1)
    def _():
        self_copy.wait()
        turned = self_w[...].T
        for n in range(STEPS):
            cols = pl.ds(pl.multiple_of(core * (2 * BLOCK), 2 * BLOCK), 2 * BLOCK)
            term = jnp.dot(turned, x[n, :, cols], preferred_element_type=jnp.float32)
            half = core if n < near else 1 - core
            for b in range(2):
                own_ref[half * (HALF_BLOCKS // 2) + n % near * 2 + b] = term[:, b * BLOCK : (b + 1) * BLOCK]

    slot_pairs(codes_ref, pairs_ref, 0, hid, w, acc)

    def one(t, carry):
        sib[t] = acc[t].astype(jnp.bfloat16)
        return carry

    lax.fori_loop(0, HALF_BLOCKS, one, 0)
    sib_copy.start()
    slot_pairs(codes_ref, pairs_ref, 1, hid, w, own_ref)
    sib_copy.wait()


def aggregate(place, codes, pairs, degrees, x_mine, x_other, wt, counts, self_weight):
    return pl.pallas_call(
        aggregate_kernel,
        in_specs=[SMEM_SPEC] * 3 + [VMEM_SPEC] * 8 + [ANY_SPEC] * 5,
        out_specs=[ANY_SPEC, VMEM_SPEC],
        out_shape=[
            jax.ShapeDtypeStruct((HALF_BLOCKS, WIDTH, BLOCK), jnp.bfloat16),
            pltpu.VMEM((HALF_BLOCKS, WIDTH, BLOCK), jnp.float32),
        ],
        scratch_shapes=[
            pltpu.VMEM((STEPS, WIDTH, CHUNK), jnp.bfloat16),
            pltpu.VMEM(HID, jnp.bfloat16),
            pltpu.VMEM((NREL, WIDTH, WIDTH), jnp.bfloat16),
            pltpu.VMEM((SLOTS + 1, BLOCK, BLOCK), jnp.bfloat16),
            pltpu.VMEM((4, PER_STEP, BLOCK, BLOCK), jnp.int32),
            pltpu.VMEM((HALF_BLOCKS, WIDTH, BLOCK), jnp.float32),
            pltpu.VMEM((HALF_BLOCKS, WIDTH, BLOCK), jnp.bfloat16),
            pltpu.VMEM((BLOCK, BLOCK), jnp.float32),
            pltpu.VMEM((WIDTH, WIDTH), jnp.bfloat16),
            pltpu.SemaphoreType.DMA((2 * STEPS + 3,)),
        ],
        compiler_params=params(52),
        cost_estimate=pl.CostEstimate(flops=2 * NODES * WIDTH * WIDTH * NREL * 2, bytes_accessed=20 * MIB, transcendentals=0),
        name="aggregate",
    )(place, codes, pairs, *degrees, x_mine, x_other, wt, counts, self_weight)


def join_kernel(own_ref, other_ref, out_ref):
    per = out_ref.shape[0]
    step = pl.program_id(0)
    for t in range(per):
        out_ref[t] = (own_ref[step * per + t] + other_ref[t].astype(jnp.float32)).astype(jnp.bfloat16)


def join(own, other):
    spec = pl.BlockSpec((4, WIDTH, BLOCK), lambda i: (i, 0, 0))
    return pl.pallas_call(
        join_kernel,
        grid=(NBLK // 2 // 4,),
        in_specs=[VMEM_SPEC, spec],
        out_specs=spec,
        out_shape=jax.ShapeDtypeStruct((NBLK // 2, WIDTH, BLOCK), jnp.bfloat16),
        compiler_params=params(12),
        cost_estimate=pl.CostEstimate(flops=MIB, bytes_accessed=8 * MIB, transcendentals=0),
        name="join",
    )(own, other)


def finish_kernel(parts_ref, bias_ref, out_ref):
    for b in range(2):
        total = parts_ref[0, b].astype(jnp.float32)
        for k in range(1, parts_ref.shape[0]):
            total = total + parts_ref[k, b].astype(jnp.float32)
        rows = slice(b * BLOCK, (b + 1) * BLOCK)
        out_ref[rows, :] = jnp.maximum(total.T + bias_ref[...], 0.0).astype(jnp.bfloat16)


def finish(parts, bias):
    return pl.pallas_call(
        finish_kernel,
        out_shape=jax.ShapeDtypeStruct((2 * BLOCK, WIDTH), jnp.bfloat16),
        compiler_params=params(32),
        name="finish",
    )(parts, bias.reshape(1, WIDTH))


def pair_lists(codes, core):
    slots = jnp.arange(SLOTS, dtype=jnp.int32)
    target = codes // NBLK % NBLK
    half = (target // 2 % 2 == core).astype(jnp.int32)
    place = target // 4 * 2 + target % 2
    group = half * (NBLK // 2) + place
    same = group[None, :] == group[:, None]
    nth = jnp.sum((same & (slots[None, :] < slots[:, None])).astype(jnp.int32), axis=1)
    groups = jnp.arange(NBLK, dtype=jnp.int32)
    size = jnp.sum((group[None, :] == groups[:, None]).astype(jnp.int32), axis=1)
    need = (size + 1) // 2
    before = (groups[None, :] < groups[:, None]) & (groups[None, :] // (NBLK // 2) == groups[:, None] // (NBLK // 2))
    base = jnp.sum(jnp.where(before, need[None, :], 0), axis=1)
    at = half * PAIRS + nth // 2 + jnp.sum(jnp.where(group[:, None] == groups[None, :], base[None, :], 0), axis=1)
    entries = jnp.arange(2 * PAIRS, dtype=jnp.int32)
    match = at[None, :] == entries[:, None]
    is_first = match & (nth % 2 == 0)[None, :]
    is_second = match & (nth % 2 == 1)[None, :]
    first = SLOTS + jnp.sum(jnp.where(is_first, slots[None, :] - SLOTS, 0), axis=1)
    second = SLOTS + jnp.sum(jnp.where(is_second, slots[None, :] - SLOTS, 0), axis=1)
    where = jnp.sum(jnp.where(is_first, place[None, :], 0), axis=1)
    steps = (jnp.sum(need.reshape(2, NBLK // 2), axis=1) + UNROLL - 1) // UNROLL
    steps = jnp.broadcast_to(steps[:, None], (2, PAIRS))
    return jnp.stack([first.reshape(2, PAIRS), second.reshape(2, PAIRS), where.reshape(2, PAIRS), steps], axis=1)


def swap(array):
    return lax.ppermute(array, "rel", [(0, 1), (1, 0)])


def on_device(features, rel_weight, self_weight, bias, block_code, block_counts):
    row, col, core = lax.axis_index("rows"), lax.axis_index("cols"), lax.axis_index("rel")
    codes = block_code[0, 0, 0]
    counts = block_counts[0, 0, 0]

    x_half = lax.dynamic_slice(features.T, (0, core * HALF), (PIECE, HALF))
    x_sent = jnp.broadcast_to(x_half[None], (8, PIECE, HALF))
    x_sent, codes, core, row = lax.optimization_barrier((x_sent, codes, core, row))
    x_mine = lax.all_to_all(x_sent, "rows", 0, 0).reshape(WIDTH, HALF)

    padded = jnp.concatenate([codes, jnp.zeros((8,), jnp.int32)])
    place = jnp.stack([core, (row == col).astype(jnp.int32)]).astype(jnp.int32)
    pairs = pair_lists(codes, core)
    padded, place, pairs = lax.optimization_barrier((padded, place, pairs))
    deg_part, wt = prep(padded, counts, rel_weight)
    degrees = [deg_part] + [lax.ppermute(deg_part, "cols", [(i, (i + k) % 8) for i in range(8)]) for k in range(1, 8)]
    x_mine, wt, degrees = lax.optimization_barrier((x_mine, wt, degrees))

    x_other = swap(x_mine)
    to_sib, own = aggregate(place, padded, pairs, degrees, x_mine, x_other, wt, counts, self_weight)
    both = join(own, swap(to_sib))
    parts = lax.all_to_all(both.reshape(8, 2, WIDTH, BLOCK), "cols", 0, 0)
    return finish(parts, bias)


def solution(mesh):
    in_specs = (
        P("cols", "rows"),
        P("rel", None, None),
        P(),
        P(),
        P("rows", "cols", "rel", None),
        P("rows", "cols", "rel", None, None, None),
    )
    out_specs = P(("rows", "cols", "rel"), None)
    return jax.shard_map(on_device, mesh=mesh, in_specs=in_specs, out_specs=out_specs, check_vma=False)
```

time: 120 us -> 106 us (0.88)
  blocking collectives: 36.8 us -> 30 us
  Pallas kernels: 37.5 us -> 31.1 us
  starting transfers between devices: 25.4 us -> 21 us
  waiting for transfers between devices: 11.7 us -> 15.6 us
  local copies, waits for them, and re-layouts: 5.9 us -> 4.41 us
    all_to_all x1, blocking collectives: 36.8 us -> 30 us  [on_device(): parts = lax.all_to_all(both.reshape(8, 2, WIDTH, BLOCK), 'cols', 0, 0)]
    pallas_call x2 -> x1, Pallas kernels: 27.7 us -> 22.5 us  [aggregate(): pl.pallas_call(aggregate_kernel, in_specs=[SMEM_SPEC] * 3 + [VMEM_SPEC] *...]
    ppermute x2, waiting for transfers between devices: 3.79 us -> 8.39 us  [swap(): return lax.ppermute(array, 'rel', [(0, 1), (1, 0)])]
    ppermute x7, waiting for transfers between devices: 7 us -> 4.68 us  [on_device(): lax.ppermute(deg_part, 'cols', [(i, (i + k) % 8) for i in range(8)])]
    ppermute x7, starting transfers between devices: 15 us -> 12.8 us  [on_device(): lax.ppermute(deg_part, 'cols', [(i, (i + k) % 8) for i in range(8)])]
    all_to_all x1, waiting for transfers between devices: 0.96 us -> 2.49 us  [on_device(): x_mine = lax.all_to_all(x_sent, 'rows', 0, 0).reshape(WIDTH, HALF)]
    ppermute x2, starting transfers between devices: 1.73 us -> 0.22 us  [swap(): return lax.ppermute(array, 'rel', [(0, 1), (1, 0)])]
    unnamed x14 -> x28, local copies, waits for them, and re-layouts: 2.67 us -> 2.41 us
  transfers between devices with their start and end apart: 11 -> 10, of which waited for: 3 -> 5; matrix products, arithmetic and copies ran while one was open for 0% -> 2% of each run, Pallas kernels for 14% -> 7%
where the time goes in v5:
time: 106 us; the launch traced here: 104 us
  Pallas kernels  31.1 us (29%)
  blocking collectives  30 us (28%)
  starting transfers between devices  21 us (20%)
  waiting for transfers between devices  15.6 us (15%)
  local copies, waits for them, and re-layouts  4.41 us (4%)
  other arithmetic  2.18 us (2%)
    all_to_all x1, blocking collectives, on_device(): parts = lax.all_to_all(both.reshape(8, 2, WIDTH, BLOCK), 'cols', 0, 0)  30 us
    pallas_call x1, Pallas kernels, aggregate(): pl.pallas_call(aggregate_kernel, in_specs=[SMEM_SPEC] * 3 + [VMEM_SPEC] *...  22.5 us
    ppermute x7, starting transfers between devices, on_device(): lax.ppermute(deg_part, 'cols', [(i, (i + k) % 8) for i in range(8)])  12.8 us
    ppermute x2, waiting for transfers between devices, swap(): return lax.ppermute(array, 'rel', [(0, 1), (1, 0)])  8.39 us
    all_to_all x1, starting transfers between devices, on_device(): x_mine = lax.all_to_all(x_sent, 'rows', 0, 0).reshape(WIDTH, HALF)  8 us
    pallas_call x1, Pallas kernels, prep(): pl.pallas_call(prep_kernel, in_specs=[SMEM_SPEC, ANY_SPEC, ANY_SPEC], out...  7.11 us
    ppermute x7, waiting for transfers between devices, on_device(): lax.ppermute(deg_part, 'cols', [(i, (i + k) % 8) for i in range(8)])  4.68 us
    all_to_all x1, waiting for transfers between devices, on_device(): x_mine = lax.all_to_all(x_sent, 'rows', 0, 0).reshape(WIDTH, HALF)  2.49 us
  transfers between devices with their start and end apart: 10, of which 5 were waited for; matrix products, arithmetic and copies ran while one was open for 2% of the time, Pallas kernels for 7%

profile of v5, /device:TPU:0, one launch (start us, length us, event | category | flops | bytes accessed | tf_op | source)
XLA Modules:
  0.0 104.5 jit_solution(11750397803383559685)
XLA Ops:
  0.0 1.0 copy-done
  1.1 1.6 %broadcast_in_dim.76 = bf16[8,64,2048]{2,1,0:T(8,128)(2,1)} broadcast(bf16[64,2048]{1,0:T(8,128)(2,1)S(1)} %dynamic-slice_bitcast_fusion), dimensions={1,2} | broadcast | bytes 2359296 | tf_op jit(solution)/shard_map/broadcast_in_dim | solution.py:310
  2.6 8.0 %all-to-all-start = ((bf16[8,64,2048]{2,1,0:T(8,128)(2,1)}), bf16[8,64,2048]{2,1,0:T(8,128)(2,1)S(1)}, u32[]{:S(2)}, u32[]{:S(2)}) async-start(bf16[8,64,2048]{2,1,0:T(8,128)(2,1)} %broadcast_in_dim.76), calls=%async_computation | async-start | bytes 4194304 | tf_op jit(solution)/shard_map/all_to_all | solution.py:312
  11.9 0.6 pad_add_fusion.1.place_ref
  12.7 0.6 pad_add_fusion.pairs_ref
  13.3 7.1 %prep.1 = (bf16[128,128]{1,0:T(8,128)(2,1)S(1)}, bf16[4,512,512]{2,1,0:T(8,128)(2,1)}) custom-call(s32[136]{0:T(256)S(1)} %concatenate.3.codes_ref, s32[128,128,128]{2,1,0:T(8,128)} %bitcast.11, bf16[4,512,512]{2,1,0:T(8,128)(2,1)} %weight_hbm.1), custom_call_target="tpu_custom_call" | custom-call | flops 33554432 | bytes 12582912 | tf_op jit(solution)/shard_map/prep/pallas_call | solution.py:80
  20.5 3.3 %collective-permute-start.6 = (bf16[128,128]{1,0:T(8,128)(2,1)S(1)}, bf16[128,128]{1,0:T(8,128)(2,1)S(1)}, u32[]{:S(2)}, u32[]{:S(2)}) collective-permute-start(bf16[128,128]{1,0:T(8,128)(2,1)S(1)} %get-tuple-element.35.refs_0_), channel_id=1, source_target_pairs={{0,14},{2,0},{4,2},{6,4},{8,6},{10,8},{12,10},{14,12},{1,15},{3,1}... | collective-permute-start | bytes 98312 | tf_op jit(solution)/shard_map/ppermute | solution.py:319
  23.7 0.8 collective-permute-start.5
  24.5 1.3 %collective-permute-start.4 = (bf16[128,128]{1,0:T(8,128)(2,1)S(1)}, bf16[128,128]{1,0:T(8,128)(2,1)S(1)}, u32[]{:S(2)}, u32[]{:S(2)}) collective-permute-start(bf16[128,128]{1,0:T(8,128)(2,1)S(1)} %get-tuple-element.35.refs_0_), channel_id=1, source_target_pairs={{0,10},{2,12},{4,14},{6,0},{8,2},{10,4},{12,6},{14,8},{1,11},{3,13... | collective-permute-start | bytes 98312 | tf_op jit(solution)/shard_map/ppermute | solution.py:319
  25.9 1.0 collective-permute-start.3
  26.9 1.9 %collective-permute-start.2 = (bf16[128,128]{1,0:T(8,128)(2,1)S(1)}, bf16[128,128]{1,0:T(8,128)(2,1)S(1)}, u32[]{:S(2)}, u32[]{:S(2)}) collective-permute-start(bf16[128,128]{1,0:T(8,128)(2,1)S(1)} %get-tuple-element.35.refs_0_), channel_id=1, source_target_pairs={{0,6},{2,8},{4,10},{6,12},{8,14},{10,0},{12,2},{14,4},{1,7},{3,9},... | collective-permute-start | bytes 98312 | tf_op jit(solution)/shard_map/ppermute | solution.py:319
  28.8 2.4 %collective-permute-start.1 = (bf16[128,128]{1,0:T(8,128)(2,1)S(1)}, bf16[128,128]{1,0:T(8,128)(2,1)S(1)}, u32[]{:S(2)}, u32[]{:S(2)}) collective-permute-start(bf16[128,128]{1,0:T(8,128)(2,1)S(1)} %get-tuple-element.35.refs_0_), channel_id=1, source_target_pairs={{0,4},{2,6},{4,8},{6,10},{8,12},{10,14},{12,0},{14,2},{1,5},{3,7},... | collective-permute-start | bytes 98312 | tf_op jit(solution)/shard_map/ppermute | solution.py:319
  31.2 2.1 %collective-permute-start = (bf16[128,128]{1,0:T(8,128)(2,1)S(1)}, bf16[128,128]{1,0:T(8,128)(2,1)S(1)}, u32[]{:S(2)}, u32[]{:S(2)}) collective-permute-start(bf16[128,128]{1,0:T(8,128)(2,1)S(1)} %get-tuple-element.35.refs_0_), channel_id=1, source_target_pairs={{0,2},{2,4},{4,6},{6,8},{8,10},{10,12},{12,14},{14,0},{1,3},{3,5},... | collective-permute-start | bytes 98312 | tf_op jit(solution)/shard_map/ppermute | solution.py:319
  33.3 2.5 %collective-permute-done.1.refs_2_ = bf16[128,128]{1,0:T(8,128)(2,1)S(1)} collective-permute-done((bf16[128,128]{1,0:T(8,128)(2,1)S(1)}, bf16[128,128]{1,0:T(8,128)(2,1)S(1)}, u32[]{:S(2)}, u32[]{:S(2)}) %collective-permute-start.1) | collective-permute-done | bytes 32800 | tf_op jit(solution)/shard_map/ppermute | solution.py:319
  35.9 2.1 %collective-permute-done.refs_1_ = bf16[128,128]{1,0:T(8,128)(2,1)S(1)} collective-permute-done((bf16[128,128]{1,0:T(8,128)(2,1)S(1)}, bf16[128,128]{1,0:T(8,128)(2,1)S(1)}, u32[]{:S(2)}, u32[]{:S(2)}) %collective-permute-start) | collective-permute-done | bytes 32800 | tf_op jit(solution)/shard_map/ppermute | solution.py:319
  38.0 2.5 %all-to-all-done = bf16[8,64,2048]{2,1,0:T(8,128)(2,1)S(1)} async-done(((bf16[8,64,2048]{2,1,0:T(8,128)(2,1)}), bf16[8,64,2048]{2,1,0:T(8,128)(2,1)S(1)}, u32[]{:S(2)}, u32[]{:S(2)}) %all-to-all-start) | async-done | bytes 2097184 | tf_op jit(solution)/shard_map/all_to_all | solution.py:312
  40.5 4.2 %collective-permute-done.7.refs_9_ = bf16[512,2048]{1,0:T(8,128)(2,1)S(1)} collective-permute-done((bf16[512,2048]{1,0:T(8,128)(2,1)S(1)}, bf16[512,2048]{1,0:T(8,128)(2,1)S(1)}, u32[]{:S(2)}, u32[]{:S(2)}) %collective-permute-start.7) | collective-permute-done | bytes 2097184 | tf_op jit(solution)/shard_map/ppermute | solution.py:301
  44.7 1.3 %copy-done.6 = bf16[512,2048]{1,0:T(8,128)(2,1)} copy-done((bf16[512,2048]{1,0:T(8,128)(2,1)}, bf16[512,2048]{1,0:T(8,128)(2,1)S(1)}, u32[]{:S(2)}) %copy-start.6) | copy-done | bytes 2097176
  46.1 22.5 %aggregate.1 = (bf16[16,512,128]{2,1,0:T(8,128)(2,1)}, f32[16,512,128]{2,1,0:T(8,128)S(1)}) custom-call(s32[2]{0:T(128)} %pad_add_fusion.1.place_ref, s32[136]{0:T(256)} %copy-done.1, s32[2,4,72]{2,1,0:T(4,128)} %pad_add_fusion.pairs_ref, bf16[128,128]{1,0:T(8,128)(2,1)} %copy-done.3, bf16[128,128]{1,0:T(8,128)(2,1)} %copy-done.13, ...), custom_call_target="tpu_custom_call" | custom-call | flops 17179869184 | bytes 20971520 | tf_op jit(solution)/shard_map/aggregate/pallas_call | solution.py:209
  68.6 0.2 collective-permute-start.8
  68.8 4.2 %collective-permute-done.8.other_ref = bf16[16,512,128]{2,1,0:T(8,128)(2,1)S(1)} collective-permute-done((bf16[16,512,128]{2,1,0:T(8,128)(2,1)}, bf16[16,512,128]{2,1,0:T(8,128)(2,1)S(1)}, u32[]{:S(2)}, u32[]{:S(2)}) %collective-permute-start.8) | collective-permute-done | bytes 2097184 | tf_op jit(solution)/shard_map/ppermute | solution.py:301
  73.0 0.4 join.1
  73.5 30.0 %all_to_all.10.parts_ref = bf16[8,2,512,128]{3,2,1,0:T(8,128)(2,1)S(1)} all-to-all(bf16[8,2,512,128]{3,2,1,0:T(8,128)(2,1)S(1)} %bitcast.9), channel_id=1, replica_groups=mesh['rows'=8,'cols'=8,'rel'=2] {'cols'}, dimensions={0} | all-to-all | bytes 4194304 | tf_op jit(solution)/shard_map/all_to_all | solution.py:325
  103.4 1.1 %finish.1 = bf16[256,512]{1,0:T(8,128)(2,1)} custom-call(bf16[8,2,512,128]{3,2,1,0:T(8,128)(2,1)S(1)} %all_to_all.10.parts_ref, f32[1,512]{1,0:T(1,128)S(1)} %bitcast.10), custom_call_target="tpu_custom_call" | custom-call | tf_op jit(solution)/shard_map/finish/pallas_call | solution.py:266
  (54 shorter events, 1.5 us)
Async XLA Ops:
  0.0 1.0 copy-start
  2.6 8.0 %copy-start.5 = (s32[1,1,1,128]{3,2,1,0:T(1,128)S(1)}, s32[1,1,1,128]{3,2,1,0:T(1,128)}, u32[]{:S(2)}) copy-start(s32[1,1,1,128]{3,2,1,0:T(1,128)} %param.10) | copy-start | bytes 1540
  2.6 37.9 %all-to-all-start = ((bf16[8,64,2048]{2,1,0:T(8,128)(2,1)}), bf16[8,64,2048]{2,1,0:T(8,128)(2,1)S(1)}, u32[]{:S(2)}, u32[]{:S(2)}) async-start(bf16[8,64,2048]{2,1,0:T(8,128)(2,1)} %broadcast_in_dim.76), calls=%async_computation | async-start | bytes 4194304 | tf_op jit(solution)/shard_map/all_to_all | solution.py:312
  10.7 9.8 %copy-start.1 = (s32[136]{0:T(256)}, s32[136]{0:T(256)S(1)}, u32[]{:S(2)}) copy-start(s32[136]{0:T(256)S(1)} %concatenate.3.codes_ref) | copy-start | bytes 1636
  20.4 24.2 %copy-start.3 = (bf16[128,128]{1,0:T(8,128)(2,1)}, bf16[128,128]{1,0:T(8,128)(2,1)S(1)}, u32[]{:S(2)}) copy-start(bf16[128,128]{1,0:T(8,128)(2,1)S(1)} %get-tuple-element.35.refs_0_) | copy-start | bytes 98308
  20.5 8.3 %collective-permute-start.6 = (bf16[128,128]{1,0:T(8,128)(2,1)S(1)}, bf16[128,128]{1,0:T(8,128)(2,1)S(1)}, u32[]{:S(2)}, u32[]{:S(2)}) collective-permute-start(bf16[128,128]{1,0:T(8,128)(2,1)S(1)} %get-tuple-element.35.refs_0_), channel_id=1, source_target_pairs={{0,14},{2,0},{4,2},{6,4},{8,6},{10,8},{12,10},{14,12},{1,15},{3,1}... | collective-permute-start | bytes 98312 | tf_op jit(solution)/shard_map/ppermute | solution.py:319
  23.7 7.5 %collective-permute-start.5 = (bf16[128,128]{1,0:T(8,128)(2,1)S(1)}, bf16[128,128]{1,0:T(8,128)(2,1)S(1)}, u32[]{:S(2)}, u32[]{:S(2)}) collective-permute-start(bf16[128,128]{1,0:T(8,128)(2,1)S(1)} %get-tuple-element.35.refs_0_), channel_id=1, source_target_pairs={{0,12},{2,14},{4,0},{6,2},{8,4},{10,6},{12,8},{14,10},{1,13},{3,15... | collective-permute-start | bytes 98312 | tf_op jit(solution)/shard_map/ppermute | solution.py:319
  24.5 8.7 %collective-permute-start.4 = (bf16[128,128]{1,0:T(8,128)(2,1)S(1)}, bf16[128,128]{1,0:T(8,128)(2,1)S(1)}, u32[]{:S(2)}, u32[]{:S(2)}) collective-permute-start(bf16[128,128]{1,0:T(8,128)(2,1)S(1)} %get-tuple-element.35.refs_0_), channel_id=1, source_target_pairs={{0,10},{2,12},{4,14},{6,0},{8,2},{10,4},{12,6},{14,8},{1,11},{3,13... | collective-permute-start | bytes 98312 | tf_op jit(solution)/shard_map/ppermute | solution.py:319
  25.9 7.4 %collective-permute-start.3 = (bf16[128,128]{1,0:T(8,128)(2,1)S(1)}, bf16[128,128]{1,0:T(8,128)(2,1)S(1)}, u32[]{:S(2)}, u32[]{:S(2)}) collective-permute-start(bf16[128,128]{1,0:T(8,128)(2,1)S(1)} %get-tuple-element.35.refs_0_), channel_id=1, source_target_pairs={{0,8},{2,10},{4,12},{6,14},{8,0},{10,2},{12,4},{14,6},{1,9},{3,11}... | collective-permute-start | bytes 98312 | tf_op jit(solution)/shard_map/ppermute | solution.py:319
  26.9 6.4 %collective-permute-start.2 = (bf16[128,128]{1,0:T(8,128)(2,1)S(1)}, bf16[128,128]{1,0:T(8,128)(2,1)S(1)}, u32[]{:S(2)}, u32[]{:S(2)}) collective-permute-start(bf16[128,128]{1,0:T(8,128)(2,1)S(1)} %get-tuple-element.35.refs_0_), channel_id=1, source_target_pairs={{0,6},{2,8},{4,10},{6,12},{8,14},{10,0},{12,2},{14,4},{1,7},{3,9},... | collective-permute-start | bytes 98312 | tf_op jit(solution)/shard_map/ppermute | solution.py:319
  28.8 15.9 %copy-start.7 = (bf16[128,128]{1,0:T(8,128)(2,1)}, bf16[128,128]{1,0:T(8,128)(2,1)S(1)}, u32[]{:S(2)}) copy-start(bf16[128,128]{1,0:T(8,128)(2,1)S(1)} %collective-permute-done.6.refs_7_) | copy-start | bytes 98308
  28.8 7.1 %collective-permute-start.1 = (bf16[128,128]{1,0:T(8,128)(2,1)S(1)}, bf16[128,128]{1,0:T(8,128)(2,1)S(1)}, u32[]{:S(2)}, u32[]{:S(2)}) collective-permute-start(bf16[128,128]{1,0:T(8,128)(2,1)S(1)} %get-tuple-element.35.refs_0_), channel_id=1, source_target_pairs={{0,4},{2,6},{4,8},{6,10},{8,12},{10,14},{12,0},{14,2},{1,5},{3,7},... | collective-permute-start | bytes 98312 | tf_op jit(solution)/shard_map/ppermute | solution.py:319
  31.2 13.4 %copy-start.8 = (bf16[128,128]{1,0:T(8,128)(2,1)}, bf16[128,128]{1,0:T(8,128)(2,1)S(1)}, u32[]{:S(2)}) copy-start(bf16[128,128]{1,0:T(8,128)(2,1)S(1)} %collective-permute-done.5.refs_6_) | copy-start | bytes 98308
  31.2 6.8 %collective-permute-start = (bf16[128,128]{1,0:T(8,128)(2,1)S(1)}, bf16[128,128]{1,0:T(8,128)(2,1)S(1)}, u32[]{:S(2)}, u32[]{:S(2)}) collective-permute-start(bf16[128,128]{1,0:T(8,128)(2,1)S(1)} %get-tuple-element.35.refs_0_), channel_id=1, source_target_pairs={{0,2},{2,4},{4,6},{6,8},{8,10},{10,12},{12,14},{14,0},{1,3},{3,5},... | collective-permute-start | bytes 98312 | tf_op jit(solution)/shard_map/ppermute | solution.py:319
  33.3 11.4 %copy-start.9 = (bf16[128,128]{1,0:T(8,128)(2,1)}, bf16[128,128]{1,0:T(8,128)(2,1)S(1)}, u32[]{:S(2)}) copy-start(bf16[128,128]{1,0:T(8,128)(2,1)S(1)} %collective-permute-done.4.refs_5_) | copy-start | bytes 98308
  33.3 11.4 %copy-start.10 = (bf16[128,128]{1,0:T(8,128)(2,1)}, bf16[128,128]{1,0:T(8,128)(2,1)S(1)}, u32[]{:S(2)}) copy-start(bf16[128,128]{1,0:T(8,128)(2,1)S(1)} %collective-permute-done.3.refs_4_) | copy-start | bytes 98308
  33.3 11.4 %copy-start.11 = (bf16[128,128]{1,0:T(8,128)(2,1)}, bf16[128,128]{1,0:T(8,128)(2,1)S(1)}, u32[]{:S(2)}) copy-start(bf16[128,128]{1,0:T(8,128)(2,1)S(1)} %collective-permute-done.2.refs_3_) | copy-start | bytes 98308
  35.9 8.8 %copy-start.12 = (bf16[128,128]{1,0:T(8,128)(2,1)}, bf16[128,128]{1,0:T(8,128)(2,1)S(1)}, u32[]{:S(2)}) copy-start(bf16[128,128]{1,0:T(8,128)(2,1)S(1)} %collective-permute-done.1.refs_2_) | copy-start | bytes 98308
  38.0 6.7 %copy-start.13 = (bf16[128,128]{1,0:T(8,128)(2,1)}, bf16[128,128]{1,0:T(8,128)(2,1)S(1)}, u32[]{:S(2)}) copy-start(bf16[128,128]{1,0:T(8,128)(2,1)S(1)} %collective-permute-done.refs_1_) | copy-start | bytes 98308
  40.5 4.2 %copy-start.4 = (bf16[8,64,2048]{2,1,0:T(8,128)(2,1)}, bf16[8,64,2048]{2,1,0:T(8,128)(2,1)S(1)}, u32[]{:S(2)}) copy-start(bf16[8,64,2048]{2,1,0:T(8,128)(2,1)S(1)} %all-to-all-done) | copy-start | bytes 6291460
  40.5 4.2 %collective-permute-start.7 = (bf16[512,2048]{1,0:T(8,128)(2,1)S(1)}, bf16[512,2048]{1,0:T(8,128)(2,1)S(1)}, u32[]{:S(2)}, u32[]{:S(2)}) collective-permute-start(bf16[512,2048]{1,0:T(8,128)(2,1)S(1)} %bitcast.13), channel_id=1, source_target_pairs={{0,1},{1,0},{2,3},{3,2},{4,5},{5,4},{6,7},{7,6},{8,9},{9,8},{10,11... | collective-permute-start | bytes 6291464 | tf_op jit(solution)/shard_map/ppermute | solution.py:301
  44.7 1.3 %copy-start.6 = (bf16[512,2048]{1,0:T(8,128)(2,1)}, bf16[512,2048]{1,0:T(8,128)(2,1)S(1)}, u32[]{:S(2)}) copy-start(bf16[512,2048]{1,0:T(8,128)(2,1)S(1)} %collective-permute-done.7.refs_9_) | copy-start | bytes 6291460
  68.6 4.5 %collective-permute-start.8 = (bf16[16,512,128]{2,1,0:T(8,128)(2,1)}, bf16[16,512,128]{2,1,0:T(8,128)(2,1)S(1)}, u32[]{:S(2)}, u32[]{:S(2)}) collective-permute-start(bf16[16,512,128]{2,1,0:T(8,128)(2,1)} %get-tuple-element.46), channel_id=1, source_target_pairs={{0,1},{1,0},{2,3},{3,2},{4,5},{5,4},{6,7},{7,6},{8,9},{9,8},{10,11... | collective-permute-start | bytes 6291464 | tf_op jit(solution)/shard_map/ppermute | solution.py:301
  73.4 30.0 %copy-start.2 = (f32[512]{0:T(512)S(1)}, f32[512]{0:T(512)}, u32[]{:S(2)}) copy-start(f32[512]{0:T(512)} %param.9) | copy-start | bytes 6148

commit v6 on v5

--- a/solution.py
+++ b/solution.py
@@ -43,7 +43,7 @@
     return copy
 
 
-def prep_kernel(codes_ref, counts_hbm, weight_hbm, out_ref, wt_hbm, counts, weight, wt, deg_ref, sems):
+def prep_kernel(codes_ref, counts_hbm, weight_hbm, out_ref, cnt_hbm, wt_hbm, counts, cnt, weight, wt, deg_ref, sems):
     counts_copy = counts_copies(counts_hbm, counts, sems)
     weight_copy = pltpu.make_async_copy(weight_hbm, weight, sems.at[CHUNKS])
     wt_copy = pltpu.make_async_copy(wt, wt_hbm, sems.at[CHUNKS + 1])
@@ -53,14 +53,20 @@
     deg_ref[...] = jnp.zeros_like(deg_ref)
     ones = jnp.ones((8, BLOCK), jnp.bfloat16)
 
+    def cnt_copy(i):
+        at = pl.ds(i * PER, PER)
+        return pltpu.make_async_copy(cnt.at[at], cnt_hbm.at[at], sems.at[CHUNKS + 2 + i])
+
     def some(i, carry):
         counts_copy(i).wait()
         for s in range(PER):
             slot = i * PER + s
             c = counts[slot].astype(jnp.float32).astype(jnp.bfloat16)
+            cnt[slot] = c
             row = lax.dot_general(ones, c, NT, preferred_element_type=jnp.float32)
             seg = lax.shift_right_logical(codes_ref[slot], 5)
             deg_ref[pl.ds(seg, 1), :] += row[0:1]
+        cnt_copy(i).start()
         return carry
 
     lax.fori_loop(0, CHUNKS, some, 0)
@@ -73,6 +79,8 @@
 
     lax.fori_loop(0, NREL, turn, 0)
     wt_copy.start()
+    for i in range(CHUNKS):
+        cnt_copy(i).wait()
     wt_copy.wait()
 
 
@@ -80,17 +88,19 @@
     return pl.pallas_call(
         prep_kernel,
         in_specs=[SMEM_SPEC, ANY_SPEC, ANY_SPEC],
-        out_specs=[VMEM_SPEC, ANY_SPEC],
+        out_specs=[VMEM_SPEC, ANY_SPEC, ANY_SPEC],
         out_shape=[
             jax.ShapeDtypeStruct((NREL * NBLK, BLOCK), jnp.bfloat16),
+            jax.ShapeDtypeStruct((SLOTS, BLOCK, BLOCK), jnp.bfloat16),
             jax.ShapeDtypeStruct((NREL, WIDTH, WIDTH), jnp.bfloat16),
         ],
         scratch_shapes=[
             pltpu.VMEM((SLOTS, BLOCK, BLOCK), jnp.int32),
+            pltpu.VMEM((SLOTS, BLOCK, BLOCK), jnp.bfloat16),
             pltpu.VMEM((NREL, WIDTH, WIDTH), jnp.bfloat16),
             pltpu.VMEM((NREL, WIDTH, WIDTH), jnp.bfloat16),
             pltpu.VMEM((NREL * NBLK, BLOCK), jnp.float32),
-            pltpu.SemaphoreType.DMA((CHUNKS + 2,)),
+            pltpu.SemaphoreType.DMA((2 * CHUNKS + 2,)),
         ],
         compiler_params=params(52),
         cost_estimate=pl.CostEstimate(flops=2 * SLOTS * BLOCK * BLOCK * 8, bytes_accessed=12 * MIB, transcendentals=0),
@@ -123,113 +133,131 @@
 PER_STEP = SLOTS // STEPS
 
 
-def aggregate_kernel(place_ref, codes_ref, pairs_ref, *refs):
-    deg_refs, refs = refs[:8], refs[8:]
-    xm_hbm, xo_hbm, wt_hbm, counts_hbm, self_hbm, sib_hbm, own_ref, x, hid, wt, w, counts, acc, sib, inv_ref, self_w, sems = refs
-    core = place_ref[CORE]
-    near = STEPS // 2
-
-    def x_copy(n, source):
-        at = pl.ds(pl.multiple_of(lax.rem(n, near) * CHUNK, CHUNK), CHUNK)
-        return pltpu.make_async_copy(source.at[:, at], x.at[n], sems.at[n])
-
-    def counts_copy(n):
-        at = pl.ds(n * PER_STEP, PER_STEP)
-        return pltpu.make_async_copy(counts_hbm.at[at], counts.at[lax.rem(n, 4)], sems.at[STEPS + n])
-
-    wt_copy = pltpu.make_async_copy(wt_hbm, wt, sems.at[2 * STEPS])
-    sib_copy = pltpu.make_async_copy(sib, sib_hbm, sems.at[2 * STEPS + 1])
-    self_copy = pltpu.make_async_copy(self_hbm, self_w, sems.at[2 * STEPS + 2])
-    wt_copy.start()
-    for n in range(STEPS):
-        x_copy(n, xm_hbm if n < near else xo_hbm).start()
-        if n < 4:
-            counts_copy(n).start()
-
-    @pl.when(place_ref[DIAGONAL] == 1)
-    def _():
-        self_copy.start()
-
+def load_kernel(*refs):
+    deg_refs, (wt_hbm, cnt_hbm, wt_ref, cnt_ref, inv_ref, sems) = refs[:8], refs[8:]
+    copies = [pltpu.make_async_copy(wt_hbm, wt_ref, sems.at[0]), pltpu.make_async_copy(cnt_hbm, cnt_ref, sems.at[1])]
+    for copy in copies:
+        copy.start()
     degree = deg_refs[0][...].astype(jnp.float32)
     for ref in deg_refs[1:]:
         degree = degree + ref[...].astype(jnp.float32)
     inv_ref[...] = (1.0 / jnp.maximum(degree, 1.0)).T
+    for copy in copies:
+        copy.wait()
+
+
+def load(degrees, wt, cnt):
+    return pl.pallas_call(
+        load_kernel,
+        in_specs=[VMEM_SPEC] * 8 + [ANY_SPEC] * 2,
+        out_specs=[VMEM_SPEC] * 3,
+        out_shape=[
+            pltpu.VMEM(wt.shape, wt.dtype),
+            pltpu.VMEM(cnt.shape, cnt.dtype),
+            pltpu.VMEM((BLOCK, NREL * NBLK), jnp.float32),
+        ],
+        scratch_shapes=[pltpu.SemaphoreType.DMA((2,))],
+        compiler_params=params(12),
+        cost_estimate=pl.CostEstimate(flops=1, bytes_accessed=12 * MIB, transcendentals=0),
+        name="load",
+    )(*degrees, wt, cnt)
+
+
+def here(*arrays):
+    return [pltpu.with_memory_space_constraint(a, pltpu.VMEM) for a in arrays]
+
+
+def sibling_kernel(place_ref, codes_ref, pairs_ref, inv_ref, xm_ref, xo_ref, wt, cnt, sib_ref, hid, w, acc):
+    core = place_ref[CORE]
+    near = STEPS // 2
     w[SLOTS] = jnp.zeros((BLOCK, BLOCK), jnp.bfloat16)
-    wt_copy.wait()
-
-    def step(n, carry):
-        x_copy(n, xm_hbm).wait()
-        counts_copy(n).wait()
-        for u in range(PER_STEP):
-            slot = n * PER_STEP + u
-            seg = lax.shift_right_logical(codes_ref[slot], 5)
-            factor = jnp.take_along_axis(inv_ref[...], jnp.full((BLOCK, BLOCK), seg, jnp.int32), axis=1)
-            w[slot] = (counts[lax.rem(n, 4), u].astype(jnp.float32) * factor).astype(jnp.bfloat16)
-        zeros = jnp.zeros((HALF_BLOCKS // STEPS, WIDTH, BLOCK), jnp.float32)
-        acc[pl.ds(n * (HALF_BLOCKS // STEPS), HALF_BLOCKS // STEPS)] = zeros
-        own_ref[pl.ds(n * (HALF_BLOCKS // STEPS), HALF_BLOCKS // STEPS)] = zeros
-        first = jnp.where(n < near, core, 1 - core) * HALF_BLOCKS + lax.rem(n, near) * (CHUNK // BLOCK)
-        for r in range(NREL):
-            h = jnp.dot(wt[r], x[n], preferred_element_type=jnp.float32).astype(jnp.bfloat16)
-            for b in range(CHUNK // BLOCK):
-                hid[r, first + b] = h[:, b * BLOCK : (b + 1) * BLOCK]
-
-        @pl.when(n < STEPS - 4)
-        def _():
-            counts_copy(n + 4).start()
-
+
+    for k, x_ref in enumerate((xm_ref, xo_ref)):
+
+        def step(i, carry):
+            n = k * near + i
+            first = (core, 1 - core)[k] * HALF_BLOCKS + i * (CHUNK // BLOCK)
+            x = x_ref[:, pl.ds(pl.multiple_of(i * CHUNK, CHUNK), CHUNK)]
+            for r in range(NREL):
+                h = jnp.dot(wt[r], x, preferred_element_type=jnp.float32).astype(jnp.bfloat16)
+                for u in range(r * PER_STEP // NREL, (r + 1) * PER_STEP // NREL):
+                    slot = n * PER_STEP + u
+                    seg = lax.shift_right_logical(codes_ref[slot], 5)
+                    factor = jnp.take_along_axis(inv_ref[...], jnp.full((BLOCK, BLOCK), seg, jnp.int32), axis=1)
+                    w[slot] = (cnt[slot].astype(jnp.float32) * factor).astype(jnp.bfloat16)
+                for b in range(CHUNK // BLOCK):
+                    hid[r, first + b] = h[:, b * BLOCK : (b + 1) * BLOCK]
+            for t in range(HALF_BLOCKS // STEPS):
+                acc[n * (HALF_BLOCKS // STEPS) + t] = jnp.zeros((WIDTH, BLOCK), jnp.float32)
+            return carry
+
+        lax.fori_loop(0, near, step, 0)
+
+    slot_pairs(codes_ref, pairs_ref, 0, hid, w, acc)
+
+    def one(t, carry):
+        sib_ref[t] = acc[t].astype(jnp.bfloat16)
         return carry
 
-    lax.fori_loop(0, STEPS, step, 0)
+    lax.fori_loop(0, HALF_BLOCKS, one, 0)
+
+
+def sibling_part(place, codes, pairs, inverse, x_mine, x_other, wt, cnt):
+    return pl.pallas_call(
+        sibling_kernel,
+        in_specs=[SMEM_SPEC] * 3 + [VMEM_SPEC] * 5,
+        out_specs=[VMEM_SPEC] * 3,
+        out_shape=[
+            pltpu.VMEM((HALF_BLOCKS, WIDTH, BLOCK), jnp.bfloat16),
+            pltpu.VMEM(HID, jnp.bfloat16),
+            pltpu.VMEM((SLOTS + 1, BLOCK, BLOCK), jnp.bfloat16),
+        ],
+        scratch_shapes=[pltpu.VMEM((HALF_BLOCKS, WIDTH, BLOCK), jnp.float32)],
+        compiler_params=params(12),
+        cost_estimate=pl.CostEstimate(flops=2 * NODES * WIDTH * WIDTH * NREL, bytes_accessed=20 * MIB, transcendentals=0),
+        name="sibling_part",
+    )(place, codes, pairs, *here(inverse, x_mine, x_other, wt, cnt))
+
+
+def own_kernel(place_ref, codes_ref, pairs_ref, xm_ref, xo_ref, self_hbm, hid, w, own_ref, self_w, sems):
+    core = place_ref[CORE]
+    self_copy = pltpu.make_async_copy(self_hbm, self_w, sems.at[0])
+
+    @pl.when(place_ref[DIAGONAL] == 0)
+    def _():
+        def one(t, carry):
+            own_ref[t] = jnp.zeros((WIDTH, BLOCK), jnp.float32)
+            return carry
+
+        lax.fori_loop(0, HALF_BLOCKS, one, 0)
 
     @pl.when(place_ref[DIAGONAL] == 1)
     def _():
+        self_copy.start()
         self_copy.wait()
         turned = self_w[...].T
-        for n in range(STEPS):
-            cols = pl.ds(pl.multiple_of(core * (2 * BLOCK), 2 * BLOCK), 2 * BLOCK)
-            term = jnp.dot(turned, x[n, :, cols], preferred_element_type=jnp.float32)
-            half = core if n < near else 1 - core
-            for b in range(2):
-                own_ref[half * (HALF_BLOCKS // 2) + n % near * 2 + b] = term[:, b * BLOCK : (b + 1) * BLOCK]
-
-    slot_pairs(codes_ref, pairs_ref, 0, hid, w, acc)
-
-    def one(t, carry):
-        sib[t] = acc[t].astype(jnp.bfloat16)
-        return carry
-
-    lax.fori_loop(0, HALF_BLOCKS, one, 0)
-    sib_copy.start()
+        for half, x_ref in ((core, xm_ref), (1 - core, xo_ref)):
+            for q in range(HALF_BLOCKS // 4):
+                at = pl.multiple_of(core * (2 * BLOCK) + q * (4 * BLOCK), 2 * BLOCK)
+                term = jnp.dot(turned, x_ref[:, pl.ds(at, 2 * BLOCK)], preferred_element_type=jnp.float32)
+                for b in range(2):
+                    own_ref[half * (HALF_BLOCKS // 2) + q * 2 + b] = term[:, b * BLOCK : (b + 1) * BLOCK]
+
     slot_pairs(codes_ref, pairs_ref, 1, hid, w, own_ref)
-    sib_copy.wait()
-
-
-def aggregate(place, codes, pairs, degrees, x_mine, x_other, wt, counts, self_weight):
-    return pl.pallas_call(
-        aggregate_kernel,
-        in_specs=[SMEM_SPEC] * 3 + [VMEM_SPEC] * 8 + [ANY_SPEC] * 5,
-        out_specs=[ANY_SPEC, VMEM_SPEC],
-        out_shape=[
-            jax.ShapeDtypeStruct((HALF_BLOCKS, WIDTH, BLOCK), jnp.bfloat16),
-            pltpu.VMEM((HALF_BLOCKS, WIDTH, BLOCK), jnp.float32),
-        ],
-        scratch_shapes=[
-            pltpu.VMEM((STEPS, WIDTH, CHUNK), jnp.bfloat16),
-            pltpu.VMEM(HID, jnp.bfloat16),
-            pltpu.VMEM((NREL, WIDTH, WIDTH), jnp.bfloat16),
-            pltpu.VMEM((SLOTS + 1, BLOCK, BLOCK), jnp.bfloat16),
-            pltpu.VMEM((4, PER_STEP, BLOCK, BLOCK), jnp.int32),
-            pltpu.VMEM((HALF_BLOCKS, WIDTH, BLOCK), jnp.float32),
-            pltpu.VMEM((HALF_BLOCKS, WIDTH, BLOCK), jnp.bfloat16),
-            pltpu.VMEM((BLOCK, BLOCK), jnp.float32),
-            pltpu.VMEM((WIDTH, WIDTH), jnp.bfloat16),
-            pltpu.SemaphoreType.DMA((2 * STEPS + 3,)),
-        ],
-        compiler_params=params(52),
-        cost_estimate=pl.CostEstimate(flops=2 * NODES * WIDTH * WIDTH * NREL * 2, bytes_accessed=20 * MIB, transcendentals=0),
-        name="aggregate",
-    )(place, codes, pairs, *degrees, x_mine, x_other, wt, counts, self_weight)
+
+
+def own_part(place, codes, pairs, x_mine, x_other, self_weight, hid, w):
+    x_mine, x_other, hid, w = here(x_mine, x_other, hid, w)
+    return pl.pallas_call(
+        own_kernel,
+        in_specs=[SMEM_SPEC] * 3 + [VMEM_SPEC] * 2 + [ANY_SPEC] + [VMEM_SPEC] * 2,
+        out_specs=VMEM_SPEC,
+        out_shape=pltpu.VMEM((HALF_BLOCKS, WIDTH, BLOCK), jnp.float32),
+        scratch_shapes=[pltpu.VMEM((WIDTH, WIDTH), jnp.bfloat16), pltpu.SemaphoreType.DMA((1,))],
+        compiler_params=params(12),
+        cost_estimate=pl.CostEstimate(flops=2 * HALF * WIDTH * WIDTH * NREL, bytes_accessed=20 * MIB, transcendentals=0),
+        name="own_part",
+    )(place, codes, pairs, x_mine, x_other, self_weight, hid, w)
 
 
 def join_kernel(own_ref, other_ref, out_ref):
@@ -315,13 +343,16 @@
     place = jnp.stack([core, (row == col).astype(jnp.int32)]).astype(jnp.int32)
     pairs = pair_lists(codes, core)
     padded, place, pairs = lax.optimization_barrier((padded, place, pairs))
-    deg_part, wt = prep(padded, counts, rel_weight)
+    deg_part, cnt, wt = prep(padded, counts, rel_weight)
     degrees = [deg_part] + [lax.ppermute(deg_part, "cols", [(i, (i + k) % 8) for i in range(8)]) for k in range(1, 8)]
-    x_mine, wt, degrees = lax.optimization_barrier((x_mine, wt, degrees))
+    x_mine, cnt, wt, degrees = lax.optimization_barrier((x_mine, cnt, wt, degrees))
 
     x_other = swap(x_mine)
-    to_sib, own = aggregate(place, padded, pairs, degrees, x_mine, x_other, wt, counts, self_weight)
-    both = join(own, swap(to_sib))
+    wt, cnt, inverse = load(degrees, wt, cnt)
+    to_sib, hid, w = sibling_part(place, padded, pairs, inverse, x_mine, x_other, wt, cnt)
+    other = swap(to_sib)
+    own = own_part(place, padded, pairs, x_mine, x_other, self_weight, hid, w)
+    both = join(own, other)
     parts = lax.all_to_all(both.reshape(8, 2, WIDTH, BLOCK), "cols", 0, 0)
     return finish(parts, bias)
 

time: 106 us -> 98.4 us (0.928)
  waiting for transfers between devices: 15.6 us -> 7.28 us
  local copies, waits for them, and re-layouts: 4.41 us -> 6.85 us
  starting transfers between devices: 21 us -> 22.2 us
  other arithmetic: 2.18 us -> 1.05 us
    ppermute x2, waiting for transfers between devices: 8.39 us -> 0.01 us  [swap(): return lax.ppermute(array, 'rel', [(0, 1), (1, 0)])]
    unnamed x28 -> x12, local copies, waits for them, and re-layouts: 2.41 us -> 4.84 us
    pallas_call x1 -> x3, Pallas kernels: 22.5 us -> 20.4 us  [the longest x1 14.1 us: sibling_part(): pl.pallas_call(sibling_kernel, in_specs=[SMEM_SPEC] * 3 + [VMEM_SPEC] * 5...]
    ppermute x2, starting transfers between devices: 0.22 us -> 1.35 us  [swap(): return lax.ppermute(array, 'rel', [(0, 1), (1, 0)])]
    pallas_call x1, Pallas kernels: 7.11 us -> 8.21 us  [prep(): pl.pallas_call(prep_kernel, in_specs=[SMEM_SPEC, ANY_SPEC, ANY_SPEC], out...]
  transfers between devices with their start and end apart: 10 -> 10, of which waited for: 5 -> 3; matrix products, arithmetic and copies ran while one was open for 2% -> 2% of each run, Pallas kernels for 7% -> 15%
where the time goes in v6:
time: 98.4 us; the launch traced here: 97.4 us
  Pallas kernels  30.1 us (31%)
  blocking collectives  29.9 us (30%)
  starting transfers between devices  22.2 us (23%)
  waiting for transfers between devices  7.28 us (7%)
  local copies, waits for them, and re-layouts  6.85 us (7%)
  other arithmetic  1.05 us (1%)
    all_to_all x1, blocking collectives, on_device(): parts = lax.all_to_all(both.reshape(8, 2, WIDTH, BLOCK), 'cols', 0, 0)  29.9 us
    pallas_call x1, Pallas kernels, sibling_part(): pl.pallas_call(sibling_kernel, in_specs=[SMEM_SPEC] * 3 + [VMEM_SPEC] * 5...  14.1 us
    ppermute x7, starting transfers between devices, on_device(): lax.ppermute(deg_part, 'cols', [(i, (i + k) % 8) for i in range(8)])  12.8 us
    pallas_call x1, Pallas kernels, prep(): pl.pallas_call(prep_kernel, in_specs=[SMEM_SPEC, ANY_SPEC, ANY_SPEC], out...  8.21 us
    all_to_all x1, starting transfers between devices, on_device(): x_mine = lax.all_to_all(x_sent, 'rows', 0, 0).reshape(WIDTH, HALF)  8 us
    pallas_call x1, Pallas kernels, own_part(): pl.pallas_call(own_kernel, in_specs=[SMEM_SPEC] * 3 + [VMEM_SPEC] * 2 + [...  5.75 us
    unnamed x12, local copies, waits for them, and re-layouts  4.84 us
    ppermute x7, waiting for transfers between devices, on_device(): lax.ppermute(deg_part, 'cols', [(i, (i + k) % 8) for i in range(8)])  4.72 us
  transfers between devices with their start and end apart: 10, of which 3 were waited for; matrix products, arithmetic and copies ran while one was open for 2% of the time, Pallas kernels for 15%

profile of v6, /device:TPU:0, one launch (start us, length us, event | category | flops | bytes accessed | tf_op | source)
XLA Modules:
  0.0 97.4 jit_solution(13445434363477010873)
XLA Ops:
  0.0 1.0 %copy-done = bf16[4096,64]{0,1:T(8,128)(2,1)S(1)} copy-done((bf16[4096,64]{0,1:T(8,128)(2,1)S(1)}, bf16[4096,64]{0,1:T(8,128)(2,1)}, u32[]{:S(2)}) %copy-start) | copy-done | bytes 524312
  1.1 1.6 %broadcast_in_dim.76 = bf16[8,64,2048]{2,1,0:T(8,128)(2,1)} broadcast(bf16[64,2048]{1,0:T(8,128)(2,1)S(1)} %dynamic-slice_bitcast_fusion), dimensions={1,2} | broadcast | bytes 2359296 | tf_op jit(solution)/shard_map/broadcast_in_dim | solution.py:338
  2.7 8.0 %all-to-all-start = ((bf16[8,64,2048]{2,1,0:T(8,128)(2,1)}), bf16[8,64,2048]{2,1,0:T(8,128)(2,1)S(1)}, u32[]{:S(2)}, u32[]{:S(2)}) async-start(bf16[8,64,2048]{2,1,0:T(8,128)(2,1)} %broadcast_in_dim.76), calls=%async_computation | async-start | bytes 4194304 | tf_op jit(solution)/shard_map/all_to_all | solution.py:340
  11.4 0.2 select_reduce_fusion.2
  12.2 8.2 %prep.1 = (bf16[128,128]{1,0:T(8,128)(2,1)S(1)}, bf16[128,128,128]{2,1,0:T(8,128)(2,1)}, bf16[4,512,512]{2,1,0:T(8,128)(2,1)}) custom-call(s32[136]{0:T(256)S(1)} %concatenate.3.codes_ref, s32[128,128,128]{2,1,0:T(8,128)} %bitcast.14, bf16[4,512,512]{2,1,0:T(8,128)(2,1)} %weight_hbm.1), custom_call_target="tpu_custom_call" | custom-call | flops 33554432 | bytes 12582912 | tf_op jit(solution)/shard_map/prep/pallas_call | solution.py:88
  20.4 3.3 %collective-permute-start.6 = (bf16[128,128]{1,0:T(8,128)(2,1)S(1)}, bf16[128,128]{1,0:T(8,128)(2,1)S(1)}, u32[]{:S(2)}, u32[]{:S(2)}) collective-permute-start(bf16[128,128]{1,0:T(8,128)(2,1)S(1)} %get-tuple-element.43.refs_0_), channel_id=1, source_target_pairs={{0,14},{2,0},{4,2},{6,4},{8,6},{10,8},{12,10},{14,12},{1,15},{3,1}... | collective-permute-start | bytes 98312 | tf_op jit(solution)/shard_map/ppermute | solution.py:347
  23.7 0.8 collective-permute-start.5
  24.5 1.3 %collective-permute-start.4 = (bf16[128,128]{1,0:T(8,128)(2,1)S(1)}, bf16[128,128]{1,0:T(8,128)(2,1)S(1)}, u32[]{:S(2)}, u32[]{:S(2)}) collective-permute-start(bf16[128,128]{1,0:T(8,128)(2,1)S(1)} %get-tuple-element.43.refs_0_), channel_id=1, source_target_pairs={{0,10},{2,12},{4,14},{6,0},{8,2},{10,4},{12,6},{14,8},{1,11},{3,13... | collective-permute-start | bytes 98312 | tf_op jit(solution)/shard_map/ppermute | solution.py:347
  25.8 1.0 %collective-permute-start.3 = (bf16[128,128]{1,0:T(8,128)(2,1)S(1)}, bf16[128,128]{1,0:T(8,128)(2,1)S(1)}, u32[]{:S(2)}, u32[]{:S(2)}) collective-permute-start(bf16[128,128]{1,0:T(8,128)(2,1)S(1)} %get-tuple-element.43.refs_0_), channel_id=1, source_target_pairs={{0,8},{2,10},{4,12},{6,14},{8,0},{10,2},{12,4},{14,6},{1,9},{3,11}... | collective-permute-start | bytes 98312 | tf_op jit(solution)/shard_map/ppermute | solution.py:347
  26.8 1.9 %collective-permute-start.2 = (bf16[128,128]{1,0:T(8,128)(2,1)S(1)}, bf16[128,128]{1,0:T(8,128)(2,1)S(1)}, u32[]{:S(2)}, u32[]{:S(2)}) collective-permute-start(bf16[128,128]{1,0:T(8,128)(2,1)S(1)} %get-tuple-element.43.refs_0_), channel_id=1, source_target_pairs={{0,6},{2,8},{4,10},{6,12},{8,14},{10,0},{12,2},{14,4},{1,7},{3,9},... | collective-permute-start | bytes 98312 | tf_op jit(solution)/shard_map/ppermute | solution.py:347
  28.7 2.4 %collective-permute-start.1 = (bf16[128,128]{1,0:T(8,128)(2,1)S(1)}, bf16[128,128]{1,0:T(8,128)(2,1)S(1)}, u32[]{:S(2)}, u32[]{:S(2)}) collective-permute-start(bf16[128,128]{1,0:T(8,128)(2,1)S(1)} %get-tuple-element.43.refs_0_), channel_id=1, source_target_pairs={{0,4},{2,6},{4,8},{6,10},{8,12},{10,14},{12,0},{14,2},{1,5},{3,7},... | collective-permute-start | bytes 98312 | tf_op jit(solution)/shard_map/ppermute | solution.py:347
  31.2 2.1 %collective-permute-start = (bf16[128,128]{1,0:T(8,128)(2,1)S(1)}, bf16[128,128]{1,0:T(8,128)(2,1)S(1)}, u32[]{:S(2)}, u32[]{:S(2)}) collective-permute-start(bf16[128,128]{1,0:T(8,128)(2,1)S(1)} %get-tuple-element.43.refs_0_), channel_id=1, source_target_pairs={{0,2},{2,4},{4,6},{6,8},{8,10},{10,12},{12,14},{14,0},{1,3},{3,5},... | collective-permute-start | bytes 98312 | tf_op jit(solution)/shard_map/ppermute | solution.py:347
  33.2 2.6 %collective-permute-done.1.refs_2_ = bf16[128,128]{1,0:T(8,128)(2,1)S(1)} collective-permute-done((bf16[128,128]{1,0:T(8,128)(2,1)S(1)}, bf16[128,128]{1,0:T(8,128)(2,1)S(1)}, u32[]{:S(2)}, u32[]{:S(2)}) %collective-permute-start.1) | collective-permute-done | bytes 32800 | tf_op jit(solution)/shard_map/ppermute | solution.py:347
  35.8 2.1 %collective-permute-done.refs_1_ = bf16[128,128]{1,0:T(8,128)(2,1)S(1)} collective-permute-done((bf16[128,128]{1,0:T(8,128)(2,1)S(1)}, bf16[128,128]{1,0:T(8,128)(2,1)S(1)}, u32[]{:S(2)}, u32[]{:S(2)}) %collective-permute-start) | collective-permute-done | bytes 32800 | tf_op jit(solution)/shard_map/ppermute | solution.py:347
  38.0 2.6 %all-to-all-done = bf16[8,64,2048]{2,1,0:T(8,128)(2,1)S(1)} async-done(((bf16[8,64,2048]{2,1,0:T(8,128)(2,1)}), bf16[8,64,2048]{2,1,0:T(8,128)(2,1)S(1)}, u32[]{:S(2)}, u32[]{:S(2)}) %all-to-all-start) | async-done | bytes 2097184 | tf_op jit(solution)/shard_map/all_to_all | solution.py:340
  40.5 2.2 %copy-done.1 = bf16[128,128,128]{2,1,0:T(8,128)(2,1)S(1)} copy-done((bf16[128,128,128]{2,1,0:T(8,128)(2,1)S(1)}, bf16[128,128,128]{2,1,0:T(8,128)(2,1)}, u32[]{:S(2)}) %copy-start.1) | copy-done | bytes 4194328
  42.7 1.6 %copy-done.2 = bf16[4,512,512]{2,1,0:T(8,128)(2,1)S(1)} copy-done((bf16[4,512,512]{2,1,0:T(8,128)(2,1)S(1)}, bf16[4,512,512]{2,1,0:T(8,128)(2,1)}, u32[]{:S(2)}) %copy-start.2) | copy-done | bytes 2097176
  44.3 0.6 load.1
  44.9 14.1 %sibling_part.1 = (bf16[16,512,128]{2,1,0:T(8,128)(2,1)S(1)}, bf16[4,32,512,128]{3,2,1,0:T(8,128)(2,1)S(1)}, bf16[129,128,128]{2,1,0:T(8,128)(2,1)S(1)}) custom-call(s32[2]{0:T(128)S(1)} %pad_add_fusion.1.place_ref, s32[136]{0:T(256)S(1)} %concatenate.3.codes_ref, s32[2,4,72]{2,1,0:T(4,128)S(1)} %pad_add_fusion.pairs_ref, ...), custom_call_target="tpu_custom_call" | custom-call | flops 8589934592 | bytes 20971520 | tf_op jit(solution)/shard_map/sibling_part/pallas_call | solution.py:206
  58.9 1.3 %collective-permute-start.8 = (bf16[16,512,128]{2,1,0:T(8,128)(2,1)S(1)}, bf16[16,512,128]{2,1,0:T(8,128)(2,1)S(1)}, u32[]{:S(2)}, u32[]{:S(2)}) collective-permute-start(bf16[16,512,128]{2,1,0:T(8,128)(2,1)S(1)} %get-tuple-element.58), channel_id=1, source_target_pairs={{0,1},{1,0},{2,3},{3,2},{4,5},{5,4},{6,7},{7,6},{8,9},{9,8},{10,11... | collective-permute-start | bytes 6291464 | tf_op jit(solution)/shard_map/ppermute | solution.py:329
  60.3 5.8 %own_part.1.own_ref = f32[16,512,128]{2,1,0:T(8,128)S(1)} custom-call(s32[2]{0:T(128)S(1)} %pad_add_fusion.1.place_ref, s32[136]{0:T(256)S(1)} %concatenate.3.codes_ref, s32[2,4,72]{2,1,0:T(4,128)S(1)} %pad_add_fusion.pairs_ref, bf16[512,2048]{1,0:T(8,128)(2,1)S(1)} %bitcast.11, bf16[512,2048]{1,0:T(8,128)(2,1)S(1)} %collective-permute-done.7.xo_ref, ...), custom_call_target="tpu_custom_call" | custom-call | flops 4294967296 | bytes 20971520 | tf_op jit(solution)/shard_map/own_part/pallas_call | solution.py:251
  66.1 0.4 join.1
  66.5 29.9 %all_to_all.10.parts_ref = bf16[8,2,512,128]{3,2,1,0:T(8,128)(2,1)S(1)} all-to-all(bf16[8,2,512,128]{3,2,1,0:T(8,128)(2,1)S(1)} %bitcast.12), channel_id=1, replica_groups=mesh['rows'=8,'cols'=8,'rel'=2] {'cols'}, dimensions={0} | all-to-all | bytes 4194304 | tf_op jit(solution)/shard_map/all_to_all | solution.py:356
  96.4 1.1 %finish.1 = bf16[256,512]{1,0:T(8,128)(2,1)} custom-call(bf16[8,2,512,128]{3,2,1,0:T(8,128)(2,1)S(1)} %all_to_all.10.parts_ref, f32[1,512]{1,0:T(1,128)S(1)} %bitcast.13), custom_call_target="tpu_custom_call" | custom-call | tf_op jit(solution)/shard_map/finish/pallas_call | solution.py:294
  (40 shorter events, 1.3 us)
Async XLA Ops:
  0.0 1.0 %copy-start = (bf16[4096,64]{0,1:T(8,128)(2,1)S(1)}, bf16[4096,64]{0,1:T(8,128)(2,1)}, u32[]{:S(2)}) copy-start(bf16[4096,64]{0,1:T(8,128)(2,1)} %param.6) | copy-start | bytes 1572868
  2.6 8.0 %copy-start.5 = (s32[1,1,1,128]{3,2,1,0:T(1,128)S(1)}, s32[1,1,1,128]{3,2,1,0:T(1,128)}, u32[]{:S(2)}) copy-start(s32[1,1,1,128]{3,2,1,0:T(1,128)} %param.10) | copy-start | bytes 1540
  2.7 37.9 %all-to-all-start = ((bf16[8,64,2048]{2,1,0:T(8,128)(2,1)}), bf16[8,64,2048]{2,1,0:T(8,128)(2,1)S(1)}, u32[]{:S(2)}, u32[]{:S(2)}) async-start(bf16[8,64,2048]{2,1,0:T(8,128)(2,1)} %broadcast_in_dim.76), calls=%async_computation | async-start | bytes 4194304 | tf_op jit(solution)/shard_map/all_to_all | solution.py:340
  20.4 8.3 %collective-permute-start.6 = (bf16[128,128]{1,0:T(8,128)(2,1)S(1)}, bf16[128,128]{1,0:T(8,128)(2,1)S(1)}, u32[]{:S(2)}, u32[]{:S(2)}) collective-permute-start(bf16[128,128]{1,0:T(8,128)(2,1)S(1)} %get-tuple-element.43.refs_0_), channel_id=1, source_target_pairs={{0,14},{2,0},{4,2},{6,4},{8,6},{10,8},{12,10},{14,12},{1,15},{3,1}... | collective-permute-start | bytes 98312 | tf_op jit(solution)/shard_map/ppermute | solution.py:347
  23.7 7.5 %collective-permute-start.5 = (bf16[128,128]{1,0:T(8,128)(2,1)S(1)}, bf16[128,128]{1,0:T(8,128)(2,1)S(1)}, u32[]{:S(2)}, u32[]{:S(2)}) collective-permute-start(bf16[128,128]{1,0:T(8,128)(2,1)S(1)} %get-tuple-element.43.refs_0_), channel_id=1, source_target_pairs={{0,12},{2,14},{4,0},{6,2},{8,4},{10,6},{12,8},{14,10},{1,13},{3,15... | collective-permute-start | bytes 98312 | tf_op jit(solution)/shard_map/ppermute | solution.py:347
  24.5 8.7 %collective-permute-start.4 = (bf16[128,128]{1,0:T(8,128)(2,1)S(1)}, bf16[128,128]{1,0:T(8,128)(2,1)S(1)}, u32[]{:S(2)}, u32[]{:S(2)}) collective-permute-start(bf16[128,128]{1,0:T(8,128)(2,1)S(1)} %get-tuple-element.43.refs_0_), channel_id=1, source_target_pairs={{0,10},{2,12},{4,14},{6,0},{8,2},{10,4},{12,6},{14,8},{1,11},{3,13... | collective-permute-start | bytes 98312 | tf_op jit(solution)/shard_map/ppermute | solution.py:347
  25.8 7.4 %collective-permute-start.3 = (bf16[128,128]{1,0:T(8,128)(2,1)S(1)}, bf16[128,128]{1,0:T(8,128)(2,1)S(1)}, u32[]{:S(2)}, u32[]{:S(2)}) collective-permute-start(bf16[128,128]{1,0:T(8,128)(2,1)S(1)} %get-tuple-element.43.refs_0_), channel_id=1, source_target_pairs={{0,8},{2,10},{4,12},{6,14},{8,0},{10,2},{12,4},{14,6},{1,9},{3,11}... | collective-permute-start | bytes 98312 | tf_op jit(solution)/shard_map/ppermute | solution.py:347
  26.8 6.4 %collective-permute-start.2 = (bf16[128,128]{1,0:T(8,128)(2,1)S(1)}, bf16[128,128]{1,0:T(8,128)(2,1)S(1)}, u32[]{:S(2)}, u32[]{:S(2)}) collective-permute-start(bf16[128,128]{1,0:T(8,128)(2,1)S(1)} %get-tuple-element.43.refs_0_), channel_id=1, source_target_pairs={{0,6},{2,8},{4,10},{6,12},{8,14},{10,0},{12,2},{14,4},{1,7},{3,9},... | collective-permute-start | bytes 98312 | tf_op jit(solution)/shard_map/ppermute | solution.py:347
  28.7 7.1 %collective-permute-start.1 = (bf16[128,128]{1,0:T(8,128)(2,1)S(1)}, bf16[128,128]{1,0:T(8,128)(2,1)S(1)}, u32[]{:S(2)}, u32[]{:S(2)}) collective-permute-start(bf16[128,128]{1,0:T(8,128)(2,1)S(1)} %get-tuple-element.43.refs_0_), channel_id=1, source_target_pairs={{0,4},{2,6},{4,8},{6,10},{8,12},{10,14},{12,0},{14,2},{1,5},{3,7},... | collective-permute-start | bytes 98312 | tf_op jit(solution)/shard_map/ppermute | solution.py:347
  31.2 6.8 %collective-permute-start = (bf16[128,128]{1,0:T(8,128)(2,1)S(1)}, bf16[128,128]{1,0:T(8,128)(2,1)S(1)}, u32[]{:S(2)}, u32[]{:S(2)}) collective-permute-start(bf16[128,128]{1,0:T(8,128)(2,1)S(1)} %get-tuple-element.43.refs_0_), channel_id=1, source_target_pairs={{0,2},{2,4},{4,6},{6,8},{8,10},{10,12},{12,14},{14,0},{1,3},{3,5},... | collective-permute-start | bytes 98312 | tf_op jit(solution)/shard_map/ppermute | solution.py:347
  40.5 4.3 %collective-permute-start.7 = (bf16[512,2048]{1,0:T(8,128)(2,1)S(1)}, bf16[512,2048]{1,0:T(8,128)(2,1)S(1)}, u32[]{:S(2)}, u32[]{:S(2)}) collective-permute-start(bf16[512,2048]{1,0:T(8,128)(2,1)S(1)} %bitcast.9), channel_id=1, source_target_pairs={{0,1},{1,0},{2,3},{3,2},{4,5},{5,4},{6,7},{7,6},{8,9},{9,8},{10,11... | collective-permute-start | bytes 6291464 | tf_op jit(solution)/shard_map/ppermute | solution.py:329
  40.5 2.2 %copy-start.1 = (bf16[128,128,128]{2,1,0:T(8,128)(2,1)S(1)}, bf16[128,128,128]{2,1,0:T(8,128)(2,1)}, u32[]{:S(2)}) copy-start(bf16[128,128,128]{2,1,0:T(8,128)(2,1)} %get-tuple-element.52.refs_9_) | copy-start | bytes 12582916
  42.7 1.6 %copy-start.2 = (bf16[4,512,512]{2,1,0:T(8,128)(2,1)S(1)}, bf16[4,512,512]{2,1,0:T(8,128)(2,1)}, u32[]{:S(2)}) copy-start(bf16[4,512,512]{2,1,0:T(8,128)(2,1)} %get-tuple-element.51.refs_8_) | copy-start | bytes 6291460
  44.9 15.4 %copy-start.3 = (bf16[512,512]{1,0:T(8,128)(2,1)S(1)}, bf16[512,512]{1,0:T(8,128)(2,1)}, u32[]{:S(2)}) copy-start(bf16[512,512]{1,0:T(8,128)(2,1)} %self_hbm.1) | copy-start | bytes 1572868
  58.9 7.1 %collective-permute-start.8 = (bf16[16,512,128]{2,1,0:T(8,128)(2,1)S(1)}, bf16[16,512,128]{2,1,0:T(8,128)(2,1)S(1)}, u32[]{:S(2)}, u32[]{:S(2)}) collective-permute-start(bf16[16,512,128]{2,1,0:T(8,128)(2,1)S(1)} %get-tuple-element.58), channel_id=1, source_target_pairs={{0,1},{1,0},{2,3},{3,2},{4,5},{5,4},{6,7},{7,6},{8,9},{9,8},{10,11... | collective-permute-start | bytes 6291464 | tf_op jit(solution)/shard_map/ppermute | solution.py:329
  66.5 29.9 %copy-start.4 = (f32[512]{0:T(512)S(1)}, f32[512]{0:T(512)}, u32[]{:S(2)}) copy-start(f32[512]{0:T(512)} %param.9) | copy-start | bytes 6148

commit v7 on v6

--- a/solution.py
+++ b/solution.py
@@ -134,7 +134,7 @@
 
 
 def load_kernel(*refs):
-    deg_refs, (wt_hbm, cnt_hbm, wt_ref, cnt_ref, inv_ref, sems) = refs[:8], refs[8:]
+    deg_refs, (place_ref, x_ref, wt_hbm, cnt_hbm, wt_ref, cnt_ref, inv_ref, hid, sems) = refs[:8], refs[8:]
     copies = [pltpu.make_async_copy(wt_hbm, wt_ref, sems.at[0]), pltpu.make_async_copy(cnt_hbm, cnt_ref, sems.at[1])]
     for copy in copies:
         copy.start()
@@ -142,57 +142,66 @@
     for ref in deg_refs[1:]:
         degree = degree + ref[...].astype(jnp.float32)
     inv_ref[...] = (1.0 / jnp.maximum(degree, 1.0)).T
-    for copy in copies:
-        copy.wait()
-
-
-def load(degrees, wt, cnt):
+    copies[0].wait()
+
+    def step(i, carry):
+        first = place_ref[CORE] * HALF_BLOCKS + i * (CHUNK // BLOCK)
+        x = x_ref[:, pl.ds(pl.multiple_of(i * CHUNK, CHUNK), CHUNK)]
+        for r in range(NREL):
+            h = jnp.dot(wt_ref[r], x, preferred_element_type=jnp.float32).astype(jnp.bfloat16)
+            for b in range(CHUNK // BLOCK):
+                hid[r, first + b] = h[:, b * BLOCK : (b + 1) * BLOCK]
+        return carry
+
+    lax.fori_loop(0, STEPS // 2, step, 0)
+    copies[1].wait()
+
+
+def load(degrees, place, x_mine, wt, cnt):
     return pl.pallas_call(
         load_kernel,
-        in_specs=[VMEM_SPEC] * 8 + [ANY_SPEC] * 2,
-        out_specs=[VMEM_SPEC] * 3,
+        in_specs=[VMEM_SPEC] * 8 + [SMEM_SPEC, VMEM_SPEC] + [ANY_SPEC] * 2,
+        out_specs=[VMEM_SPEC] * 4,
         out_shape=[
             pltpu.VMEM(wt.shape, wt.dtype),
             pltpu.VMEM(cnt.shape, cnt.dtype),
             pltpu.VMEM((BLOCK, NREL * NBLK), jnp.float32),
+            pltpu.VMEM(HID, jnp.bfloat16),
         ],
         scratch_shapes=[pltpu.SemaphoreType.DMA((2,))],
-        compiler_params=params(12),
-        cost_estimate=pl.CostEstimate(flops=1, bytes_accessed=12 * MIB, transcendentals=0),
-        name="load",
-    )(*degrees, wt, cnt)
+        compiler_params=params(28),
+        cost_estimate=pl.CostEstimate(flops=NODES * WIDTH * WIDTH * NREL, bytes_accessed=12 * MIB, transcendentals=0),
+        name="own_hidden",
+    )(*degrees, place, *here(x_mine), wt, cnt)
 
 
 def here(*arrays):
     return [pltpu.with_memory_space_constraint(a, pltpu.VMEM) for a in arrays]
 
 
-def sibling_kernel(place_ref, codes_ref, pairs_ref, inv_ref, xm_ref, xo_ref, wt, cnt, sib_ref, hid, w, acc):
+def sibling_kernel(place_ref, codes_ref, pairs_ref, inv_ref, x_ref, wt, cnt, hid_in, sib_ref, hid, w, acc):
     core = place_ref[CORE]
-    near = STEPS // 2
     w[SLOTS] = jnp.zeros((BLOCK, BLOCK), jnp.bfloat16)
-
-    for k, x_ref in enumerate((xm_ref, xo_ref)):
-
-        def step(i, carry):
-            n = k * near + i
-            first = (core, 1 - core)[k] * HALF_BLOCKS + i * (CHUNK // BLOCK)
-            x = x_ref[:, pl.ds(pl.multiple_of(i * CHUNK, CHUNK), CHUNK)]
-            for r in range(NREL):
-                h = jnp.dot(wt[r], x, preferred_element_type=jnp.float32).astype(jnp.bfloat16)
-                for u in range(r * PER_STEP // NREL, (r + 1) * PER_STEP // NREL):
-                    slot = n * PER_STEP + u
-                    seg = lax.shift_right_logical(codes_ref[slot], 5)
-                    factor = jnp.take_along_axis(inv_ref[...], jnp.full((BLOCK, BLOCK), seg, jnp.int32), axis=1)
-                    w[slot] = (cnt[slot].astype(jnp.float32) * factor).astype(jnp.bfloat16)
-                for b in range(CHUNK // BLOCK):
-                    hid[r, first + b] = h[:, b * BLOCK : (b + 1) * BLOCK]
-            for t in range(HALF_BLOCKS // STEPS):
-                acc[n * (HALF_BLOCKS // STEPS) + t] = jnp.zeros((WIDTH, BLOCK), jnp.float32)
-            return carry
-
-        lax.fori_loop(0, near, step, 0)
-
+    per_step = 2 * PER_STEP
+    clear = 2 * HALF_BLOCKS // STEPS
+
+    def step(i, carry):
+        first = (1 - core) * HALF_BLOCKS + i * (CHUNK // BLOCK)
+        x = x_ref[:, pl.ds(pl.multiple_of(i * CHUNK, CHUNK), CHUNK)]
+        for r in range(NREL):
+            h = jnp.dot(wt[r], x, preferred_element_type=jnp.float32).astype(jnp.bfloat16)
+            for u in range(r * per_step // NREL, (r + 1) * per_step // NREL):
+                slot = i * per_step + u
+                seg = lax.shift_right_logical(codes_ref[slot], 5)
+                factor = jnp.take_along_axis(inv_ref[...], jnp.full((BLOCK, BLOCK), seg, jnp.int32), axis=1)
+                w[slot] = (cnt[slot].astype(jnp.float32) * factor).astype(jnp.bfloat16)
+            for b in range(CHUNK // BLOCK):
+                hid[r, first + b] = h[:, b * BLOCK : (b + 1) * BLOCK]
+        for t in range(clear):
+            acc[i * clear + t] = jnp.zeros((WIDTH, BLOCK), jnp.float32)
+        return carry
+
+    lax.fori_loop(0, STEPS // 2, step, 0)
     slot_pairs(codes_ref, pairs_ref, 0, hid, w, acc)
 
     def one(t, carry):
@@ -202,7 +211,7 @@
     lax.fori_loop(0, HALF_BLOCKS, one, 0)
 
 
-def sibling_part(place, codes, pairs, inverse, x_mine, x_other, wt, cnt):
+def sibling_part(place, codes, pairs, inverse, x_other, wt, cnt, hid):
     return pl.pallas_call(
         sibling_kernel,
         in_specs=[SMEM_SPEC] * 3 + [VMEM_SPEC] * 5,
@@ -212,16 +221,16 @@
             pltpu.VMEM(HID, jnp.bfloat16),
             pltpu.VMEM((SLOTS + 1, BLOCK, BLOCK), jnp.bfloat16),
         ],
+        input_output_aliases={7: 1},
         scratch_shapes=[pltpu.VMEM((HALF_BLOCKS, WIDTH, BLOCK), jnp.float32)],
         compiler_params=params(12),
         cost_estimate=pl.CostEstimate(flops=2 * NODES * WIDTH * WIDTH * NREL, bytes_accessed=20 * MIB, transcendentals=0),
         name="sibling_part",
-    )(place, codes, pairs, *here(inverse, x_mine, x_other, wt, cnt))
-
-
-def own_kernel(place_ref, codes_ref, pairs_ref, xm_ref, xo_ref, self_hbm, hid, w, own_ref, self_w, sems):
+    )(place, codes, pairs, *here(inverse, x_other, wt, cnt, hid))
+
+
+def own_kernel(place_ref, codes_ref, pairs_ref, xm_ref, xo_ref, self_ref, hid, w, own_ref):
     core = place_ref[CORE]
-    self_copy = pltpu.make_async_copy(self_hbm, self_w, sems.at[0])
 
     @pl.when(place_ref[DIAGONAL] == 0)
     def _():
@@ -233,9 +242,7 @@
 
     @pl.when(place_ref[DIAGONAL] == 1)
     def _():
-        self_copy.start()
-        self_copy.wait()
-        turned = self_w[...].T
+        turned = self_ref[...].T
         for half, x_ref in ((core, xm_ref), (1 - core, xo_ref)):
             for q in range(HALF_BLOCKS // 4):
                 at = pl.multiple_of(core * (2 * BLOCK) + q * (4 * BLOCK), 2 * BLOCK)
@@ -250,10 +257,9 @@
     x_mine, x_other, hid, w = here(x_mine, x_other, hid, w)
     return pl.pallas_call(
         own_kernel,
-        in_specs=[SMEM_SPEC] * 3 + [VMEM_SPEC] * 2 + [ANY_SPEC] + [VMEM_SPEC] * 2,
+        in_specs=[SMEM_SPEC] * 3 + [VMEM_SPEC] * 5,
         out_specs=VMEM_SPEC,
         out_shape=pltpu.VMEM((HALF_BLOCKS, WIDTH, BLOCK), jnp.float32),
-        scratch_shapes=[pltpu.VMEM((WIDTH, WIDTH), jnp.bfloat16), pltpu.SemaphoreType.DMA((1,))],
         compiler_params=params(12),
         cost_estimate=pl.CostEstimate(flops=2 * HALF * WIDTH * WIDTH * NREL, bytes_accessed=20 * MIB, transcendentals=0),
         name="own_part",
@@ -348,8 +354,8 @@
     x_mine, cnt, wt, degrees = lax.optimization_barrier((x_mine, cnt, wt, degrees))
 
     x_other = swap(x_mine)
-    wt, cnt, inverse = load(degrees, wt, cnt)
-    to_sib, hid, w = sibling_part(place, padded, pairs, inverse, x_mine, x_other, wt, cnt)
+    wt, cnt, inverse, hid = load(degrees, place, x_mine, wt, cnt)
+    to_sib, hid, w = sibling_part(place, padded, pairs, inverse, x_other, wt, cnt, hid)
     other = swap(to_sib)
     own = own_part(place, padded, pairs, x_mine, x_other, self_weight, hid, w)
     both = join(own, other)

time: 98.4 us -> 96.2 us (0.978)
  local copies, waits for them, and re-layouts: 6.85 us -> 3.07 us
  Pallas kernels: 30.1 us -> 32.5 us
    pallas_call x2, Pallas kernels: 6.31 us -> 12.9 us  [the longest x1 7.21 us: load(): pl.pallas_call(load_kernel, in_specs=[VMEM_SPEC] * 8 + [SMEM_SPEC, VMEM_S...]
    pallas_call x1, Pallas kernels: 14.1 us -> 9.87 us  [sibling_part(): pl.pallas_call(sibling_kernel, in_specs=[SMEM_SPEC] * 3 + [VMEM_SPEC] * 5...]
    unnamed x12 -> x8, local copies, waits for them, and re-layouts: 4.84 us -> 1.06 us
  transfers between devices with their start and end apart: 10 -> 10, of which waited for: 3 -> 3; matrix products, arithmetic and copies ran while one was open for 2% -> 2% of each run, Pallas kernels for 15% -> 22%
where the time goes in v7:
time: 96.2 us; the launch traced here: 95.3 us
  Pallas kernels  32.5 us (34%)
  blocking collectives  29.9 us (31%)
  starting transfers between devices  21.4 us (22%)
  waiting for transfers between devices  7.28 us (8%)
  local copies, waits for them, and re-layouts  3.07 us (3%)
  other arithmetic  1.05 us (1%)
    all_to_all x1, blocking collectives, on_device(): parts = lax.all_to_all(both.reshape(8, 2, WIDTH, BLOCK), 'cols', 0, 0)  29.9 us
    ppermute x7, starting transfers between devices, on_device(): lax.ppermute(deg_part, 'cols', [(i, (i + k) % 8) for i in range(8)])  12.8 us
    pallas_call x1, Pallas kernels, sibling_part(): pl.pallas_call(sibling_kernel, in_specs=[SMEM_SPEC] * 3 + [VMEM_SPEC] * 5...  9.87 us
    pallas_call x1, Pallas kernels, prep(): pl.pallas_call(prep_kernel, in_specs=[SMEM_SPEC, ANY_SPEC, ANY_SPEC], out...  8.22 us
    all_to_all x1, starting transfers between devices, on_device(): x_mine = lax.all_to_all(x_sent, 'rows', 0, 0).reshape(WIDTH, HALF)  8 us
    pallas_call x1, Pallas kernels, load(): pl.pallas_call(load_kernel, in_specs=[VMEM_SPEC] * 8 + [SMEM_SPEC, VMEM_S...  7.21 us
    pallas_call x1, Pallas kernels, own_part(): pl.pallas_call(own_kernel, in_specs=[SMEM_SPEC] * 3 + [VMEM_SPEC] * 5, ou...  5.7 us
    ppermute x7, waiting for transfers between devices, on_device(): lax.ppermute(deg_part, 'cols', [(i, (i + k) % 8) for i in range(8)])  4.72 us
  transfers between devices with their start and end apart: 10, of which 3 were waited for; matrix products, arithmetic and copies ran while one was open for 2% of the time, Pallas kernels for 22%

profile of v7, /device:TPU:0, one launch (start us, length us, event | category | flops | bytes accessed | tf_op | source)
XLA Modules:
  0.0 95.3 jit_solution(5138336255860339667)
XLA Ops:
  0.0 1.0 %copy-done = bf16[4096,64]{0,1:T(8,128)(2,1)S(1)} copy-done((bf16[4096,64]{0,1:T(8,128)(2,1)S(1)}, bf16[4096,64]{0,1:T(8,128)(2,1)}, u32[]{:S(2)}) %copy-start) | copy-done | bytes 524312
  1.1 1.6 %broadcast_in_dim.76 = bf16[8,64,2048]{2,1,0:T(8,128)(2,1)} broadcast(bf16[64,2048]{1,0:T(8,128)(2,1)S(1)} %dynamic-slice_bitcast_fusion), dimensions={1,2} | broadcast | bytes 2359296 | tf_op jit(solution)/shard_map/broadcast_in_dim | solution.py:344
  2.7 8.0 %all-to-all-start = ((bf16[8,64,2048]{2,1,0:T(8,128)(2,1)}), bf16[8,64,2048]{2,1,0:T(8,128)(2,1)S(1)}, u32[]{:S(2)}, u32[]{:S(2)}) async-start(bf16[8,64,2048]{2,1,0:T(8,128)(2,1)} %broadcast_in_dim.76), calls=%async_computation | async-start | bytes 4194304 | tf_op jit(solution)/shard_map/all_to_all | solution.py:346
  10.7 0.2 convert_reduce_fusion
  11.0 0.2 select_reduce_fusion.4
  11.4 0.2 select_reduce_fusion.2
  12.2 8.2 %prep.1 = (bf16[128,128]{1,0:T(8,128)(2,1)S(1)}, bf16[128,128,128]{2,1,0:T(8,128)(2,1)}, bf16[4,512,512]{2,1,0:T(8,128)(2,1)}) custom-call(s32[136]{0:T(256)S(1)} %concatenate.3.codes_ref, s32[128,128,128]{2,1,0:T(8,128)} %bitcast.14, bf16[4,512,512]{2,1,0:T(8,128)(2,1)} %weight_hbm.1), custom_call_target="tpu_custom_call" | custom-call | flops 33554432 | bytes 12582912 | tf_op jit(solution)/shard_map/prep/pallas_call | solution.py:88
  20.4 3.3 %collective-permute-start.6 = (bf16[128,128]{1,0:T(8,128)(2,1)S(1)}, bf16[128,128]{1,0:T(8,128)(2,1)S(1)}, u32[]{:S(2)}, u32[]{:S(2)}) collective-permute-start(bf16[128,128]{1,0:T(8,128)(2,1)S(1)} %get-tuple-element.44.refs_0_), channel_id=1, source_target_pairs={{0,14},{2,0},{4,2},{6,4},{8,6},{10,8},{12,10},{14,12},{1,15},{3,1}... | collective-permute-start | bytes 98312 | tf_op jit(solution)/shard_map/ppermute | solution.py:353
  23.7 0.8 collective-permute-start.5
  24.5 1.3 %collective-permute-start.4 = (bf16[128,128]{1,0:T(8,128)(2,1)S(1)}, bf16[128,128]{1,0:T(8,128)(2,1)S(1)}, u32[]{:S(2)}, u32[]{:S(2)}) collective-permute-start(bf16[128,128]{1,0:T(8,128)(2,1)S(1)} %get-tuple-element.44.refs_0_), channel_id=1, source_target_pairs={{0,10},{2,12},{4,14},{6,0},{8,2},{10,4},{12,6},{14,8},{1,11},{3,13... | collective-permute-start | bytes 98312 | tf_op jit(solution)/shard_map/ppermute | solution.py:353
  25.8 1.0 %collective-permute-start.3 = (bf16[128,128]{1,0:T(8,128)(2,1)S(1)}, bf16[128,128]{1,0:T(8,128)(2,1)S(1)}, u32[]{:S(2)}, u32[]{:S(2)}) collective-permute-start(bf16[128,128]{1,0:T(8,128)(2,1)S(1)} %get-tuple-element.44.refs_0_), channel_id=1, source_target_pairs={{0,8},{2,10},{4,12},{6,14},{8,0},{10,2},{12,4},{14,6},{1,9},{3,11}... | collective-permute-start | bytes 98312 | tf_op jit(solution)/shard_map/ppermute | solution.py:353
  26.9 1.9 %collective-permute-start.2 = (bf16[128,128]{1,0:T(8,128)(2,1)S(1)}, bf16[128,128]{1,0:T(8,128)(2,1)S(1)}, u32[]{:S(2)}, u32[]{:S(2)}) collective-permute-start(bf16[128,128]{1,0:T(8,128)(2,1)S(1)} %get-tuple-element.44.refs_0_), channel_id=1, source_target_pairs={{0,6},{2,8},{4,10},{6,12},{8,14},{10,0},{12,2},{14,4},{1,7},{3,9},... | collective-permute-start | bytes 98312 | tf_op jit(solution)/shard_map/ppermute | solution.py:353
  28.8 2.4 %collective-permute-start.1 = (bf16[128,128]{1,0:T(8,128)(2,1)S(1)}, bf16[128,128]{1,0:T(8,128)(2,1)S(1)}, u32[]{:S(2)}, u32[]{:S(2)}) collective-permute-start(bf16[128,128]{1,0:T(8,128)(2,1)S(1)} %get-tuple-element.44.refs_0_), channel_id=1, source_target_pairs={{0,4},{2,6},{4,8},{6,10},{8,12},{10,14},{12,0},{14,2},{1,5},{3,7},... | collective-permute-start | bytes 98312 | tf_op jit(solution)/shard_map/ppermute | solution.py:353
  31.2 2.1 %collective-permute-start = (bf16[128,128]{1,0:T(8,128)(2,1)S(1)}, bf16[128,128]{1,0:T(8,128)(2,1)S(1)}, u32[]{:S(2)}, u32[]{:S(2)}) collective-permute-start(bf16[128,128]{1,0:T(8,128)(2,1)S(1)} %get-tuple-element.44.refs_0_), channel_id=1, source_target_pairs={{0,2},{2,4},{4,6},{6,8},{8,10},{10,12},{12,14},{14,0},{1,3},{3,5},... | collective-permute-start | bytes 98312 | tf_op jit(solution)/shard_map/ppermute | solution.py:353
  33.3 2.6 %collective-permute-done.1.refs_2_ = bf16[128,128]{1,0:T(8,128)(2,1)S(1)} collective-permute-done((bf16[128,128]{1,0:T(8,128)(2,1)S(1)}, bf16[128,128]{1,0:T(8,128)(2,1)S(1)}, u32[]{:S(2)}, u32[]{:S(2)}) %collective-permute-start.1) | collective-permute-done | bytes 32800 | tf_op jit(solution)/shard_map/ppermute | solution.py:353
  35.8 2.1 %collective-permute-done.refs_1_ = bf16[128,128]{1,0:T(8,128)(2,1)S(1)} collective-permute-done((bf16[128,128]{1,0:T(8,128)(2,1)S(1)}, bf16[128,128]{1,0:T(8,128)(2,1)S(1)}, u32[]{:S(2)}, u32[]{:S(2)}) %collective-permute-start) | collective-permute-done | bytes 32800 | tf_op jit(solution)/shard_map/ppermute | solution.py:353
  38.0 2.6 %all-to-all-done = bf16[8,64,2048]{2,1,0:T(8,128)(2,1)S(1)} async-done(((bf16[8,64,2048]{2,1,0:T(8,128)(2,1)}), bf16[8,64,2048]{2,1,0:T(8,128)(2,1)S(1)}, u32[]{:S(2)}, u32[]{:S(2)}) %all-to-all-start) | async-done | bytes 2097184 | tf_op jit(solution)/shard_map/all_to_all | solution.py:346
  40.5 7.2 %own_hidden.1 = (bf16[4,512,512]{2,1,0:T(8,128)(2,1)S(1)}, bf16[128,128,128]{2,1,0:T(8,128)(2,1)S(1)}, f32[128,128]{1,0:T(8,128)S(1)}, bf16[4,32,512,128]{3,2,1,0:T(8,128)(2,1)S(1)}) custom-call(bf16[128,128]{1,0:T(8,128)(2,1)S(1)} %get-tuple-element.44.refs_0_, bf16[128,128]{1,0:T(8,128)(2,1)S(1)} %collective-permute-done.refs_1_, ...), custom_call_target="tpu_custom_call" | custom-call | flops 4294967296 | bytes 12582912 | tf_op jit(solution)/shard_map/own_hidden/pallas_call | solution.py:161
  47.8 9.9 %sibling_part.1 = (bf16[16,512,128]{2,1,0:T(8,128)(2,1)S(1)}, bf16[4,32,512,128]{3,2,1,0:T(8,128)(2,1)S(1)}, bf16[129,128,128]{2,1,0:T(8,128)(2,1)S(1)}) custom-call(s32[2]{0:T(128)S(1)} %pad_add_fusion.1.refs_8_.place_ref, s32[136]{0:T(256)S(1)} %concatenate.3.codes_ref, s32[2,4,72]{2,1,0:T(4,128)S(1)} %pad_add_fusion.pairs_ref, ...), custom_call_target="tpu_custom_call", output_to_operand_aliasing={{1}: (7, {})} | custom-call | flops 8589934592 | bytes 20971520 | tf_op jit(solution)/shard_map/sibling_part/pallas_call | solution.py:215
  57.6 0.6 collective-permute-start.8
  58.2 5.7 %own_part.1.own_ref = f32[16,512,128]{2,1,0:T(8,128)S(1)} custom-call(s32[2]{0:T(128)S(1)} %pad_add_fusion.1.refs_8_.place_ref, s32[136]{0:T(256)S(1)} %concatenate.3.codes_ref, s32[2,4,72]{2,1,0:T(4,128)S(1)} %pad_add_fusion.pairs_ref, bf16[512,2048]{1,0:T(8,128)(2,1)S(1)} %bitcast.11, bf16[512,2048]{1,0:T(8,128)(2,1)S(1)} %collective-permute-done.7.x_ref.xo_ref, ...), custom_call_target="tpu_custom_call" | custom-call | flops 4294967296 | bytes 20971520 | tf_op jit(solution)/shard_map/own_part/pallas_call | solution.py:258
  63.9 0.4 join.1
  64.4 29.9 %all_to_all.10.parts_ref = bf16[8,2,512,128]{3,2,1,0:T(8,128)(2,1)S(1)} all-to-all(bf16[8,2,512,128]{3,2,1,0:T(8,128)(2,1)S(1)} %bitcast.12), channel_id=1, replica_groups=mesh['rows'=8,'cols'=8,'rel'=2] {'cols'}, dimensions={0} | all-to-all | bytes 4194304 | tf_op jit(solution)/shard_map/all_to_all | solution.py:362
  94.2 1.1 %finish.1 = bf16[256,512]{1,0:T(8,128)(2,1)} custom-call(bf16[8,2,512,128]{3,2,1,0:T(8,128)(2,1)S(1)} %all_to_all.10.parts_ref, f32[1,512]{1,0:T(1,128)S(1)} %bitcast.13), custom_call_target="tpu_custom_call" | custom-call | tf_op jit(solution)/shard_map/finish/pallas_call | solution.py:300
  (36 shorter events, 1.0 us)
Async XLA Ops:
  0.0 1.0 %copy-start = (bf16[4096,64]{0,1:T(8,128)(2,1)S(1)}, bf16[4096,64]{0,1:T(8,128)(2,1)}, u32[]{:S(2)}) copy-start(bf16[4096,64]{0,1:T(8,128)(2,1)} %param.6) | copy-start | bytes 1572868
  2.7 8.0 %copy-start.3 = (s32[1,1,1,128]{3,2,1,0:T(1,128)S(1)}, s32[1,1,1,128]{3,2,1,0:T(1,128)}, u32[]{:S(2)}) copy-start(s32[1,1,1,128]{3,2,1,0:T(1,128)} %param.10) | copy-start | bytes 1540
  2.7 37.9 %all-to-all-start = ((bf16[8,64,2048]{2,1,0:T(8,128)(2,1)}), bf16[8,64,2048]{2,1,0:T(8,128)(2,1)S(1)}, u32[]{:S(2)}, u32[]{:S(2)}) async-start(bf16[8,64,2048]{2,1,0:T(8,128)(2,1)} %broadcast_in_dim.76), calls=%async_computation | async-start | bytes 4194304 | tf_op jit(solution)/shard_map/all_to_all | solution.py:346
  20.4 8.3 %collective-permute-start.6 = (bf16[128,128]{1,0:T(8,128)(2,1)S(1)}, bf16[128,128]{1,0:T(8,128)(2,1)S(1)}, u32[]{:S(2)}, u32[]{:S(2)}) collective-permute-start(bf16[128,128]{1,0:T(8,128)(2,1)S(1)} %get-tuple-element.44.refs_0_), channel_id=1, source_target_pairs={{0,14},{2,0},{4,2},{6,4},{8,6},{10,8},{12,10},{14,12},{1,15},{3,1}... | collective-permute-start | bytes 98312 | tf_op jit(solution)/shard_map/ppermute | solution.py:353
  23.7 7.5 %collective-permute-start.5 = (bf16[128,128]{1,0:T(8,128)(2,1)S(1)}, bf16[128,128]{1,0:T(8,128)(2,1)S(1)}, u32[]{:S(2)}, u32[]{:S(2)}) collective-permute-start(bf16[128,128]{1,0:T(8,128)(2,1)S(1)} %get-tuple-element.44.refs_0_), channel_id=1, source_target_pairs={{0,12},{2,14},{4,0},{6,2},{8,4},{10,6},{12,8},{14,10},{1,13},{3,15... | collective-permute-start | bytes 98312 | tf_op jit(solution)/shard_map/ppermute | solution.py:353
  24.5 8.7 %collective-permute-start.4 = (bf16[128,128]{1,0:T(8,128)(2,1)S(1)}, bf16[128,128]{1,0:T(8,128)(2,1)S(1)}, u32[]{:S(2)}, u32[]{:S(2)}) collective-permute-start(bf16[128,128]{1,0:T(8,128)(2,1)S(1)} %get-tuple-element.44.refs_0_), channel_id=1, source_target_pairs={{0,10},{2,12},{4,14},{6,0},{8,2},{10,4},{12,6},{14,8},{1,11},{3,13... | collective-permute-start | bytes 98312 | tf_op jit(solution)/shard_map/ppermute | solution.py:353
  25.8 7.4 %collective-permute-start.3 = (bf16[128,128]{1,0:T(8,128)(2,1)S(1)}, bf16[128,128]{1,0:T(8,128)(2,1)S(1)}, u32[]{:S(2)}, u32[]{:S(2)}) collective-permute-start(bf16[128,128]{1,0:T(8,128)(2,1)S(1)} %get-tuple-element.44.refs_0_), channel_id=1, source_target_pairs={{0,8},{2,10},{4,12},{6,14},{8,0},{10,2},{12,4},{14,6},{1,9},{3,11}... | collective-permute-start | bytes 98312 | tf_op jit(solution)/shard_map/ppermute | solution.py:353
  26.9 6.4 %collective-permute-start.2 = (bf16[128,128]{1,0:T(8,128)(2,1)S(1)}, bf16[128,128]{1,0:T(8,128)(2,1)S(1)}, u32[]{:S(2)}, u32[]{:S(2)}) collective-permute-start(bf16[128,128]{1,0:T(8,128)(2,1)S(1)} %get-tuple-element.44.refs_0_), channel_id=1, source_target_pairs={{0,6},{2,8},{4,10},{6,12},{8,14},{10,0},{12,2},{14,4},{1,7},{3,9},... | collective-permute-start | bytes 98312 | tf_op jit(solution)/shard_map/ppermute | solution.py:353
  28.8 7.1 %collective-permute-start.1 = (bf16[128,128]{1,0:T(8,128)(2,1)S(1)}, bf16[128,128]{1,0:T(8,128)(2,1)S(1)}, u32[]{:S(2)}, u32[]{:S(2)}) collective-permute-start(bf16[128,128]{1,0:T(8,128)(2,1)S(1)} %get-tuple-element.44.refs_0_), channel_id=1, source_target_pairs={{0,4},{2,6},{4,8},{6,10},{8,12},{10,14},{12,0},{14,2},{1,5},{3,7},... | collective-permute-start | bytes 98312 | tf_op jit(solution)/shard_map/ppermute | solution.py:353
  31.2 6.8 %collective-permute-start = (bf16[128,128]{1,0:T(8,128)(2,1)S(1)}, bf16[128,128]{1,0:T(8,128)(2,1)S(1)}, u32[]{:S(2)}, u32[]{:S(2)}) collective-permute-start(bf16[128,128]{1,0:T(8,128)(2,1)S(1)} %get-tuple-element.44.refs_0_), channel_id=1, source_target_pairs={{0,2},{2,4},{4,6},{6,8},{8,10},{10,12},{12,14},{14,0},{1,3},{3,5},... | collective-permute-start | bytes 98312 | tf_op jit(solution)/shard_map/ppermute | solution.py:353
  40.5 7.2 %collective-permute-start.7 = (bf16[512,2048]{1,0:T(8,128)(2,1)S(1)}, bf16[512,2048]{1,0:T(8,128)(2,1)S(1)}, u32[]{:S(2)}, u32[]{:S(2)}) collective-permute-start(bf16[512,2048]{1,0:T(8,128)(2,1)S(1)} %bitcast.9), channel_id=1, source_target_pairs={{0,1},{1,0},{2,3},{3,2},{4,5},{5,4},{6,7},{7,6},{8,9},{9,8},{10,11... | collective-permute-start | bytes 6291464 | tf_op jit(solution)/shard_map/ppermute | solution.py:335
  47.7 10.5 %copy-start.1 = (bf16[512,512]{1,0:T(8,128)(2,1)S(1)}, bf16[512,512]{1,0:T(8,128)(2,1)}, u32[]{:S(2)}) copy-start(bf16[512,512]{1,0:T(8,128)(2,1)} %self_ref.1) | copy-start | bytes 1572868
  57.6 6.3 %collective-permute-start.8 = (bf16[16,512,128]{2,1,0:T(8,128)(2,1)S(1)}, bf16[16,512,128]{2,1,0:T(8,128)(2,1)S(1)}, u32[]{:S(2)}, u32[]{:S(2)}) collective-permute-start(bf16[16,512,128]{2,1,0:T(8,128)(2,1)S(1)} %get-tuple-element.60), channel_id=1, source_target_pairs={{0,1},{1,0},{2,3},{3,2},{4,5},{5,4},{6,7},{7,6},{8,9},{9,8},{10,11... | collective-permute-start | bytes 6291464 | tf_op jit(solution)/shard_map/ppermute | solution.py:335
  64.4 29.9 %copy-start.2 = (f32[512]{0:T(512)S(1)}, f32[512]{0:T(512)}, u32[]{:S(2)}) copy-start(f32[512]{0:T(512)} %param.9) | copy-start | bytes 6148

commit v8 on v7

--- a/solution.py
+++ b/solution.py
@@ -135,26 +135,28 @@
 
 def load_kernel(*refs):
     deg_refs, (place_ref, x_ref, wt_hbm, cnt_hbm, wt_ref, cnt_ref, inv_ref, hid, sems) = refs[:8], refs[8:]
-    copies = [pltpu.make_async_copy(wt_hbm, wt_ref, sems.at[0]), pltpu.make_async_copy(cnt_hbm, cnt_ref, sems.at[1])]
+    copies = [pltpu.make_async_copy(wt_hbm.at[r], wt_ref.at[r], sems.at[r]) for r in range(NREL)]
+    copies.append(pltpu.make_async_copy(cnt_hbm, cnt_ref, sems.at[NREL]))
     for copy in copies:
         copy.start()
     degree = deg_refs[0][...].astype(jnp.float32)
     for ref in deg_refs[1:]:
         degree = degree + ref[...].astype(jnp.float32)
     inv_ref[...] = (1.0 / jnp.maximum(degree, 1.0)).T
-    copies[0].wait()
-
-    def step(i, carry):
+    def step(i, carry, wait=False):
         first = place_ref[CORE] * HALF_BLOCKS + i * (CHUNK // BLOCK)
         x = x_ref[:, pl.ds(pl.multiple_of(i * CHUNK, CHUNK), CHUNK)]
         for r in range(NREL):
+            if wait:
+                copies[r].wait()
             h = jnp.dot(wt_ref[r], x, preferred_element_type=jnp.float32).astype(jnp.bfloat16)
             for b in range(CHUNK // BLOCK):
                 hid[r, first + b] = h[:, b * BLOCK : (b + 1) * BLOCK]
         return carry
 
-    lax.fori_loop(0, STEPS // 2, step, 0)
-    copies[1].wait()
+    step(0, 0, wait=True)
+    lax.fori_loop(1, STEPS // 2, step, 0)
+    copies[NREL].wait()
 
 
 def load(degrees, place, x_mine, wt, cnt):
@@ -168,7 +170,7 @@
             pltpu.VMEM((BLOCK, NREL * NBLK), jnp.float32),
             pltpu.VMEM(HID, jnp.bfloat16),
         ],
-        scratch_shapes=[pltpu.SemaphoreType.DMA((2,))],
+        scratch_shapes=[pltpu.SemaphoreType.DMA((NREL + 1,))],
         compiler_params=params(28),
         cost_estimate=pl.CostEstimate(flops=NODES * WIDTH * WIDTH * NREL, bytes_accessed=12 * MIB, transcendentals=0),
         name="own_hidden",

time: 96.2 us -> 96.8 us (level)
  no operation moved by 1% of the time
where the time goes in v8:
time: 96.8 us; the launch traced here: 95.3 us
  Pallas kernels  32.4 us (33%)
  blocking collectives  29.9 us (31%)
  starting transfers between devices  21.4 us (22%)
  waiting for transfers between devices  7.28 us (8%)
  local copies, waits for them, and re-layouts  3.07 us (3%)
  other arithmetic  1.05 us (1%)
    all_to_all x1, blocking collectives, on_device(): parts = lax.all_to_all(both.reshape(8, 2, WIDTH, BLOCK), 'cols', 0, 0)  29.9 us
    ppermute x7, starting transfers between devices, on_device(): lax.ppermute(deg_part, 'cols', [(i, (i + k) % 8) for i in range(8)])  12.8 us
    pallas_call x1, Pallas kernels, sibling_part(): pl.pallas_call(sibling_kernel, in_specs=[SMEM_SPEC] * 3 + [VMEM_SPEC] * 5...  9.87 us
    pallas_call x1, Pallas kernels, prep(): pl.pallas_call(prep_kernel, in_specs=[SMEM_SPEC, ANY_SPEC, ANY_SPEC], out...  8.22 us
    all_to_all x1, starting transfers between devices, on_device(): x_mine = lax.all_to_all(x_sent, 'rows', 0, 0).reshape(WIDTH, HALF)  8 us
    pallas_call x1, Pallas kernels, load(): pl.pallas_call(load_kernel, in_specs=[VMEM_SPEC] * 8 + [SMEM_SPEC, VMEM_S...  7.17 us
    pallas_call x1, Pallas kernels, own_part(): pl.pallas_call(own_kernel, in_specs=[SMEM_SPEC] * 3 + [VMEM_SPEC] * 5, ou...  5.7 us
    ppermute x7, waiting for transfers between devices, on_device(): lax.ppermute(deg_part, 'cols', [(i, (i + k) % 8) for i in range(8)])  4.72 us
  transfers between devices with their start and end apart: 10, of which 3 were waited for; matrix products, arithmetic and copies ran while one was open for 2% of the time, Pallas kernels for 22%

profile of v8, /device:TPU:0, one launch (start us, length us, event | category | flops | bytes accessed | tf_op | source)
XLA Modules:
  0.0 95.3 jit_solution(14643114611639509350)
XLA Ops:
  0.0 1.0 %copy-done = bf16[4096,64]{0,1:T(8,128)(2,1)S(1)} copy-done((bf16[4096,64]{0,1:T(8,128)(2,1)S(1)}, bf16[4096,64]{0,1:T(8,128)(2,1)}, u32[]{:S(2)}) %copy-start) | copy-done | bytes 524312
  1.1 1.6 %broadcast_in_dim.76 = bf16[8,64,2048]{2,1,0:T(8,128)(2,1)} broadcast(bf16[64,2048]{1,0:T(8,128)(2,1)S(1)} %dynamic-slice_bitcast_fusion), dimensions={1,2} | broadcast | bytes 2359296 | tf_op jit(solution)/shard_map/broadcast_in_dim | solution.py:346
  2.7 8.0 %all-to-all-start = ((bf16[8,64,2048]{2,1,0:T(8,128)(2,1)}), bf16[8,64,2048]{2,1,0:T(8,128)(2,1)S(1)}, u32[]{:S(2)}, u32[]{:S(2)}) async-start(bf16[8,64,2048]{2,1,0:T(8,128)(2,1)} %broadcast_in_dim.76), calls=%async_computation | async-start | bytes 4194304 | tf_op jit(solution)/shard_map/all_to_all | solution.py:348
  10.7 0.2 convert_reduce_fusion
  11.0 0.2 select_reduce_fusion.4
  11.4 0.2 select_reduce_fusion.2
  12.2 8.2 %prep.1 = (bf16[128,128]{1,0:T(8,128)(2,1)S(1)}, bf16[128,128,128]{2,1,0:T(8,128)(2,1)}, bf16[4,512,512]{2,1,0:T(8,128)(2,1)}) custom-call(s32[136]{0:T(256)S(1)} %concatenate.3.codes_ref, s32[128,128,128]{2,1,0:T(8,128)} %bitcast.14, bf16[4,512,512]{2,1,0:T(8,128)(2,1)} %weight_hbm.1), custom_call_target="tpu_custom_call" | custom-call | flops 33554432 | bytes 12582912 | tf_op jit(solution)/shard_map/prep/pallas_call | solution.py:88
  20.4 3.3 %collective-permute-start.6 = (bf16[128,128]{1,0:T(8,128)(2,1)S(1)}, bf16[128,128]{1,0:T(8,128)(2,1)S(1)}, u32[]{:S(2)}, u32[]{:S(2)}) collective-permute-start(bf16[128,128]{1,0:T(8,128)(2,1)S(1)} %get-tuple-element.44.refs_0_), channel_id=1, source_target_pairs={{0,14},{2,0},{4,2},{6,4},{8,6},{10,8},{12,10},{14,12},{1,15},{3,1}... | collective-permute-start | bytes 98312 | tf_op jit(solution)/shard_map/ppermute | solution.py:355
  23.7 0.8 collective-permute-start.5
  24.5 1.3 %collective-permute-start.4 = (bf16[128,128]{1,0:T(8,128)(2,1)S(1)}, bf16[128,128]{1,0:T(8,128)(2,1)S(1)}, u32[]{:S(2)}, u32[]{:S(2)}) collective-permute-start(bf16[128,128]{1,0:T(8,128)(2,1)S(1)} %get-tuple-element.44.refs_0_), channel_id=1, source_target_pairs={{0,10},{2,12},{4,14},{6,0},{8,2},{10,4},{12,6},{14,8},{1,11},{3,13... | collective-permute-start | bytes 98312 | tf_op jit(solution)/shard_map/ppermute | solution.py:355
  25.8 1.0 %collective-permute-start.3 = (bf16[128,128]{1,0:T(8,128)(2,1)S(1)}, bf16[128,128]{1,0:T(8,128)(2,1)S(1)}, u32[]{:S(2)}, u32[]{:S(2)}) collective-permute-start(bf16[128,128]{1,0:T(8,128)(2,1)S(1)} %get-tuple-element.44.refs_0_), channel_id=1, source_target_pairs={{0,8},{2,10},{4,12},{6,14},{8,0},{10,2},{12,4},{14,6},{1,9},{3,11}... | collective-permute-start | bytes 98312 | tf_op jit(solution)/shard_map/ppermute | solution.py:355
  26.9 1.9 %collective-permute-start.2 = (bf16[128,128]{1,0:T(8,128)(2,1)S(1)}, bf16[128,128]{1,0:T(8,128)(2,1)S(1)}, u32[]{:S(2)}, u32[]{:S(2)}) collective-permute-start(bf16[128,128]{1,0:T(8,128)(2,1)S(1)} %get-tuple-element.44.refs_0_), channel_id=1, source_target_pairs={{0,6},{2,8},{4,10},{6,12},{8,14},{10,0},{12,2},{14,4},{1,7},{3,9},... | collective-permute-start | bytes 98312 | tf_op jit(solution)/shard_map/ppermute | solution.py:355
  28.8 2.4 %collective-permute-start.1 = (bf16[128,128]{1,0:T(8,128)(2,1)S(1)}, bf16[128,128]{1,0:T(8,128)(2,1)S(1)}, u32[]{:S(2)}, u32[]{:S(2)}) collective-permute-start(bf16[128,128]{1,0:T(8,128)(2,1)S(1)} %get-tuple-element.44.refs_0_), channel_id=1, source_target_pairs={{0,4},{2,6},{4,8},{6,10},{8,12},{10,14},{12,0},{14,2},{1,5},{3,7},... | collective-permute-start | bytes 98312 | tf_op jit(solution)/shard_map/ppermute | solution.py:355
  31.2 2.1 %collective-permute-start = (bf16[128,128]{1,0:T(8,128)(2,1)S(1)}, bf16[128,128]{1,0:T(8,128)(2,1)S(1)}, u32[]{:S(2)}, u32[]{:S(2)}) collective-permute-start(bf16[128,128]{1,0:T(8,128)(2,1)S(1)} %get-tuple-element.44.refs_0_), channel_id=1, source_target_pairs={{0,2},{2,4},{4,6},{6,8},{8,10},{10,12},{12,14},{14,0},{1,3},{3,5},... | collective-permute-start | bytes 98312 | tf_op jit(solution)/shard_map/ppermute | solution.py:355
  33.3 2.6 %collective-permute-done.1.refs_2_ = bf16[128,128]{1,0:T(8,128)(2,1)S(1)} collective-permute-done((bf16[128,128]{1,0:T(8,128)(2,1)S(1)}, bf16[128,128]{1,0:T(8,128)(2,1)S(1)}, u32[]{:S(2)}, u32[]{:S(2)}) %collective-permute-start.1) | collective-permute-done | bytes 32800 | tf_op jit(solution)/shard_map/ppermute | solution.py:355
  35.8 2.1 %collective-permute-done.refs_1_ = bf16[128,128]{1,0:T(8,128)(2,1)S(1)} collective-permute-done((bf16[128,128]{1,0:T(8,128)(2,1)S(1)}, bf16[128,128]{1,0:T(8,128)(2,1)S(1)}, u32[]{:S(2)}, u32[]{:S(2)}) %collective-permute-start) | collective-permute-done | bytes 32800 | tf_op jit(solution)/shard_map/ppermute | solution.py:355
  38.0 2.6 %all-to-all-done = bf16[8,64,2048]{2,1,0:T(8,128)(2,1)S(1)} async-done(((bf16[8,64,2048]{2,1,0:T(8,128)(2,1)}), bf16[8,64,2048]{2,1,0:T(8,128)(2,1)S(1)}, u32[]{:S(2)}, u32[]{:S(2)}) %all-to-all-start) | async-done | bytes 2097184 | tf_op jit(solution)/shard_map/all_to_all | solution.py:348
  40.5 7.2 %own_hidden.1 = (bf16[4,512,512]{2,1,0:T(8,128)(2,1)S(1)}, bf16[128,128,128]{2,1,0:T(8,128)(2,1)S(1)}, f32[128,128]{1,0:T(8,128)S(1)}, bf16[4,32,512,128]{3,2,1,0:T(8,128)(2,1)S(1)}) custom-call(bf16[128,128]{1,0:T(8,128)(2,1)S(1)} %get-tuple-element.44.refs_0_, bf16[128,128]{1,0:T(8,128)(2,1)S(1)} %collective-permute-done.refs_1_, ...), custom_call_target="tpu_custom_call" | custom-call | flops 4294967296 | bytes 12582912 | tf_op jit(solution)/shard_map/own_hidden/pallas_call | solution.py:163
  47.7 9.9 %sibling_part.1 = (bf16[16,512,128]{2,1,0:T(8,128)(2,1)S(1)}, bf16[4,32,512,128]{3,2,1,0:T(8,128)(2,1)S(1)}, bf16[129,128,128]{2,1,0:T(8,128)(2,1)S(1)}) custom-call(s32[2]{0:T(128)S(1)} %pad_add_fusion.1.refs_8_.place_ref, s32[136]{0:T(256)S(1)} %concatenate.3.codes_ref, s32[2,4,72]{2,1,0:T(4,128)S(1)} %pad_add_fusion.pairs_ref, ...), custom_call_target="tpu_custom_call", output_to_operand_aliasing={{1}: (7, {})} | custom-call | flops 8589934592 | bytes 20971520 | tf_op jit(solution)/shard_map/sibling_part/pallas_call | solution.py:217
  57.6 0.6 collective-permute-start.8
  58.2 5.7 %own_part.1.own_ref = f32[16,512,128]{2,1,0:T(8,128)S(1)} custom-call(s32[2]{0:T(128)S(1)} %pad_add_fusion.1.refs_8_.place_ref, s32[136]{0:T(256)S(1)} %concatenate.3.codes_ref, s32[2,4,72]{2,1,0:T(4,128)S(1)} %pad_add_fusion.pairs_ref, bf16[512,2048]{1,0:T(8,128)(2,1)S(1)} %bitcast.11, bf16[512,2048]{1,0:T(8,128)(2,1)S(1)} %collective-permute-done.7.x_ref.xo_ref, ...), custom_call_target="tpu_custom_call" | custom-call | flops 4294967296 | bytes 20971520 | tf_op jit(solution)/shard_map/own_part/pallas_call | solution.py:260
  63.9 0.4 join.1
  64.3 29.9 %all_to_all.10.parts_ref = bf16[8,2,512,128]{3,2,1,0:T(8,128)(2,1)S(1)} all-to-all(bf16[8,2,512,128]{3,2,1,0:T(8,128)(2,1)S(1)} %bitcast.12), channel_id=1, replica_groups=mesh['rows'=8,'cols'=8,'rel'=2] {'cols'}, dimensions={0} | all-to-all | bytes 4194304 | tf_op jit(solution)/shard_map/all_to_all | solution.py:364
  94.2 1.1 %finish.1 = bf16[256,512]{1,0:T(8,128)(2,1)} custom-call(bf16[8,2,512,128]{3,2,1,0:T(8,128)(2,1)S(1)} %all_to_all.10.parts_ref, f32[1,512]{1,0:T(1,128)S(1)} %bitcast.13), custom_call_target="tpu_custom_call" | custom-call | tf_op jit(solution)/shard_map/finish/pallas_call | solution.py:302
  (36 shorter events, 1.0 us)
Async XLA Ops:
  0.0 1.0 %copy-start = (bf16[4096,64]{0,1:T(8,128)(2,1)S(1)}, bf16[4096,64]{0,1:T(8,128)(2,1)}, u32[]{:S(2)}) copy-start(bf16[4096,64]{0,1:T(8,128)(2,1)} %param.6) | copy-start | bytes 1572868
  2.7 8.0 %copy-start.3 = (s32[1,1,1,128]{3,2,1,0:T(1,128)S(1)}, s32[1,1,1,128]{3,2,1,0:T(1,128)}, u32[]{:S(2)}) copy-start(s32[1,1,1,128]{3,2,1,0:T(1,128)} %param.10) | copy-start | bytes 1540
  2.7 37.9 %all-to-all-start = ((bf16[8,64,2048]{2,1,0:T(8,128)(2,1)}), bf16[8,64,2048]{2,1,0:T(8,128)(2,1)S(1)}, u32[]{:S(2)}, u32[]{:S(2)}) async-start(bf16[8,64,2048]{2,1,0:T(8,128)(2,1)} %broadcast_in_dim.76), calls=%async_computation | async-start | bytes 4194304 | tf_op jit(solution)/shard_map/all_to_all | solution.py:348
  20.4 8.3 %collective-permute-start.6 = (bf16[128,128]{1,0:T(8,128)(2,1)S(1)}, bf16[128,128]{1,0:T(8,128)(2,1)S(1)}, u32[]{:S(2)}, u32[]{:S(2)}) collective-permute-start(bf16[128,128]{1,0:T(8,128)(2,1)S(1)} %get-tuple-element.44.refs_0_), channel_id=1, source_target_pairs={{0,14},{2,0},{4,2},{6,4},{8,6},{10,8},{12,10},{14,12},{1,15},{3,1}... | collective-permute-start | bytes 98312 | tf_op jit(solution)/shard_map/ppermute | solution.py:355
  23.7 7.5 %collective-permute-start.5 = (bf16[128,128]{1,0:T(8,128)(2,1)S(1)}, bf16[128,128]{1,0:T(8,128)(2,1)S(1)}, u32[]{:S(2)}, u32[]{:S(2)}) collective-permute-start(bf16[128,128]{1,0:T(8,128)(2,1)S(1)} %get-tuple-element.44.refs_0_), channel_id=1, source_target_pairs={{0,12},{2,14},{4,0},{6,2},{8,4},{10,6},{12,8},{14,10},{1,13},{3,15... | collective-permute-start | bytes 98312 | tf_op jit(solution)/shard_map/ppermute | solution.py:355
  24.5 8.7 %collective-permute-start.4 = (bf16[128,128]{1,0:T(8,128)(2,1)S(1)}, bf16[128,128]{1,0:T(8,128)(2,1)S(1)}, u32[]{:S(2)}, u32[]{:S(2)}) collective-permute-start(bf16[128,128]{1,0:T(8,128)(2,1)S(1)} %get-tuple-element.44.refs_0_), channel_id=1, source_target_pairs={{0,10},{2,12},{4,14},{6,0},{8,2},{10,4},{12,6},{14,8},{1,11},{3,13... | collective-permute-start | bytes 98312 | tf_op jit(solution)/shard_map/ppermute | solution.py:355
  25.8 7.4 %collective-permute-start.3 = (bf16[128,128]{1,0:T(8,128)(2,1)S(1)}, bf16[128,128]{1,0:T(8,128)(2,1)S(1)}, u32[]{:S(2)}, u32[]{:S(2)}) collective-permute-start(bf16[128,128]{1,0:T(8,128)(2,1)S(1)} %get-tuple-element.44.refs_0_), channel_id=1, source_target_pairs={{0,8},{2,10},{4,12},{6,14},{8,0},{10,2},{12,4},{14,6},{1,9},{3,11}... | collective-permute-start | bytes 98312 | tf_op jit(solution)/shard_map/ppermute | solution.py:355
  26.9 6.4 %collective-permute-start.2 = (bf16[128,128]{1,0:T(8,128)(2,1)S(1)}, bf16[128,128]{1,0:T(8,128)(2,1)S(1)}, u32[]{:S(2)}, u32[]{:S(2)}) collective-permute-start(bf16[128,128]{1,0:T(8,128)(2,1)S(1)} %get-tuple-element.44.refs_0_), channel_id=1, source_target_pairs={{0,6},{2,8},{4,10},{6,12},{8,14},{10,0},{12,2},{14,4},{1,7},{3,9},... | collective-permute-start | bytes 98312 | tf_op jit(solution)/shard_map/ppermute | solution.py:355
  28.8 7.1 %collective-permute-start.1 = (bf16[128,128]{1,0:T(8,128)(2,1)S(1)}, bf16[128,128]{1,0:T(8,128)(2,1)S(1)}, u32[]{:S(2)}, u32[]{:S(2)}) collective-permute-start(bf16[128,128]{1,0:T(8,128)(2,1)S(1)} %get-tuple-element.44.refs_0_), channel_id=1, source_target_pairs={{0,4},{2,6},{4,8},{6,10},{8,12},{10,14},{12,0},{14,2},{1,5},{3,7},... | collective-permute-start | bytes 98312 | tf_op jit(solution)/shard_map/ppermute | solution.py:355
  31.2 6.8 %collective-permute-start = (bf16[128,128]{1,0:T(8,128)(2,1)S(1)}, bf16[128,128]{1,0:T(8,128)(2,1)S(1)}, u32[]{:S(2)}, u32[]{:S(2)}) collective-permute-start(bf16[128,128]{1,0:T(8,128)(2,1)S(1)} %get-tuple-element.44.refs_0_), channel_id=1, source_target_pairs={{0,2},{2,4},{4,6},{6,8},{8,10},{10,12},{12,14},{14,0},{1,3},{3,5},... | collective-permute-start | bytes 98312 | tf_op jit(solution)/shard_map/ppermute | solution.py:355
  40.5 7.2 %collective-permute-start.7 = (bf16[512,2048]{1,0:T(8,128)(2,1)S(1)}, bf16[512,2048]{1,0:T(8,128)(2,1)S(1)}, u32[]{:S(2)}, u32[]{:S(2)}) collective-permute-start(bf16[512,2048]{1,0:T(8,128)(2,1)S(1)} %bitcast.9), channel_id=1, source_target_pairs={{0,1},{1,0},{2,3},{3,2},{4,5},{5,4},{6,7},{7,6},{8,9},{9,8},{10,11... | collective-permute-start | bytes 6291464 | tf_op jit(solution)/shard_map/ppermute | solution.py:337
  47.7 10.5 %copy-start.1 = (bf16[512,512]{1,0:T(8,128)(2,1)S(1)}, bf16[512,512]{1,0:T(8,128)(2,1)}, u32[]{:S(2)}) copy-start(bf16[512,512]{1,0:T(8,128)(2,1)} %self_ref.1) | copy-start | bytes 1572868
  57.6 6.3 %collective-permute-start.8 = (bf16[16,512,128]{2,1,0:T(8,128)(2,1)S(1)}, bf16[16,512,128]{2,1,0:T(8,128)(2,1)S(1)}, u32[]{:S(2)}, u32[]{:S(2)}) collective-permute-start(bf16[16,512,128]{2,1,0:T(8,128)(2,1)S(1)} %get-tuple-element.60), channel_id=1, source_target_pairs={{0,1},{1,0},{2,3},{3,2},{4,5},{5,4},{6,7},{7,6},{8,9},{9,8},{10,11... | collective-permute-start | bytes 6291464 | tf_op jit(solution)/shard_map/ppermute | solution.py:337
  64.3 29.9 %copy-start.2 = (f32[512]{0:T(512)S(1)}, f32[512]{0:T(512)}, u32[]{:S(2)}) copy-start(f32[512]{0:T(512)} %param.9) | copy-start | bytes 6148
